TPU v7x, 32 devices: a whole 2x2x4 slice. The times are simulated.
32 devices in a mesh: seq: 4 (over x, core), dp: 8 (over z, y).
Axes of the slice: x: 2, y: 2, z: 4, core: 2. Of those that a mesh axis runs over, the one named last changes fastest.
Arguments:
- block_input: bfloat16 [8, 1024, 2048], P('dp', 'seq'), may hold values from -6 to 6
- out_grad: bfloat16 [8, 1024, 2048], P('dp', 'seq'), may hold values from -6 to 6
- lengths: int32 [8, 2], P('dp'), may hold values from 128 to 896, as said below
- vectors: float32 [16, 2048], P(None, ('seq', 'dp')), may hold values from -12 to 3, as said below
- vectors_moment: float32 [16, 2048], P(None, ('seq', 'dp')), may hold values from -28 to 28
- vectors_average: float32 [16, 2048], P(None, ('seq', 'dp')), may hold values from -3 to 3
- mix_weights: float32 [5, 2048, 2048], P(None, ('seq', 'dp')), may hold values from -0.125 to 0.125
- mix_moment: float32 [5, 2048, 2048], P(None, ('seq', 'dp')), may hold values from -5 to 5
- mix_average: float32 [5, 2048, 2048], P(None, ('seq', 'dp')), may hold values from -0.125 to 0.125
- ffn_key: float32 [2048, 7168], P(('seq', 'dp')), may hold values from -0.125 to 0.125
- ffn_key_moment: float32 [2048, 7168], P(('seq', 'dp')), may hold values from -5 to 5
- ffn_key_average: float32 [2048, 7168], P(('seq', 'dp')), may hold values from -0.125 to 0.125
- ffn_recept: float32 [2048, 2048], P(('seq', 'dp')), may hold values from -0.125 to 0.125
- ffn_recept_moment: float32 [2048, 2048], P(('seq', 'dp')), may hold values from -5 to 5
- ffn_recept_average: float32 [2048, 2048], P(('seq', 'dp')), may hold values from -0.125 to 0.125
- ffn_value: float32 [7168, 2048], P(('seq', 'dp')), may hold values from -0.0625 to 0.0625
- ffn_value_moment: float32 [7168, 2048], P(('seq', 'dp')), may hold values from -5 to 5
- ffn_value_average: float32 [7168, 2048], P(('seq', 'dp')), may hold values from -0.0625 to 0.0625
- maa_down: float32 [2048, 160], P(('seq', 'dp')), may hold values from -0.125 to 0.125
- maa_down_moment: float32 [2048, 160], P(('seq', 'dp')), may hold values from -768 to 768
- maa_down_average: float32 [2048, 160], P(('seq', 'dp')), may hold values from -0.125 to 0.125
- maa_up: float32 [5, 32, 2048], P(None, None, ('seq', 'dp')), may hold values from -0.5 to 0.5
- maa_up_moment: float32 [5, 32, 2048], P(None, None, ('seq', 'dp')), may hold values from -5 to 5
- maa_up_average: float32 [5, 32, 2048], P(None, None, ('seq', 'dp')), may hold values from -0.5 to 0.5
- decay_down: float32 [2048, 64], P(('seq', 'dp')), may hold values from -0.125 to 0.125
- decay_down_moment: float32 [2048, 64], P(('seq', 'dp')), may hold values from -5 to 5
- decay_down_average: float32 [2048, 64], P(('seq', 'dp')), may hold values from -0.125 to 0.125
- decay_up: float32 [64, 2048], P(None, ('seq', 'dp')), may hold values from -0.375 to 0.375
- decay_up_moment: float32 [64, 2048], P(None, ('seq', 'dp')), may hold values from -5 to 5
- decay_up_average: float32 [64, 2048], P(None, ('seq', 'dp')), may hold values from -0.375 to 0.375
Outputs:
- block_output: float32 [8, 1024, 2048], P('dp', 'seq')
- input_grad: float32 [8, 1024, 2048], P('dp', 'seq')
- vectors_new: float32 [16, 2048], P(None, ('seq', 'dp'))
- vectors_moment_new: float32 [16, 2048], P(None, ('seq', 'dp'))
- vectors_average_new: float32 [16, 2048], P(None, ('seq', 'dp'))
- mix_new: float32 [5, 2048, 2048], P(None, ('seq', 'dp'))
- mix_moment_new: float32 [5, 2048, 2048], P(None, ('seq', 'dp'))
- mix_average_new: float32 [5, 2048, 2048], P(None, ('seq', 'dp'))
- ffn_key_new: float32 [2048, 7168], P(('seq', 'dp'))
- ffn_key_moment_new: float32 [2048, 7168], P(('seq', 'dp'))
- ffn_key_average_new: float32 [2048, 7168], P(('seq', 'dp'))
- ffn_recept_new: float32 [2048, 2048], P(('seq', 'dp'))
- ffn_recept_moment_new: float32 [2048, 2048], P(('seq', 'dp'))
- ffn_recept_average_new: float32 [2048, 2048], P(('seq', 'dp'))
- ffn_value_new: float32 [7168, 2048], P(('seq', 'dp'))
- ffn_value_moment_new: float32 [7168, 2048], P(('seq', 'dp'))
- ffn_value_average_new: float32 [7168, 2048], P(('seq', 'dp'))
- maa_down_new: float32 [2048, 160], P(('seq', 'dp'))
- maa_down_moment_new: float32 [2048, 160], P(('seq', 'dp'))
- maa_down_average_new: float32 [2048, 160], P(('seq', 'dp'))
- maa_up_new: float32 [5, 32, 2048], P(None, None, ('seq', 'dp'))
- maa_up_moment_new: float32 [5, 32, 2048], P(None, None, ('seq', 'dp'))
- maa_up_average_new: float32 [5, 32, 2048], P(None, None, ('seq', 'dp'))
- decay_down_new: float32 [2048, 64], P(('seq', 'dp'))
- decay_down_moment_new: float32 [2048, 64], P(('seq', 'dp'))
- decay_down_average_new: float32 [2048, 64], P(('seq', 'dp'))
- decay_up_new: float32 [64, 2048], P(None, ('seq', 'dp'))
- decay_up_moment_new: float32 [64, 2048], P(None, ('seq', 'dp'))
- decay_up_average_new: float32 [64, 2048], P(None, ('seq', 'dp'))
Inputs may be any that keep to these rules, and one draw needn't show every extreme that they name: `vectors`: row 8 holds negative base decays and the other rows values of order one. `lengths`: each sequence holds one document of 128 tokens and one of the rest, in either order.
All inputs are finite; a program needn't handle non-finite values.
Results may differ from a plain program's by a relative error of at most 0.0095.
The roundings to bfloat16 on the way count: a program that leaves them out, or rounds other values in their place, can miss the bound.
Values may be sent and summed in bfloat16 or wider, within the bound.
No kernel may reach another device: no remote copies, remote signals or barrier semaphores. Data moves between devices by JAX's collectives and lax.ppermute only.
A program may use at most 448 MiB of HBM per device.

v0:
```python
from functools import partial
import math

import jax
import jax.numpy as jnp
from jax import lax
from jax.sharding import PartitionSpec as P

CHANNELS_PER_HEM = 64


highest_precision = lax.Precision.HIGHEST
factors = (0.2, 0.03, 0.03, 0.03, 0.03, 0.03, 0.03, 0.03, 0.03)


def from_behind(array, axis, by):
    devices = lax.axis_size(axis)
    pairs = [(i, i + by) for i in range(devices) if 0 <= i + by < devices]
    return lax.ppermute(array, axis, pairs)


def prefix(array, axis, combine, identity, reverse):
    devices, here = (lax.axis_size(axis), lax.axis_index(axis))
    everything = jax.tree.map(lambda part: lax.all_gather(part, axis), array)
    start = jax.tree.map(
        lambda part, zero: jnp.broadcast_to(jnp.asarray(zero, part.dtype), part.shape),
        array,
        identity,
    )

    def lap(k, before):
        at = devices - 1 - k if reverse else k
        reached = at > here if reverse else at < here
        new = combine(before, jax.tree.map(lambda part: part[at], everything))
        return jax.tree.map(lambda a, b: jnp.where(reached, a, b), new, before)

    return lax.fori_loop(0, devices, lap, start)


def layer_norm(field, gain, bias):
    center = field - jnp.mean(field, axis=-1, keepdims=True)
    spread = jnp.mean(center * center, axis=-1, keepdims=True)
    return center * lax.rsqrt(spread + 1e-05) * gain + bias


def norm_first(field, blending_arrays):
    return layer_norm(field, blending_arrays[0], blending_arrays[1])


def norm_second(field, blending_arrays):
    return layer_norm(field, blending_arrays[12], blending_arrays[13])


def gate_part(raw_output, gate, blending_arrays):
    center = raw_output - jnp.mean(raw_output, axis=-1, keepdims=True)
    spread = jnp.mean(center * center, axis=-1, keepdims=True)
    normal_draw = (center * lax.rsqrt(spread + 0.00064)).reshape(gate.shape)
    return (normal_draw * blending_arrays[10] + blending_arrays[11]) * jax.nn.silu(gate)


def mix_inputs(
    normed, incoming, blending_arrays, mix_down_weight, mix_up_weight, ddown, dup, follows
):
    local_tokens = normed.shape[0]
    prior = jnp.concatenate([incoming, normed[:-1]], axis=0) * follows[:, None]
    delta = prior - normed
    mixed_input = normed + delta * blending_arrays[2]
    low_rank_adapter = jnp.tanh(
        jnp.dot(mixed_input, mix_down_weight, precision=highest_precision)
    ).reshape(local_tokens, 5, mix_up_weight.shape[1])
    start_offsets = jnp.einsum(
        "vjs,jsz->vjz", low_rank_adapter, mix_up_weight, precision=highest_precision
    )
    inputs = normed[:, None] + delta[:, None] * (blending_arrays[3:8][None] + start_offsets)
    decay = blending_arrays[8] + jnp.dot(
        jnp.tanh(jnp.dot(inputs[:, 0], ddown, precision=highest_precision)),
        dup,
        precision=highest_precision,
    )
    return (inputs[:, 1], inputs[:, 2], inputs[:, 3], inputs[:, 4], -jnp.exp(decay))


def channel_inputs(second, incoming, blending_arrays, follows):
    prior = jnp.concatenate([incoming, second[:-1]], axis=0) * follows[:, None]
    delta = prior - second
    return (second + delta * blending_arrays[14], second + delta * blending_arrays[15])


def recursive_section(current_boost_param, memory_table, segment_parts):
    acceptance_lines, lookup_lines, payload_lines, logarithmic_forgetting, segment_groups, prior = (
        segment_parts
    )
    order = jnp.arange(acceptance_lines.shape[0])
    total = jnp.cumsum(logarithmic_forgetting, axis=0)
    before = total - logarithmic_forgetting
    lower = (order[:, None] > order[None, :]) & (segment_groups[:, None] == segment_groups[None, :])
    lower_f = lower.astype(jnp.float32)[:, :, None, None]
    gap = jnp.where(lower[:, :, None, None], before[:, None] - total[None, :], 0.0)
    scores = jnp.einsum(
        "thk,shk,tshk->tsh",
        acceptance_lines,
        lookup_lines,
        jnp.exp(gap) * lower_f,
        precision=highest_precision,
    )
    diagonal_contribution = jnp.sum(
        acceptance_lines * current_boost_param[None] * lookup_lines, axis=-1
    )
    stratum_result = (
        jnp.einsum("tsh,shv->thv", scores, payload_lines, precision=highest_precision)
        + diagonal_contribution[:, :, None] * payload_lines
    )
    carried = (segment_groups == prior).astype(jnp.float32)
    query_rows = acceptance_lines * jnp.exp(before) * carried[:, None, None]
    stratum_result = stratum_result + jnp.einsum(
        "yco,cor->ycr", query_rows, memory_table, precision=highest_precision
    )
    last = total[-1]
    keep = (segment_groups[-1] == prior).astype(jnp.float32)
    live = (segment_groups == segment_groups[-1]).astype(jnp.float32)
    weighted_sum = lookup_lines * jnp.exp(last[None] - total) * live[:, None, None]
    fresh_state = jnp.einsum(
        "dcm,dcy->cmy", weighted_sum, payload_lines, precision=highest_precision
    )
    memory_table = memory_table * (jnp.exp(last) * keep)[:, :, None] + fresh_state
    return (memory_table, stratum_result)


def partitioned_recursion(
    acceptance_lines,
    lookup_lines,
    payload_lines,
    logarithmic_forgetting,
    current_boost_param,
    segment_groups,
    preceding_segment,
):
    length, attention_heads_number, embedding_extent = acceptance_lines.shape
    blocks = length // 32
    doc_blocks = segment_groups.reshape(blocks, 32)
    priors = jnp.concatenate([jnp.reshape(preceding_segment, (1,)), doc_blocks[:-1, -1]])
    opening_memory = jnp.zeros(
        (attention_heads_number, embedding_extent, embedding_extent), jnp.float32
    )
    segment_parts = (
        acceptance_lines.reshape(blocks, 32, attention_heads_number, embedding_extent),
        lookup_lines.reshape(blocks, 32, attention_heads_number, embedding_extent),
        payload_lines.reshape(blocks, 32, attention_heads_number, embedding_extent),
        logarithmic_forgetting.reshape(blocks, 32, attention_heads_number, embedding_extent),
        doc_blocks,
        priors,
    )
    closing_memory, stratum_result = lax.scan(
        jax.checkpoint(partial(recursive_section, current_boost_param)),
        opening_memory,
        segment_parts,
    )
    return (
        stratum_result.reshape(length, attention_heads_number, embedding_extent),
        closing_memory,
    )


def state_terms(acceptance_lines, logarithmic_forgetting, segment_groups, preceding_segment):
    total = jnp.cumsum(logarithmic_forgetting, axis=0)
    before = total - logarithmic_forgetting
    carried = (segment_groups == preceding_segment).astype(jnp.float32)
    query_rows = acceptance_lines * jnp.exp(before) * carried[:, None, None]
    carry = jnp.exp(total[-1]) * (segment_groups[-1] == preceding_segment).astype(jnp.float32)
    return (query_rows, carry)


def wkv_full(
    acceptance_lines,
    lookup_lines,
    payload_lines,
    logarithmic_forgetting,
    blending_arrays,
    incoming_state,
    segment_groups=None,
    preceding_segment=None,
):
    attention_heads_number, embedding_extent = (
        acceptance_lines.shape[1],
        acceptance_lines.shape[2],
    )
    current_boost_param = blending_arrays[9].reshape(attention_heads_number, embedding_extent)
    raw_output, closing_memory = partitioned_recursion(
        acceptance_lines,
        lookup_lines,
        payload_lines,
        logarithmic_forgetting,
        current_boost_param,
        segment_groups,
        preceding_segment,
    )
    query_rows, carry = state_terms(
        acceptance_lines, logarithmic_forgetting, segment_groups, preceding_segment
    )
    raw_output = raw_output + jnp.einsum(
        "yco,cor->ycr", query_rows, incoming_state, precision=highest_precision
    )
    return (raw_output, carry[:, :, None] * incoming_state + closing_memory)


def chain(earlier, later):
    return (earlier[0] * later[0], later[0][:, :, None] * earlier[1] + later[1])


def send_rows(field):
    return from_behind(field[-1:], "seq", 1)


def back_rows(grad_first, field):
    arrived = from_behind(grad_first, "seq", -1)
    return field + jnp.concatenate(
        [jnp.zeros((field.shape[0] - 1, field.shape[1]), jnp.float32), arrived], axis=0
    )


def product(left_factor, right_factor):
    return jnp.dot(
        left_factor.astype(jnp.bfloat16), right_factor, preferred_element_type=jnp.float32
    )


def product_t(left_factor, right_factor):
    return lax.dot_general(
        left_factor, right_factor, (((0,), (0,)), ((), ())), preferred_element_type=jnp.float32
    )


def back_product(grad, weight):
    return lax.dot_general(
        grad, weight, (((1,), (1,)), ((), ())), preferred_element_type=jnp.float32
    )


def renew(weight, moment, average, grad, factor, total_tokens):
    rate = factor / math.sqrt(total_tokens)
    moment = 0.9 * moment + grad
    weight = weight - rate * (grad + 0.9 * moment)
    average = 0.8 * average + 0.2 * weight
    return (weight, moment, average)


def local(
    block_input,
    out_grad,
    lengths,
    vectors,
    vectors_moment,
    vectors_average,
    mix_weights,
    mix_moment,
    mix_average,
    ffn_key,
    ffn_key_moment,
    ffn_key_average,
    ffn_recept,
    ffn_recept_moment,
    ffn_recept_average,
    ffn_value,
    ffn_value_moment,
    ffn_value_average,
    maa_down,
    maa_down_moment,
    maa_down_average,
    maa_up,
    maa_up_moment,
    maa_up_average,
    decay_down,
    decay_down_moment,
    decay_down_average,
    decay_up,
    decay_up_moment,
    decay_up_average,
):
    length = block_input.shape[1]
    embedding_extent = block_input.shape[2]
    attention_heads_number = embedding_extent // CHANNELS_PER_HEM
    total_tokens = length * lax.axis_size("seq") * lax.axis_size("dp")
    first_pos = lax.axis_index("seq") * length
    split_at = lengths[0, 0]
    segment_groups = (first_pos + jnp.arange(length) >= split_at).astype(jnp.int32)
    preceding_segment = jnp.where(first_pos > 0, (first_pos - 1 >= split_at).astype(jnp.int32), -1)
    previous = jnp.concatenate([jnp.reshape(preceding_segment, (1,)), segment_groups[:-1]])
    follows = (segment_groups == previous).astype(jnp.float32)
    blending_arrays, mix_down_weight, mix_up_weight, ddown, dup = (
        lax.all_gather(vectors, ("seq", "dp"), axis=1, tiled=True),
        lax.all_gather(maa_down, ("seq", "dp"), axis=0, tiled=True),
        lax.all_gather(maa_up, ("seq", "dp"), axis=2, tiled=True),
        lax.all_gather(decay_down, ("seq", "dp"), axis=0, tiled=True),
        lax.all_gather(decay_up, ("seq", "dp"), axis=1, tiled=True),
    )
    time_full = lax.all_gather(mix_weights.astype(jnp.bfloat16), ("seq", "dp"), axis=1, tiled=True)
    hidden = block_input[0].astype(jnp.float32)
    normed = norm_first(hidden, blending_arrays)
    incoming = send_rows(normed)
    xkey, xval, xrec, xgate, logarithmic_forgetting = mix_inputs(
        normed, incoming, blending_arrays, mix_down_weight, mix_up_weight, ddown, dup, follows
    )
    lookup_lines = product(xkey, time_full[0])
    payload_lines = product(xval, time_full[1])
    acceptance_lines = product(xrec, time_full[2])
    gate = product(xgate, time_full[3])
    split_shape = (length, attention_heads_number, CHANNELS_PER_HEM)
    recept_h = acceptance_lines.reshape(split_shape)
    keys_h = lookup_lines.reshape(split_shape)
    values_h = payload_lines.reshape(split_shape)
    decay_h = logarithmic_forgetting.reshape(split_shape)
    local_raw_output, closing_memory = partitioned_recursion(
        recept_h,
        keys_h,
        values_h,
        decay_h,
        blending_arrays[9].reshape(attention_heads_number, CHANNELS_PER_HEM),
        segment_groups,
        preceding_segment,
    )
    query_rows, carry = state_terms(recept_h, decay_h, segment_groups, preceding_segment)
    identity = (jnp.ones_like(carry), jnp.zeros_like(closing_memory))
    incoming_state = prefix((carry, closing_memory), "seq", chain, identity, False)[1]
    raw_output = local_raw_output + jnp.einsum(
        "yco,cor->ycr", query_rows, incoming_state, precision=highest_precision
    )
    gated = gate_part(raw_output, gate, blending_arrays)
    attn = product(gated, time_full[4])
    middle = hidden + attn
    time_full = None
    chan_full = (
        lax.all_gather(ffn_key.astype(jnp.bfloat16), ("seq", "dp"), axis=0, tiled=True),
        lax.all_gather(ffn_recept.astype(jnp.bfloat16), ("seq", "dp"), axis=0, tiled=True),
        lax.all_gather(ffn_value.astype(jnp.bfloat16), ("seq", "dp"), axis=0, tiled=True),
    )
    second = norm_second(middle, blending_arrays)
    incoming_two = send_rows(second)
    key_in, rec_in = channel_inputs(second, incoming_two, blending_arrays, follows)
    kpre = product(key_in, chan_full[0])
    squared = jnp.square(jax.nn.relu(kpre))
    kvals = product(squared, chan_full[2])
    rpre = product(rec_in, chan_full[1])
    sigma = jax.nn.sigmoid(rpre)
    stratum_result = middle + sigma * kvals
    chan_full = None
    chan_back = (
        lax.all_gather(ffn_key.astype(jnp.bfloat16), ("seq", "dp"), axis=0, tiled=True),
        lax.all_gather(ffn_recept.astype(jnp.bfloat16), ("seq", "dp"), axis=0, tiled=True),
        lax.all_gather(ffn_value.astype(jnp.bfloat16), ("seq", "dp"), axis=0, tiled=True),
    )
    upstream = out_grad[0].astype(jnp.float32)
    grad_kvals = (upstream * sigma).astype(jnp.bfloat16)
    grad_rpre = (upstream * kvals * sigma * (1.0 - sigma)).astype(jnp.bfloat16)
    grad_fval = product_t(squared.astype(jnp.bfloat16), grad_kvals)
    grad_kpre = (back_product(grad_kvals, chan_back[2]) * 2.0 * jax.nn.relu(kpre)).astype(
        jnp.bfloat16
    )
    grad_fkey = product_t(key_in.astype(jnp.bfloat16), grad_kpre)
    grad_frec = product_t(rec_in.astype(jnp.bfloat16), grad_rpre)
    grad_key_in = back_product(grad_kpre, chan_back[0])
    grad_rec_in = back_product(grad_rpre, chan_back[1])
    chan_back = None
    part_fkey, part_frec, part_fval = (
        lax.psum_scatter(grad_fkey, "seq", scatter_dimension=0, tiled=True),
        lax.psum_scatter(grad_frec, "seq", scatter_dimension=0, tiled=True),
        lax.psum_scatter(grad_fval, "seq", scatter_dimension=0, tiled=True),
    )
    sum_fkey, sum_frec, sum_fval = (
        lax.psum_scatter(part_fkey, "dp", scatter_dimension=0, tiled=True),
        lax.psum_scatter(part_frec, "dp", scatter_dimension=0, tiled=True),
        lax.psum_scatter(part_fval, "dp", scatter_dimension=0, tiled=True),
    )
    spare, pull = jax.vjp(
        partial(channel_inputs, follows=follows), second, incoming_two, blending_arrays
    )
    grad_second, grad_inc_two, vec_one = pull((grad_key_in, grad_rec_in))
    grad_second = back_rows(grad_inc_two, grad_second)
    spare, pull = jax.vjp(norm_second, middle, blending_arrays)
    grad_mid, vec_two = pull(grad_second)
    grad_middle = upstream + grad_mid
    time_back = lax.all_gather(mix_weights.astype(jnp.bfloat16), ("seq", "dp"), axis=1, tiled=True)
    grad_attn = grad_middle.astype(jnp.bfloat16)
    grad_wout = product_t(gated.astype(jnp.bfloat16), grad_attn)
    grad_gated = back_product(grad_attn, time_back[4])
    spare, pull = jax.vjp(gate_part, raw_output, gate, blending_arrays)
    unscaled_gradient, grad_gate, vec_three = pull(grad_gated)
    direct_term = jnp.einsum(
        "ajg,ajs->jgs", query_rows, unscaled_gradient, precision=highest_precision
    )
    later_grads = prefix((carry, direct_term), "seq", chain, identity, True)[1]
    spare, pull = jax.vjp(
        partial(wkv_full, segment_groups=segment_groups, preceding_segment=preceding_segment),
        recept_h,
        keys_h,
        values_h,
        decay_h,
        blending_arrays,
        incoming_state,
    )
    grad_rec_h, grad_key_h, grad_val_h, grad_dec_h, vec_four, unused_state = pull(
        (unscaled_gradient, later_grads)
    )
    grad_keys = grad_key_h.reshape(length, embedding_extent).astype(jnp.bfloat16)
    grad_values = grad_val_h.reshape(length, embedding_extent).astype(jnp.bfloat16)
    grad_recept = grad_rec_h.reshape(length, embedding_extent).astype(jnp.bfloat16)
    grad_gate_b = grad_gate.astype(jnp.bfloat16)
    grad_mix = jnp.stack(
        [
            product_t(xkey.astype(jnp.bfloat16), grad_keys),
            product_t(xval.astype(jnp.bfloat16), grad_values),
            product_t(xrec.astype(jnp.bfloat16), grad_recept),
            product_t(xgate.astype(jnp.bfloat16), grad_gate_b),
            grad_wout,
        ]
    )
    grad_xkey = back_product(grad_keys, time_back[0])
    grad_xval = back_product(grad_values, time_back[1])
    grad_xrec = back_product(grad_recept, time_back[2])
    grad_xgate = back_product(grad_gate_b, time_back[3])
    time_back = None
    spare, pull = jax.vjp(
        partial(mix_inputs, follows=follows),
        normed,
        incoming,
        blending_arrays,
        mix_down_weight,
        mix_up_weight,
        ddown,
        dup,
    )
    grad_normed, grad_inc, vec_five, grad_mdown, grad_mup, grad_ddown, grad_dup = pull(
        (grad_xkey, grad_xval, grad_xrec, grad_xgate, grad_dec_h.reshape(length, embedding_extent))
    )
    grad_normed = back_rows(grad_inc, grad_normed)
    spare, pull = jax.vjp(norm_first, hidden, blending_arrays)
    grad_hidden, vec_six = pull(grad_normed)
    input_grad = grad_middle + grad_hidden
    grad_vecs = vec_one + vec_two + vec_three + vec_four + vec_five + vec_six
    part_mix, part_vecs, part_mdown, part_mup, part_ddown, part_dup = (
        lax.psum_scatter(grad_mix, "seq", scatter_dimension=1, tiled=True),
        lax.psum_scatter(grad_vecs, "seq", scatter_dimension=1, tiled=True),
        lax.psum_scatter(grad_mdown, "seq", scatter_dimension=0, tiled=True),
        lax.psum_scatter(grad_mup, "seq", scatter_dimension=2, tiled=True),
        lax.psum_scatter(grad_ddown, "seq", scatter_dimension=0, tiled=True),
        lax.psum_scatter(grad_dup, "seq", scatter_dimension=1, tiled=True),
    )
    sum_mix, sum_vecs, sum_mdown, sum_mup, sum_ddown, sum_dup = (
        lax.psum_scatter(part_mix, "dp", scatter_dimension=1, tiled=True),
        lax.psum_scatter(part_vecs, "dp", scatter_dimension=1, tiled=True),
        lax.psum_scatter(part_mdown, "dp", scatter_dimension=0, tiled=True),
        lax.psum_scatter(part_mup, "dp", scatter_dimension=2, tiled=True),
        lax.psum_scatter(part_ddown, "dp", scatter_dimension=0, tiled=True),
        lax.psum_scatter(part_dup, "dp", scatter_dimension=1, tiled=True),
    )
    params = (
        vectors,
        mix_weights,
        ffn_key,
        ffn_recept,
        ffn_value,
        maa_down,
        maa_up,
        decay_down,
        decay_up,
    )
    moments = (
        vectors_moment,
        mix_moment,
        ffn_key_moment,
        ffn_recept_moment,
        ffn_value_moment,
        maa_down_moment,
        maa_up_moment,
        decay_down_moment,
        decay_up_moment,
    )
    averages = (
        vectors_average,
        mix_average,
        ffn_key_average,
        ffn_recept_average,
        ffn_value_average,
        maa_down_average,
        maa_up_average,
        decay_down_average,
        decay_up_average,
    )
    summed = (
        sum_vecs,
        sum_mix,
        sum_fkey,
        sum_frec,
        sum_fval,
        sum_mdown,
        sum_mup,
        sum_ddown,
        sum_dup,
    )
    results = [stratum_result[None], input_grad[None]]
    for index in range(9):
        results.extend(
            renew(
                params[index],
                moments[index],
                averages[index],
                summed[index],
                factors[index],
                total_tokens,
            )
        )
    return tuple(results)


def solution(mesh):
    in_specs = (
        P("dp", "seq", None),
        P("dp", "seq", None),
        P("dp", None),
        P(None, ("seq", "dp")),
        P(None, ("seq", "dp")),
        P(None, ("seq", "dp")),
        P(None, ("seq", "dp"), None),
        P(None, ("seq", "dp"), None),
        P(None, ("seq", "dp"), None),
        P(("seq", "dp"), None),
        P(("seq", "dp"), None),
        P(("seq", "dp"), None),
        P(("seq", "dp"), None),
        P(("seq", "dp"), None),
        P(("seq", "dp"), None),
        P(("seq", "dp"), None),
        P(("seq", "dp"), None),
        P(("seq", "dp"), None),
        P(("seq", "dp"), None),
        P(("seq", "dp"), None),
        P(("seq", "dp"), None),
        P(None, None, ("seq", "dp")),
        P(None, None, ("seq", "dp")),
        P(None, None, ("seq", "dp")),
        P(("seq", "dp"), None),
        P(("seq", "dp"), None),
        P(("seq", "dp"), None),
        P(None, ("seq", "dp")),
        P(None, ("seq", "dp")),
        P(None, ("seq", "dp")),
    )
    out_specs = (
        P("dp", "seq", None),
        P("dp", "seq", None),
        P(None, ("seq", "dp")),
        P(None, ("seq", "dp")),
        P(None, ("seq", "dp")),
        P(None, ("seq", "dp"), None),
        P(None, ("seq", "dp"), None),
        P(None, ("seq", "dp"), None),
        P(("seq", "dp"), None),
        P(("seq", "dp"), None),
        P(("seq", "dp"), None),
        P(("seq", "dp"), None),
        P(("seq", "dp"), None),
        P(("seq", "dp"), None),
        P(("seq", "dp"), None),
        P(("seq", "dp"), None),
        P(("seq", "dp"), None),
        P(("seq", "dp"), None),
        P(("seq", "dp"), None),
        P(("seq", "dp"), None),
        P(None, None, ("seq", "dp")),
        P(None, None, ("seq", "dp")),
        P(None, None, ("seq", "dp")),
        P(("seq", "dp"), None),
        P(("seq", "dp"), None),
        P(("seq", "dp"), None),
        P(None, ("seq", "dp")),
        P(None, ("seq", "dp")),
        P(None, ("seq", "dp")),
    )
    return jax.shard_map(local, mesh=mesh, in_specs=in_specs, out_specs=out_specs, check_vma=False)
```

profile of v0, /device:TPU:0, one launch (start us, length us, event | category | flops | bytes accessed | tf_op | source)
XLA Modules:
  0.0 5329.1 jit_solution(5788579380354676472)
XLA Ops:
  12.9 73.0 %all-gather.2 = f32[32,64,16]{1,2,0:T(8,128)S(1)} all-gather(f32[1,64,16]{1,2,0:T(8,128)S(1)} %bitcast.766), channel_id=1, replica_groups=mesh['seq'=4,'dp'=8] {'seq','dp'}, dimensions={0}, use_global_device_ids=true | all-gather | bytes 135168 | tf_op jit(solution)/shard_map/all_gather | solution.py:290
  91.0 76.6 %all_gather.52 = f32[2048,64]{1,0:T(8,128)} all-gather(f32[64,64]{1,0:T(8,128)S(1)} %copy-done.117), channel_id=1, replica_groups=mesh['seq'=4,'dp'=8] {'seq','dp'}, dimensions={0}, use_global_device_ids=true | all-gather | bytes 540672 | tf_op jit(solution)/shard_map/all_gather | solution.py:293
  167.6 87.2 %all_gather.53 = f32[64,2048]{0,1:T(8,128)} all-gather(f32[64,64]{0,1:T(8,128)S(1)} %copy.591), channel_id=1, replica_groups=mesh['seq'=4,'dp'=8] {'seq','dp'}, dimensions={1}, use_global_device_ids=true | all-gather | bytes 540672 | tf_op jit(solution)/shard_map/all_gather | solution.py:294
  270.7 15.6 fusion.193
  301.3 97.0 %all-gather.16.cloned.1.call-done = bf16[5,2048,2048]{2,1,0:T(8,128)(2,1)} async-done(((bf16[5,64,2048]{2,1,0:T(8,128)(2,1)}), bf16[5,2048,2048]{2,1,0:T(8,128)(2,1)}) %all-gather.16.cloned.1.call-update) | async-done | bytes 41943056 | tf_op jit(solution)/shard_map/all_gather | solution.py:296
  398.3 11.9 slice_bitcast_fusion.11
  410.2 12.3 copy.592
  433.9 12.2 copy.593
  466.2 337.7 %while.81 = (s32[]{:T(128)}, f32[32,64,64]{2,1,0:T(8,128)S(1)}, f32[8,32,32,64]{3,2,1,0:T(8,128)}, f32[8,32,32,64]{3,2,1,0:T(8,128)}, s32[8,32]{1,0:T(8,128)S(1)...) while((s32[]{:T(128)}, f32[32,64,64]{2,1,0:T(8,128)S(1)}, ...), condition=%wide.region_5.6_spmd.clone, body=%wide.region_2.5_spmd.clone.sunk | while | flops 141726848 | bytes 28169932 | solution.py:153
  479.0 18.1 fusion.320
  521.2 18.1 fusion.320
  563.4 18.1 fusion.320
  605.5 18.1 fusion.320
  647.7 18.1 fusion.320
  689.8 18.1 fusion.320
  732.0 18.1 fusion.320
  774.2 18.1 fusion.320
  816.7 64.4 %reduce-window.14 = f32[64,32,2,128]{3,1,2,0:T(8,128)S(1)} reduce-window(f32[64,32,2,128]{3,1,2,0:T(8,128)} %copy.598, f32[]{:T(128)} %constant.243.clone.1), window={size=1x1x1x128 pad=0_0x0_0x0_0x127_0}, to_apply=%region_6.7 | reduce-window | flops 66584576 | bytes 4194308 | tf_op jit(solution)/shard_map/reduce-window
  965.6 50.6 all-gather.20.cloned.1.call-done
  1016.3 15.4 convolution_maximum_fusion
  1031.6 63.8 %all-gather.18.cloned.1.call-done = bf16[2048,2048]{1,0:T(8,128)(2,1)} async-done(((bf16[64,2048]{1,0:T(8,128)(2,1)}), bf16[2048,2048]{1,0:T(8,128)(2,1)}) %all-gather.18.cloned.1.call-update) | async-done | bytes 8388624 | tf_op jit(solution)/shard_map/all_gather | solution.py:333
  1102.9 23.6 fusion.147
  1126.6 396.4 %reduce-scatter.43.cloned.1.call-done = f32[1792,2048]{1,0:T(8,128)} async-done(((f32[7168,2048]{1,0:T(8,128)}), f32[1792,2048]{1,0:T(8,128)}) %reduce-scatter.43.cloned.1.call-update) | async-done | bytes 14680080 | tf_op jit(solution)/shard_map/reduce_scatter | solution.py:366
  1523.1 240.5 %reduce-scatter.45.cloned.1.call-done = f32[224,2048]{1,0:T(8,128)} async-done(((f32[1792,2048]{1,0:T(8,128)}), f32[224,2048]{1,0:T(8,128)}) %reduce-scatter.45.cloned.1.call-update) | async-done | bytes 1835024 | tf_op jit(solution)/shard_map/reduce_scatter | solution.py:371
  1771.2 174.0 %all-gather.22.cloned.1.call-done = bf16[7168,2048]{1,0:T(8,128)(2,1)} async-done(((bf16[224,2048]{1,0:T(8,128)(2,1)}), bf16[7168,2048]{1,0:T(8,128)(2,1)}) %all-gather.22.cloned.1.call-update) | async-done | bytes 29360144 | tf_op jit(solution)/shard_map/all_gather | solution.py:334
  1945.2 17.9 fusion.90
  1963.1 17.3 fusion.138
  1980.4 13.9 fusion.203
  2039.9 90.0 %while.84 = (s32[]{:T(128)}, f32[32,64,64]{2,1,0:T(8,128)S(1)}, f32[8,32,64,64]{3,2,1,0:T(8,128)}, f32[8,32,32,64]{3,2,1,0:T(8,128)}, s32[8,32]{1,0:T(8,128)}, /...) while((s32[]{:T(128)}, f32[32,64,64]{2,1,0:T(8,128)S(1)}, ...), condition=%wide.region_22.23_spmd.clone, body=%wide.region_20.22_spmd.clone.sunk | while | flops 53086276 | bytes 5032230 | solution.py:153
  2153.2 10.4 while.83
  2172.4 639.1 %while.85 = (s32[]{:T(128)}, f32[32,64]{1,0:T(8,128)S(1)}, f32[32,64,64]{2,1,0:T(8,128)S(1)}, f32[8,32,32,64]{3,2,1,0:T(8,128)}, bf16[8,32,32,64]{3,1,2,0:T(8,12...) while((s32[]{:T(128)}, f32[32,64]{1,0:T(8,128)S(1)}, ...), condition=%wide.region_33.34_spmd.clone, body=%wide.region_23.33_spmd.clone.sunk | while | flops 309045440 | bytes 48465852 | solution.py:153
  2206.5 9.3 fusion.350
  2218.5 18.5 fusion.349
  2286.3 9.3 fusion.350
  2298.3 18.5 fusion.349
  2366.1 9.3 fusion.350
  2378.1 18.5 fusion.349
  2457.9 18.5 fusion.349
  2537.8 18.5 fusion.349
  2617.6 18.5 fusion.349
  2697.4 18.5 fusion.349
  2777.2 18.5 fusion.349
  2812.2 12.2 pad_add_fusion.1
  2829.7 159.8 %reduce-window.16 = f32[64,32,2,128]{3,1,2,0:T(8,128)S(1)} reduce-window(f32[64,32,2,128]{3,1,2,0:T(8,128)} %copy.622, f32[]{:T(128)} %constant.243.clone.1), window={size=1x1x1x128 pad=0_0x0_0x0_0x0_127}, to_apply=%region_35.36 | reduce-window | flops 66584576 | bytes 4194308 | tf_op jit(solution)/shard_map/reduce-window.2
  3056.9 10.1 fusion.83
  3099.9 9.8 fusion.81
  3113.0 9.8 fusion.206
  3124.0 22.6 fusion.205
  3147.9 9.4 bitcast_dynamic-update-slice_fusion.6
  3157.3 9.5 bitcast_dynamic-update-slice_fusion.5
  3166.8 9.7 bitcast_dynamic-update-slice_fusion.4
  3176.5 9.9 bitcast_dynamic-update-slice_fusion.3
  3203.4 17.6 reduce-scatter.47.cloned.1.call-done
  3223.1 126.6 %reduce-scatter.39.cloned.1.call-done = f32[512,2048]{1,0:T(8,128)} async-done(((f32[2048,2048]{1,0:T(8,128)}), f32[512,2048]{1,0:T(8,128)}) %reduce-scatter.39.cloned.1.call-update) | async-done | bytes 4194320 | tf_op jit(solution)/shard_map/reduce_scatter | solution.py:365
  3349.7 400.3 %reduce-scatter.35.cloned.1.call-done = f32[512,7168]{1,0:T(8,128)} async-done(((f32[2048,7168]{1,0:T(8,128)}), f32[512,7168]{1,0:T(8,128)}) %reduce-scatter.35.cloned.1.call-update) | async-done | bytes 14680080 | tf_op jit(solution)/shard_map/reduce_scatter | solution.py:364
  3750.1 562.4 %reduce-scatter.31.cloned.1.call-done = f32[5,512,2048]{2,1,0:T(8,128)} async-done(((f32[5,2048,2048]{2,1,0:T(8,128)}), f32[5,512,2048]{2,1,0:T(8,128)}) %reduce-scatter.31.cloned.1.call-update) | async-done | bytes 20971536 | tf_op jit(solution)/shard_map/reduce_scatter | solution.py:440
  4321.1 57.0 %reduce-scatter.55.cloned.1.call-done = f32[64,16]{1,0:T(8,128)} async-done(((f32[512,16]{1,0:T(8,128)}), f32[64,16]{1,0:T(8,128)}) %reduce-scatter.55.cloned.1.call-update) | async-done | bytes 4112
  4380.2 62.2 %reduce-scatter.63.cloned.1.call-done = f32[64,64]{1,0:T(8,128)} async-done(((f32[512,64]{1,0:T(8,128)}), f32[64,64]{1,0:T(8,128)}) %reduce-scatter.63.cloned.1.call-update) | async-done | bytes 16400
  4445.3 61.7 %reduce-scatter.61.cloned.1.call-done = f32[64,64]{1,0:T(8,128)} async-done(((f32[512,64]{1,0:T(8,128)}), f32[64,64]{1,0:T(8,128)}) %reduce-scatter.61.cloned.1.call-update) | async-done | bytes 16400
  4510.0 62.4 %reduce-scatter.59.cloned.1.call-done = f32[64,160]{1,0:T(8,128)} async-done(((f32[512,160]{1,0:T(8,128)}), f32[64,160]{1,0:T(8,128)}) %reduce-scatter.59.cloned.1.call-update) | async-done | bytes 40976
  4573.4 63.8 %reduce-scatter.57.cloned.1.call-done = f32[64,160]{1,0:T(8,128)} async-done(((f32[512,160]{1,0:T(8,128)}), f32[64,160]{1,0:T(8,128)}) %reduce-scatter.57.cloned.1.call-update) | async-done | bytes 40976
  4641.1 87.2 %reduce-scatter.41.cloned.1.call-done = f32[64,2048]{1,0:T(8,128)} async-done(((f32[512,2048]{1,0:T(8,128)}), f32[64,2048]{1,0:T(8,128)}) %reduce-scatter.41.cloned.1.call-update) | async-done | bytes 524304 | tf_op jit(solution)/shard_map/reduce_scatter | solution.py:370
  4730.6 237.5 %reduce-scatter.37.cloned.1.call-done = f32[64,7168]{1,0:T(8,128)} async-done(((f32[512,7168]{1,0:T(8,128)}), f32[64,7168]{1,0:T(8,128)}) %reduce-scatter.37.cloned.1.call-update) | async-done | bytes 1835024 | tf_op jit(solution)/shard_map/reduce_scatter | solution.py:369
  4974.3 340.4 %reduce-scatter.33.cloned.1.call-done = f32[5,64,2048]{2,1,0:T(8,128)} async-done(((f32[5,512,2048]{2,1,0:T(8,128)}), f32[5,64,2048]{2,1,0:T(8,128)}) %reduce-scatter.33.cloned.1.call-update) | async-done | bytes 2621456 | tf_op jit(solution)/shard_map/reduce_scatter | solution.py:448
  (1374 shorter events, 1158.3 us)
Async XLA Ops:
  7.2 251.1 %all-gather.14.cloned.1.call-start = ((), (), s32[]{:S(2)}) async-start(), calls=%async_computation.19 | async-start | bytes 8650752 | tf_op jit(solution)/shard_map/all_gather | solution.py:292
  9.0 255.6 %all-gather.12.cloned.1.call-start = ((), (), s32[]{:S(2)}) async-start(), calls=%async_computation.18 | async-start | bytes 2162688 | tf_op jit(solution)/shard_map/all_gather | solution.py:291
  9.8 388.6 %all-gather.16.cloned.1.call-start = ((), (), s32[]{:S(2)}) async-start(), calls=%async_computation.20 | async-start | bytes 43253760 | tf_op jit(solution)/shard_map/all_gather | solution.py:296
  12.8 73.3 %copy-start.11 = (bf16[1,256,2048]{2,1,0:T(8,128)(2,1)S(1)}, bf16[1,256,2048]{2,1,0:T(8,128)(2,1)}, u32[]{:S(2)}) copy-start(bf16[1,256,2048]{2,1,0:T(8,128)(2,1)} %param.40) | copy-start | bytes 3145732
  12.8 914.4 %all-gather.24.cloned.1.call-start = ((), (), s32[]{:S(2)}) async-start(), calls=%async_computation.37 | async-start | bytes 5242880 | tf_op jit(solution)/shard_map/all_gather | solution.py:24
  86.4 178.3 %copy-start.119 = (f32[256]{0:T(256)}, f32[256]{0:T(256)S(1)}, u32[]{:S(2)}) copy-start(f32[256]{0:T(256)S(1)} %broadcast_multiply_fusion.4) | copy-start | bytes 3076
  86.8 177.8 %copy-start.125 = (f32[256]{0:T(256)}, f32[256]{0:T(256)S(1)}, u32[]{:S(2)}) copy-start(f32[256]{0:T(256)S(1)} %fusion.170) | copy-start | bytes 3076
  88.1 176.5 %copy-start.96 = (f32[1,2048]{1,0:T(1,128)}, f32[1,2048]{1,0:T(1,128)S(1)}, u32[]{:S(2)}) copy-start(f32[1,2048]{1,0:T(1,128)S(1)} %get-tuple-element.1556) | copy-start | bytes 24580
  88.1 176.5 %copy-start.109 = (f32[1,2048]{1,0:T(1,128)}, f32[1,2048]{1,0:T(1,128)S(1)}, u32[]{:S(2)}) copy-start(f32[1,2048]{1,0:T(1,128)S(1)} %get-tuple-element.1555) | copy-start | bytes 24580
  88.1 176.5 %copy-start.112 = (f32[1,2048]{1,0:T(1,128)}, f32[1,2048]{1,0:T(1,128)S(1)}, u32[]{:S(2)}) copy-start(f32[1,2048]{1,0:T(1,128)S(1)} %get-tuple-element.1554) | copy-start | bytes 24580
  88.6 166.3 %copy-start.33 = (f32[256,2048]{1,0:T(8,128)}, f32[256,2048]{1,0:T(8,128)S(1)}, u32[]{:S(2)}) copy-start(f32[256,2048]{1,0:T(8,128)S(1)} %fusion.129) | copy-start | bytes 6291460
  88.6 166.3 %collective-permute-start = (f32[1,2048]{1,0:T(1,128)S(1)}, f32[1,2048]{1,0:T(1,128)S(1)}, u32[]{:S(2)}, u32[]{:S(2)}) collective-permute-start(f32[1,2048]{1,0:T(1,128)S(1)} %slice.211), channel_id=1, source_target_pairs={{0,8},{8,16},{16,24},{1,9},{9,17},{17,25},{2,10},{10,18},{18,26},{... | collective-permute-start | bytes 24584 | tf_op jit(solution)/shard_map/ppermute | solution.py:19
  90.1 164.7 %copy-start.105 = (f32[64,64]{0,1:T(8,128)}, f32[64,64]{0,1:T(8,128)S(1)}, u32[]{:S(2)}) copy-start(f32[64,64]{0,1:T(8,128)S(1)} %copy.591) | copy-start | bytes 49156
  90.8 167.5 %copy-start.143 = (f32[256]{0:T(256)}, f32[256]{0:T(256)S(1)}, u32[]{:S(2)}) copy-start(f32[256]{0:T(256)S(1)} %compare_convert_fusion.6) | copy-start | bytes 3076
  270.7 19.6 copy-start.52
  804.9 211.4 %all-gather.20.cloned.1.call-start = ((), (), s32[]{:S(2)}) async-start(), calls=%async_computation.22 | async-start | bytes 30277632 | tf_op jit(solution)/shard_map/all_gather | solution.py:332
  807.6 287.8 %all-gather.18.cloned.1.call-start = ((), (), s32[]{:S(2)}) async-start(), calls=%async_computation.21 | async-start | bytes 8650752 | tf_op jit(solution)/shard_map/all_gather | solution.py:333
  808.5 714.6 %reduce-scatter.43.cloned.1.call-start = ((), (), s32[]{:S(2)}) async-start(), calls=%async_computation.31 | async-start | bytes 73400320 | tf_op jit(solution)/shard_map/reduce_scatter | solution.py:366
  959.2 1003.9 %copy-start.22 = (f32[256,2048]{1,0:T(8,128)}, f32[256,2048]{1,0:T(8,128)S(1)}, u32[]{:S(2)}) copy-start(f32[256,2048]{1,0:T(8,128)S(1)} %get-tuple-element.1568) | copy-start | bytes 6291460
  960.5 3.0 collective-permute-start.1
  965.6 66.0 %copy-start.69 = (bf16[256,2048]{1,0:T(8,128)(2,1)}, bf16[256,2048]{1,0:T(8,128)(2,1)S(1)}, u32[]{:S(2)}) copy-start(bf16[256,2048]{1,0:T(8,128)(2,1)S(1)} %get-tuple-element.1537) | copy-start | bytes 3145732
  1126.6 637.1 %reduce-scatter.45.cloned.1.call-start = ((), (), s32[]{:S(2)}) async-start(), calls=%async_computation.32 | async-start | bytes 16515072 | tf_op jit(solution)/shard_map/reduce_scatter | solution.py:371
  1523.1 422.1 %all-gather.22.cloned.1.call-start = ((), (), s32[]{:S(2)}) async-start(), calls=%async_computation.23 | async-start | bytes 30277632 | tf_op jit(solution)/shard_map/all_gather | solution.py:334
  1771.2 382.1 %all-gather.26.cloned.1.call-start = ((), (), s32[]{:S(2)}) async-start(), calls=%async_computation.38 | async-start | bytes 5242880 | tf_op jit(solution)/shard_map/all_gather | solution.py:24
  2004.8 3.8 collective-permute-start.2
  2039.7 1155.1 %reduce-scatter.29.cloned.1.call-start = ((), (), s32[]{:S(2)}) async-start(), calls=%async_computation.24 | async-start | bytes 163840 | tf_op jit(solution)/shard_map/reduce_scatter | solution.py:441
  2172.4 639.8 %copy-start.147 = (f32[256]{0:T(256)S(1)}, f32[256]{0:T(256)}, u32[]{:S(2)}) copy-start(f32[256]{0:T(256)} %get-tuple-element.1571) | copy-start | bytes 3076
  2218.4 18.5 copy-start.3
  2218.5 18.5 copy-start.7
  2298.2 18.5 copy-start.3
  2298.3 18.5 copy-start.7
  2378.0 18.5 copy-start.3
  2378.0 18.5 copy-start.7
  2457.9 18.5 copy-start.3
  2537.7 18.5 copy-start.3
  2617.5 18.5 copy-start.3
  2697.3 18.5 copy-start.3
  2777.1 18.5 copy-start.3
  3043.5 23.5 copy-start.64
  3078.5 4.5 collective-permute-start.3
  3091.2 105.3 %reduce-scatter.53.cloned.1.call-start = ((), (), s32[]{:S(2)}) async-start(), calls=%async_computation.36 | async-start | bytes 655360 | tf_op jit(solution)/shard_map/reduce_scatter | solution.py:445
  3095.7 102.6 %reduce-scatter.51.cloned.1.call-start = ((), (), s32[]{:S(2)}) async-start(), calls=%async_computation.35 | async-start | bytes 655360 | tf_op jit(solution)/shard_map/reduce_scatter | solution.py:444
  3099.9 100.5 %reduce-scatter.49.cloned.1.call-start = ((), (), s32[]{:S(2)}) async-start(), calls=%async_computation.34 | async-start | bytes 1638400 | tf_op jit(solution)/shard_map/reduce_scatter | solution.py:443
  3109.8 111.2 %reduce-scatter.47.cloned.1.call-start = ((), (), s32[]{:S(2)}) async-start(), calls=%async_computation.33 | async-start | bytes 1638400 | tf_op jit(solution)/shard_map/reduce_scatter | solution.py:442
  3112.9 236.7 %reduce-scatter.39.cloned.1.call-start = ((), (), s32[]{:S(2)}) async-start(), calls=%async_computation.29 | async-start | bytes 20971520 | tf_op jit(solution)/shard_map/reduce_scatter | solution.py:365
  3122.8 627.2 %reduce-scatter.35.cloned.1.call-start = ((), (), s32[]{:S(2)}) async-start(), calls=%async_computation.27 | async-start | bytes 73400320 | tf_op jit(solution)/shard_map/reduce_scatter | solution.py:364
  3146.7 1165.9 %reduce-scatter.31.cloned.1.call-start = ((), (), s32[]{:S(2)}) async-start(), calls=%async_computation.25 | async-start | bytes 104857600 | tf_op jit(solution)/shard_map/reduce_scatter | solution.py:440
  3194.7 1183.3 %reduce-scatter.55.cloned.1.call-start = ((), (), s32[]{:S(2)}) async-start(), calls=%async_computation.39 | async-start | bytes 294912
  3196.4 1246.0 %reduce-scatter.63.cloned.1.call-start = ((), (), s32[]{:S(2)}) async-start(), calls=%async_computation.43 | async-start | bytes 294912
  3198.3 1308.7 %reduce-scatter.61.cloned.1.call-start = ((), (), s32[]{:S(2)}) async-start(), calls=%async_computation.42 | async-start | bytes 294912
  3200.1 1372.2 %reduce-scatter.59.cloned.1.call-start = ((), (), s32[]{:S(2)}) async-start(), calls=%async_computation.41 | async-start | bytes 589824
  3203.3 1433.9 %reduce-scatter.57.cloned.1.call-start = ((), (), s32[]{:S(2)}) async-start(), calls=%async_computation.40 | async-start | bytes 589824
  3223.0 1505.2 %reduce-scatter.41.cloned.1.call-start = ((), (), s32[]{:S(2)}) async-start(), calls=%async_computation.30 | async-start | bytes 4718592 | tf_op jit(solution)/shard_map/reduce_scatter | solution.py:370
  3349.6 1618.5 %reduce-scatter.37.cloned.1.call-start = ((), (), s32[]{:S(2)}) async-start(), calls=%async_computation.28 | async-start | bytes 16515072 | tf_op jit(solution)/shard_map/reduce_scatter | solution.py:369
  3750.0 1564.6 %reduce-scatter.33.cloned.1.call-start = ((), (), s32[]{:S(2)}) async-start(), calls=%async_computation.26 | async-start | bytes 23592960 | tf_op jit(solution)/shard_map/reduce_scatter | solution.py:448
  4316.9 62.0 %copy-start.135 = (f32[16,64]{1,0:T(8,128)S(1)}, f32[16,64]{1,0:T(8,128)}, u32[]{:S(2)}) copy-start(f32[16,64]{1,0:T(8,128)} %param.43) | copy-start | bytes 12292
  4316.9 125.5 %copy-start.106 = (f32[64,64]{0,1:T(8,128)S(1)}, f32[64,64]{0,1:T(8,128)}, u32[]{:S(2)}) copy-start(f32[64,64]{0,1:T(8,128)} %copy-done.105) | copy-start | bytes 49156
  4321.0 319.3 %copy-start.102 = (f32[5,32,64]{2,1,0:T(8,128)S(1)}, f32[5,32,64]{2,1,0:T(8,128)}, u32[]{:S(2)}) copy-start(f32[5,32,64]{2,1,0:T(8,128)} %param.61) | copy-start | bytes 122884
  4321.0 319.3 %copy-start.121 = (f32[5,32,64]{2,1,0:T(8,128)S(1)}, f32[5,32,64]{2,1,0:T(8,128)}, u32[]{:S(2)}) copy-start(f32[5,32,64]{2,1,0:T(8,128)} %param.63) | copy-start | bytes 122884
  4321.0 319.3 %copy-start.122 = (f32[5,32,64]{2,1,0:T(8,128)S(1)}, f32[5,32,64]{2,1,0:T(8,128)}, u32[]{:S(2)}) copy-start(f32[5,32,64]{2,1,0:T(8,128)} %param.62) | copy-start | bytes 122884
  4321.0 407.2 %copy-start.82 = (f32[64,2048]{1,0:T(8,128)S(1)}, f32[64,2048]{1,0:T(8,128)}, u32[]{:S(2)}) copy-start(f32[64,2048]{1,0:T(8,128)} %param.52) | copy-start | bytes 1572868
  4321.0 407.2 %copy-start.100 = (f32[64,2048]{1,0:T(8,128)S(1)}, f32[64,2048]{1,0:T(8,128)}, u32[]{:S(2)}) copy-start(f32[64,2048]{1,0:T(8,128)} %param.54) | copy-start | bytes 1572868
  4321.0 407.2 %copy-start.101 = (f32[64,2048]{1,0:T(8,128)S(1)}, f32[64,2048]{1,0:T(8,128)}, u32[]{:S(2)}) copy-start(f32[64,2048]{1,0:T(8,128)} %param.53) | copy-start | bytes 1572868
  4730.6 584.1 %copy-start.48 = (f32[5,64,2048]{2,1,0:T(8,128)S(1)}, f32[5,64,2048]{2,1,0:T(8,128)}, u32[]{:S(2)}) copy-start(f32[5,64,2048]{2,1,0:T(8,128)} %param.46) | copy-start | bytes 7864324
  (236 other events, 1612.2 us)
Sparse Core Ops, SparseCore 0:
  11.6 81.6 all-gather.13
  96.2 57.3 all-gather.11
  157.2 241.1 all-gather.15
  805.0 32.7 all-gather.23
  841.1 175.1 all-gather.19
  1019.7 75.6 all-gather.17
  1126.7 396.2 reduce-scatter.42
  1527.1 236.5 reduce-scatter.44
  1771.3 173.8 all-gather.21
  2039.8 34.5 all-gather.25
  3091.3 20.9 reduce-scatter.28
  3115.2 21.6 reduce-scatter.52
  3140.1 21.6 reduce-scatter.50
  3164.8 26.5 reduce-scatter.48
  3194.5 26.5 reduce-scatter.46
  3223.4 126.1 reduce-scatter.38
  3352.2 397.7 reduce-scatter.34
  3752.5 559.9 reduce-scatter.30
  4316.8 61.2 reduce-scatter.54
  4382.1 60.2 reduce-scatter.62
  4446.7 60.2 reduce-scatter.60
  4511.3 61.0 reduce-scatter.58
  4576.3 60.8 reduce-scatter.56
  4641.1 87.0 reduce-scatter.40
  4731.8 236.2 reduce-scatter.36
  4971.9 342.7 reduce-scatter.32
where the time goes:
time: 5350 us; the launch traced here: 5330 us
  waiting for transfers between devices  3100 us (58%)
  other arithmetic  948 us (18%)
  matrix products  549 us (10%)
  local copies, waits for them, and re-layouts  425 us (8%)
  blocking collectives  242 us (5%)
    reduce_scatter x1, waiting for transfers between devices, local(): lax.psum_scatter(grad_mix, 'seq', scatter_dimension=1, tiled=True)  562 us
    reduce_scatter x1, waiting for transfers between devices, local(): lax.psum_scatter(grad_fkey, 'seq', scatter_dimension=0, tiled=True)  400 us
    reduce_scatter x1, waiting for transfers between devices, local(): lax.psum_scatter(grad_fval, 'seq', scatter_dimension=0, tiled=True)  396 us
    reduce_scatter x1, waiting for transfers between devices, local(): lax.psum_scatter(part_mix, 'dp', scatter_dimension=1, tiled=True)  340 us
    unnamed x31, waiting for transfers between devices  308 us
    reduce_scatter x1, waiting for transfers between devices, local(): lax.psum_scatter(part_fval, 'dp', scatter_dimension=0, tiled=True)  241 us
    reduce_scatter x1, waiting for transfers between devices, local(): lax.psum_scatter(part_fkey, 'dp', scatter_dimension=0, tiled=True)  238 us
    another operation x6, other arithmetic  228 us
  transfers between devices with their start and end apart: 30, of which 19 were waited for; matrix products, arithmetic and copies ran while one was open for 9% of the time, Pallas kernels for 0%

commit v1 on v0

v1 whole, which is shorter than its diff:
```python
import functools
import math

import jax
import jax.numpy as jnp
import numpy as np
from jax import lax
from jax.experimental import pallas as pl
from jax.experimental.pallas import tpu as pltpu
from jax.sharding import PartitionSpec as P

HEAD = 64
LANES = 128
CHUNK = 64
BF = jnp.bfloat16
F32 = jnp.float32
NN = (((1,), (0,)), ((), ()))
NT = (((1,), (1,)), ((), ()))
TN = (((0,), (0,)), ((), ()))


def levels_of(chunk):
    return [1 << e for e in reversed(range(chunk.bit_length() - 1))]


def tables(chunk):
    levels = levels_of(chunk)
    at = np.arange(chunk)
    sums = []
    for m in levels[:-1]:
        same = at[:, None] // (2 * m) == at[None, :] // (2 * m)
        right = (at & m) > 0
        up = same & right[:, None] & right[None, :] & (at[None, :] < at[:, None])
        down = same & ~right[:, None] & ~right[None, :] & (at[None, :] > at[:, None])
        sums.append(up | down)
    sums.append(at[None, :] < at[:, None])
    sums.append(at[None, :] > at[:, None])
    sums = np.concatenate(sums, 0).astype(np.float32)
    level = np.full((chunk, chunk), -1, np.int32)
    for index, m in enumerate(levels):
        same = at[:, None] // (2 * m) == at[None, :] // (2 * m)
        right = (at & m) > 0
        level = np.where(same & (right[:, None] != right[None, :]), index, level)
    level = np.concatenate([level, level], 1)
    ones = (np.arange(LANES)[:, None] // HEAD == np.arange(LANES)[None, :] // HEAD).astype(np.float32)
    return sums, level, ones


def split(value, parts):
    pieces = []
    for _ in range(parts):
        piece = value.astype(BF)
        pieces.append(piece)
        value = value - piece.astype(F32)
    return pieces


def dot3(left, right, dims):
    lh, ll = left
    rh, rl = right
    la, ra = dims[0][0][0], dims[0][1][0]
    return lax.dot_general(
        jnp.concatenate([lh, lh, ll], la),
        jnp.concatenate([rh, rl, rh], ra),
        dims,
        preferred_element_type=F32,
    )


def two(value):
    return split(value, 2)


def spread(pieces, heads):
    return [jnp.where(heads, jnp.concatenate([p, p], 0), jnp.zeros((), p.dtype)) for p in pieces]


def exponents(sums_ref, ld, lo, hi):
    parts = jnp.concatenate(split(ld, 3), 0)
    c = sums_ref[lo:hi, :]
    return lax.dot_general(
        jnp.concatenate([c, c, c], 1), parts, NN, preferred_element_type=F32
    )


def head_mask(rows):
    r = lax.broadcasted_iota(jnp.int32, (2 * rows, LANES), 0) >= rows
    c = lax.broadcasted_iota(jnp.int32, (2 * rows, LANES), 1) >= HEAD
    return r == c


def head_sum(value, ones_ref):
    a, b = two(value)
    return lax.dot_general(
        jnp.concatenate([a, b], 1),
        jnp.concatenate([ones_ref[...], ones_ref[...]], 0),
        NN,
        preferred_element_type=F32,
    )


def silu(x):
    return x / (1.0 + jnp.exp(-x))


def close_kernel(keep_ref, k_ref, v_ref, ld_ref, sums_ref, state_ref, carry_ref):
    tokens = k_ref.shape[0]
    heads = head_mask(HEAD)
    state = jnp.zeros((LANES, LANES), F32)
    carry = jnp.ones((1, LANES), F32)
    n = sums_ref.shape[0] // CHUNK
    for c in range(tokens // CHUNK):
        rows = pl.ds(c * CHUNK, CHUNK)
        keep = keep_ref[c]
        ld = ld_ref[rows, :]
        e = exponents(sums_ref, ld, (n - 1) * CHUNK, n * CHUNK)
        last = jnp.exp(e[0:1] + ld[0:1]) * keep
        carry = carry * last
        fresh = dot3(two(v_ref[rows, :]), two(k_ref[rows, :] * jnp.exp(e)), TN)
        state = state * last + jnp.where(heads, fresh, 0.0)
    state_ref[...] = state[:HEAD] + state[HEAD:]
    carry_ref[...] = carry


def level_part(index, m, q, k, x):
    right = (lax.broadcasted_iota(jnp.int32, (CHUNK, LANES), 0) & m) > 0
    z = jnp.where(right, q, k)
    if m > 1:
        z = z * x[index * CHUNK : (index + 1) * CHUNK]
    return right, z


def forward_kernel(
    keep_ref, q_ref, k_ref, v_ref, ld_ref, gate_ref, vec_ref, start_ref, sums_ref, level_ref, ones_ref,
    raw_ref, gated_ref, score_ref, state_ref,
):
    tokens = q_ref.shape[0]
    levels = levels_of(CHUNK)
    n = sums_ref.shape[0] // CHUNK
    heads = head_mask(HEAD)
    wide = head_mask(CHUNK)
    level = level_ref[...]
    t = lax.broadcasted_iota(jnp.int32, (CHUNK, 2 * CHUNK), 0)
    s = lax.broadcasted_iota(jnp.int32, (CHUNK, 2 * CHUNK), 1) & (CHUNK - 1)
    bonus = vec_ref[0:1]
    state = jnp.where(heads, jnp.concatenate([start_ref[...], start_ref[...]], 0), 0.0)
    for c in range(tokens // CHUNK):
        rows = pl.ds(c * CHUNK, CHUNK)
        state = state * keep_ref[c]
        state_ref[pl.ds(c * HEAD, HEAD), :] = state[:HEAD] + state[HEAD:]
        q, k, v, ld = q_ref[rows, :], k_ref[rows, :], v_ref[rows, :], ld_ref[rows, :]
        e = exponents(sums_ref, ld, 0, n * CHUNK)
        x = jnp.exp(e)
        score = jnp.zeros((CHUNK, 2 * CHUNK), F32)
        for index, m in enumerate(levels):
            right, z = level_part(index, m, q, k, x)
            z = two(z)
            score = jnp.where(level == index, dot3(z, spread(z, wide), NT), score)
        score = jnp.where(t > s, score, 0.0)
        score = jnp.where(t == s, head_sum(q * bonus * k, ones_ref), score)
        score_ref[rows, :] = score
        xq, xk = x[(n - 2) * CHUNK : (n - 1) * CHUNK], x[(n - 1) * CHUNK :]
        v2 = two(v)
        raw = dot3(two(score), spread(v2, wide), NN) + dot3(two(q * xq), two(state), NT)
        last = jnp.exp(e[(n - 1) * CHUNK : (n - 1) * CHUNK + 1] + ld[0:1])
        state = state * last + jnp.where(heads, dot3(v2, two(k * xk), TN), 0.0)
        raw_ref[rows, :] = raw
        center = raw - head_sum(raw, ones_ref) * (1.0 / HEAD)
        spread_of = head_sum(center * center, ones_ref) * (1.0 / HEAD)
        normal = center * lax.rsqrt(spread_of + 0.00064)
        gated_ref[rows, :] = ((normal * vec_ref[1:2] + vec_ref[2:3]) * silu(gate_ref[rows, :])).astype(BF)


def head_back_kernel(
    keep_ref, q_ref, ld_ref, raw_ref, gate_ref, grad_ref, vec_ref, sums_ref, ones_ref,
    draw_ref, dgate_ref, direct_ref, dvec_ref,
):
    tokens = q_ref.shape[0]
    n = sums_ref.shape[0] // CHUNK
    heads = head_mask(HEAD)
    direct = jnp.zeros((LANES, LANES), F32)
    gain, bias = vec_ref[1:2], vec_ref[2:3]
    dgain = jnp.zeros((1, LANES), F32)
    dbias = jnp.zeros((1, LANES), F32)
    for c in reversed(range(tokens // CHUNK)):
        rows = pl.ds(c * CHUNK, CHUNK)
        raw, gate, grad = raw_ref[rows, :], gate_ref[rows, :], grad_ref[rows, :]
        center = raw - head_sum(raw, ones_ref) * (1.0 / HEAD)
        inv = lax.rsqrt(head_sum(center * center, ones_ref) * (1.0 / HEAD) + 0.00064)
        normal = center * inv
        sig = 1.0 / (1.0 + jnp.exp(-gate))
        act = gate * sig
        affine = normal * gain + bias
        dgate_ref[rows, :] = (grad * affine * (sig + act * (1.0 - sig))).astype(BF)
        daff = grad * act
        dgain = dgain + jnp.sum(daff * normal, 0, keepdims=True)
        dbias = dbias + jnp.sum(daff, 0, keepdims=True)
        dnorm = daff * gain
        draw = inv * (
            dnorm
            - head_sum(dnorm, ones_ref) * (1.0 / HEAD)
            - normal * (head_sum(dnorm * normal, ones_ref) * (1.0 / HEAD))
        )
        draw_ref[rows, :] = draw
        ld = ld_ref[rows, :]
        e = exponents(sums_ref, ld, (n - 2) * CHUNK, (n - 1) * CHUNK)
        last = jnp.exp(e[CHUNK - 1 :] + ld[CHUNK - 1 :])
        fresh = dot3(two(draw), two(q_ref[rows, :] * jnp.exp(e)), TN)
        direct = (direct * last + jnp.where(heads, fresh, 0.0)) * keep_ref[c]
    direct_ref[...] = direct[:HEAD] + direct[HEAD:]
    dvec_ref[0:1] = dgain
    dvec_ref[1:2] = dbias


def backward_kernel(
    keep_ref, q_ref, k_ref, v_ref, ld_ref, draw_ref, score_ref, state_ref, later_ref, vec_ref,
    sums_ref, sums_t_ref, level_ref, ones_ref,
    dq_ref, dk_ref, dv_ref, dld_ref, du_ref,
):
    tokens = q_ref.shape[0]
    levels = levels_of(CHUNK)
    n = sums_ref.shape[0] // CHUNK
    heads = head_mask(HEAD)
    wide = head_mask(CHUNK)
    level = level_ref[...]
    t = lax.broadcasted_iota(jnp.int32, (CHUNK, 2 * CHUNK), 0)
    s = lax.broadcasted_iota(jnp.int32, (CHUNK, 2 * CHUNK), 1) & (CHUNK - 1)
    lower = t > s
    bonus = vec_ref[0:1]
    dstate = jnp.where(heads, jnp.concatenate([later_ref[...], later_ref[...]], 0), 0.0)
    du = jnp.zeros((1, LANES), F32)
    for c in reversed(range(tokens // CHUNK)):
        rows = pl.ds(c * CHUNK, CHUNK)
        small = state_ref[pl.ds(c * HEAD, HEAD), :]
        state = jnp.where(heads, jnp.concatenate([small, small], 0), 0.0)
        q, k, v, ld = q_ref[rows, :], k_ref[rows, :], v_ref[rows, :], ld_ref[rows, :]
        draw = draw_ref[rows, :]
        e = exponents(sums_ref, ld, 0, n * CHUNK)
        x = jnp.exp(e)
        v2, draw2 = two(v), two(draw)
        dscore = jnp.where(
            lower, dot3(draw2, spread(v2, wide), NT), dot3(v2, spread(draw2, wide), NT)
        )
        dbon = head_sum(draw * v, ones_ref) * bonus
        dq = dbon * k
        dk = dbon * q
        du = du + jnp.sum(head_sum(draw * v, ones_ref) * q * k, 0, keepdims=True)
        grads = []
        for index, m in enumerate(levels):
            right, z = level_part(index, m, q, k, x)
            dz = dot3(
                two(jnp.where(level == index, dscore, 0.0)), spread(two(z), wide), NN
            )
            if m > 1:
                grads.append(z * dz)
                dz = dz * x[index * CHUNK : (index + 1) * CHUNK]
            dq = dq + jnp.where(right, dz, 0.0)
            dk = dk + jnp.where(right, 0.0, dz)
        xq, xk = x[(n - 2) * CHUNK : (n - 1) * CHUNK], x[(n - 1) * CHUNK :]
        qx, kx = q * xq, k * xk
        dstate2 = two(dstate)
        dqx = dot3(draw2, two(state), NN)
        dkx = dot3(v2, dstate2, NN)
        grads.append(dqx * qx)
        grads.append(dkx * kx)
        dq_ref[rows, :] = (dq + dqx * xq).astype(dq_ref.dtype)
        dk_ref[rows, :] = (dk + dkx * xk).astype(dk_ref.dtype)
        back = dot3(two(score_ref[rows, :]), draw2, TN)
        back = jnp.where(wide, back, 0.0)
        dv_ref[rows, :] = (back[:CHUNK] + back[CHUNK:] + dot3(two(kx), dstate2, NT)).astype(dv_ref.dtype)
        last = jnp.exp(e[(n - 1) * CHUNK : (n - 1) * CHUNK + 1] + ld[0:1])
        through = jnp.sum(state * dstate, 0, keepdims=True) * last
        gh, gl = two(jnp.concatenate(grads, 0))
        ct = sums_t_ref[...]
        dld_ref[rows, :] = through + lax.dot_general(
            jnp.concatenate([ct, ct], 1), jnp.concatenate([gh, gl], 0), NN, preferred_element_type=F32
        )
        dstate = dstate * last + jnp.where(heads, dot3(draw2, two(qx), TN), 0.0)
        dstate = dstate * keep_ref[c]
    du_ref[...] = du


def _call(kernel, outs, ins, tokens, width, flops):
    def spec(kind):
        kind, rows = kind
        if kind == "s":
            return pl.BlockSpec(memory_space=pltpu.SMEM)
        if kind == "c":
            return pl.BlockSpec(rows, lambda i: (0, 0))
        return pl.BlockSpec((rows, LANES), lambda i: (0, i))

    return pl.pallas_call(
        kernel,
        grid=(width // LANES,),
        in_specs=[spec(kind) for kind, _ in ins],
        out_specs=[spec(("r", rows)) for rows, _ in outs],
        out_shape=[jax.ShapeDtypeStruct((rows, width), dt) for rows, dt in outs],
        compiler_params=pltpu.CompilerParams(vmem_limit_bytes=48 * 2**20),
        cost_estimate=pl.CostEstimate(flops=flops, bytes_accessed=10 * tokens * width * 4, transcendentals=8 * tokens * width),
    )(*[value for _, value in ins])


def rows_of(value):
    return (("r", value.shape[0]), value)


def const_of(value):
    return (("c", value.shape), value)


def close(keep, k, v, ld):
    tokens, width = k.shape
    sums, _, _ = tables(CHUNK)
    return _call(
        close_kernel, [(HEAD, F32), (1, F32)],
        [(("s", 0), keep), rows_of(k), rows_of(v), rows_of(ld), const_of(jnp.asarray(sums, BF))],
        tokens, width, tokens * width * 2000,
    )


def forward(keep, q, k, v, ld, gate, vec3, start):
    tokens, width = k.shape
    sums, level, ones = tables(CHUNK)
    return _call(
        forward_kernel,
        [(tokens, F32), (tokens, BF), (tokens, F32), (tokens // CHUNK * HEAD, F32)],
        [(("s", 0), keep), rows_of(q), rows_of(k), rows_of(v), rows_of(ld), rows_of(gate), rows_of(vec3), rows_of(start),
         const_of(jnp.asarray(sums, BF)), const_of(jnp.asarray(level)), const_of(jnp.asarray(ones, BF))],
        tokens, width, tokens * width * 20000,
    )


def head_back(keep, q, ld, raw, gate, grad, vec3):
    tokens, width = q.shape
    sums, level, ones = tables(CHUNK)
    return _call(
        head_back_kernel,
        [(tokens, F32), (tokens, BF), (HEAD, F32), (2, F32)],
        [(("s", 0), keep), rows_of(q), rows_of(ld), rows_of(raw), rows_of(gate), rows_of(grad), rows_of(vec3),
         const_of(jnp.asarray(sums, BF)), const_of(jnp.asarray(ones, BF))],
        tokens, width, tokens * width * 4000,
    )


def backward(keep, q, k, v, ld, draw, score, state, later, vec3):
    tokens, width = q.shape
    sums, level, ones = tables(CHUNK)
    return _call(
        backward_kernel,
        [(tokens, BF), (tokens, BF), (tokens, BF), (tokens, F32), (1, F32)],
        [(("s", 0), keep), rows_of(q), rows_of(k), rows_of(v), rows_of(ld), rows_of(draw), rows_of(score), rows_of(state),
         rows_of(later), rows_of(vec3), const_of(jnp.asarray(sums, BF)), const_of(jnp.asarray(sums.T.copy(), BF)),
         const_of(jnp.asarray(level)), const_of(jnp.asarray(ones, BF))],
        tokens, width, tokens * width * 30000,
    )


HIGHEST = lax.Precision.HIGHEST
FACTORS = (0.2, 0.03, 0.03, 0.03, 0.03, 0.03, 0.03, 0.03, 0.03)
BOTH = ("seq", "dp")


def layer_norm(field, gain, bias):
    center = field - jnp.mean(field, axis=-1, keepdims=True)
    spread_of = jnp.mean(center * center, axis=-1, keepdims=True)
    return center * lax.rsqrt(spread_of + 1e-05) * gain + bias


def norm_first(field, vecs):
    return layer_norm(field, vecs[0], vecs[1])


def norm_second(field, vecs):
    return layer_norm(field, vecs[12], vecs[13])


def shifted(field, incoming, follows):
    return jnp.concatenate([incoming, field[:-1]], axis=0) * follows


def mix_inputs(normed, incoming, vecs, down, up, ddown, dup, follows):
    delta = shifted(normed, incoming, follows) - normed
    lora = jnp.tanh(jnp.dot(normed + delta * vecs[2], down, precision=HIGHEST))
    rank = lora.shape[1] // 5
    inputs = [
        normed
        + delta
        * (
            vecs[3 + c]
            + jnp.dot(
                lora[:, c * rank : (c + 1) * rank], up[c * rank : (c + 1) * rank], precision=HIGHEST
            )
        )
        for c in range(5)
    ]
    decay = vecs[8] + jnp.dot(
        jnp.tanh(jnp.dot(inputs[0], ddown, precision=HIGHEST)), dup, precision=HIGHEST
    )
    return (inputs[1], inputs[2], inputs[3], inputs[4], -jnp.exp(decay))


def channel_inputs(second, incoming, vecs, follows):
    delta = shifted(second, incoming, follows) - second
    return (second + delta * vecs[14], second + delta * vecs[15])


def send_rows(field):
    n = lax.axis_size("seq")
    return lax.ppermute(field[-1:], "seq", [(i, i + 1) for i in range(n - 1)])


def back_rows(grad_first, field):
    n = lax.axis_size("seq")
    arrived = lax.ppermute(grad_first, "seq", [(i + 1, i) for i in range(n - 1)])
    last = lax.broadcasted_iota(jnp.int32, field.shape, 0) == field.shape[0] - 1
    return field + jnp.where(last, arrived, 0.0)


def prefix(carry, state, reverse):
    n, here = lax.axis_size("seq"), lax.axis_index("seq")
    every = lax.all_gather(jnp.concatenate([state, carry], 0), "seq")
    total = jnp.zeros_like(state)
    for k in range(n):
        at = n - 1 - k if reverse else k
        reached = at > here if reverse else at < here
        total = jnp.where(reached, every[at, -1:] * total + every[at, :-1], total)
    return total


def product(left, right):
    return jnp.dot(left, right, preferred_element_type=F32)


def product_t(left, right):
    return lax.dot_general(left, right, TN, preferred_element_type=F32)


def back_product(grad, weight):
    return lax.dot_general(grad, weight, NT, preferred_element_type=F32)


def swap(value, axis, bit):
    return lax.ppermute(value, axis, [(i, i ^ bit) for i in range(lax.axis_size(axis))])


def climb(value, step, count):
    planes = lax.axis_size("dp") // 2
    pairs = []
    for z in range(planes):
        if (step > 0 and z < count and z + 1 < planes) or (step < 0 and z >= planes - count and z > 0):
            pairs += [(2 * z + y, 2 * (z + step) + y) for y in (0, 1)]
    return lax.ppermute(value, "dp", pairs)


def pick(value, index, axis=0):
    return lax.dynamic_index_in_dim(value, index, axis, keepdims=False)


def down_z(whole, kind):
    z = lax.axis_index("dp") // 2
    planes = whole.shape[0]
    ends = []
    for step in (1, -1):
        carried = None
        for t in range(1, planes):
            part = pick(whole, (z + step * (planes - t)) % planes)
            carried = part if carried is None else part + carried
            carried = climb(carried.astype(kind), step, t).astype(F32)
        ends.append(carried)
    return pick(whole, z) + ends[0] + ends[1]


def scatter_sum(block, rows, kind, x_first):
    s, d = lax.axis_index("seq"), lax.axis_index("dp")
    y = d % 2

    def parts(value):
        return value.reshape(4, 2, rows, value.shape[-1])

    far = swap(block(s ^ 3).astype(kind), "seq", 1)
    near = swap(block(s ^ 1).astype(kind), "seq", 1)
    if x_first:
        across = swap((block(s ^ 2) + far.astype(F32)).astype(kind), "seq", 2)
        own = parts(block(s) + near.astype(F32) + across.astype(F32))
        other = swap(pick(own, 1 - y, 1).astype(kind), "dp", 1)
        own = pick(own, y, 1) + other.astype(F32)
    else:
        across = parts(block(s ^ 2) + far.astype(F32))
        own = parts(block(s) + near.astype(F32))
        a = swap(pick(across, 1 - y, 1).astype(kind), "dp", 1)
        b = swap(pick(own, 1 - y, 1).astype(kind), "dp", 1)
        a = swap((pick(across, y, 1) + a.astype(F32)).astype(kind), "seq", 2)
        own = pick(own, y, 1) + b.astype(F32) + a.astype(F32)
    return down_z(own, kind)


def weight_grad(left, grad, x_first):
    n, m = lax.axis_size("seq"), lax.axis_size("dp")
    wide = left.shape[1] // n
    if (n, m) != (4, 8):
        part = lax.psum_scatter(product_t(left, grad), "seq", scatter_dimension=0, tiled=True)
        return lax.psum_scatter(part, "dp", scatter_dimension=0, tiled=True)

    def block(i):
        return product_t(lax.dynamic_slice_in_dim(left, i * wide, wide, 1), grad)

    return scatter_sum(block, wide // m, BF, x_first)


def small_grad(whole):
    n, m = lax.axis_size("seq"), lax.axis_size("dp")
    if (n, m) != (4, 8):
        part = lax.psum_scatter(whole, "seq", scatter_dimension=0, tiled=True)
        return lax.psum_scatter(part, "dp", scatter_dimension=0, tiled=True)
    wide = whole.shape[0] // n

    def block(i):
        return lax.dynamic_slice_in_dim(whole, i * wide, wide, 0)

    return scatter_sum(block, wide // m, F32, True)


def renew(weight, moment, average, grad, factor, tokens):
    rate = factor / math.sqrt(tokens)
    moment = 0.9 * moment + grad
    weight = weight - rate * (grad + 0.9 * moment)
    average = 0.8 * average + 0.2 * weight
    return (weight, moment, average)


def local(block_input, out_grad, lengths, *state):
    params, moments, averages = state[0::3], state[1::3], state[2::3]
    vectors, mix_weights, ffn_key, ffn_recept, ffn_value, maa_down, maa_up, decay_down, decay_up = params
    length, width = block_input.shape[1:]
    tokens = length * lax.axis_size("seq") * lax.axis_size("dp")
    rank = maa_up.shape[1]
    n_vec, n_down, n_decay = vectors.shape[0], maa_down.shape[1], decay_down.shape[1]
    start = lengths[0, 0] - lax.axis_index("seq") * length
    follows = (jnp.arange(length) != start) & (
        (jnp.arange(length) > 0) | (lax.axis_index("seq") > 0)
    )
    follows = follows.astype(F32)[:, None]
    keep = (jnp.arange(length // CHUNK) * CHUNK != start).astype(F32)

    small = jnp.concatenate(
        [vectors.T, maa_down, maa_up.reshape(5 * rank, -1).T, decay_down, decay_up.T], axis=1
    )
    small = lax.all_gather(small, BOTH, axis=0, tiled=True)
    cuts = np.cumsum([n_vec, n_down, 5 * rank, n_decay, n_decay])
    vecs, down, up, ddown, dup = jnp.split(small, cuts[:-1], axis=1)
    vecs, up, dup = vecs.T, up.T, dup.T

    mix = lax.all_gather(mix_weights.astype(BF), BOTH, axis=1, tiled=True)
    fkey = lax.all_gather(ffn_key.astype(BF), BOTH, axis=0, tiled=True)
    fval = lax.all_gather(ffn_value.astype(BF), BOTH, axis=0, tiled=True)
    frec = lax.all_gather(ffn_recept.astype(BF), BOTH, axis=0, tiled=True)

    hidden = block_input[0].astype(F32)
    normed, pull_norm_one = jax.vjp(norm_first, hidden, vecs)
    incoming = send_rows(normed)
    (xkey, xval, xrec, xgate, logdec), pull_mix = jax.vjp(
        functools.partial(mix_inputs, follows=follows), normed, incoming, vecs, down, up, ddown, dup
    )
    xkey, xval, xrec, xgate = (v.astype(BF) for v in (xkey, xval, xrec, xgate))
    keys = product(xkey, mix[0])
    values = product(xval, mix[1])
    closing, carry = close(keep, keys, values, logdec)
    before = prefix(carry, closing, False)
    recept = product(xrec, mix[2])
    gate = product(xgate, mix[3])
    vec3 = vecs[9:12]
    raw, gated, score, states = forward(keep, recept, keys, values, logdec, gate, vec3, before)
    middle = hidden + product(gated, mix[4])

    second, pull_norm_two = jax.vjp(norm_second, middle, vecs)
    incoming_two = send_rows(second)
    (key_in, rec_in), pull_channel = jax.vjp(
        functools.partial(channel_inputs, follows=follows), second, incoming_two, vecs
    )
    key_in, rec_in = key_in.astype(BF), rec_in.astype(BF)
    positive = jnp.maximum(product(key_in, fkey), 0.0)
    squared = (positive * positive).astype(BF)
    kvals = product(squared, fval)
    sigma = jax.nn.sigmoid(product(rec_in, frec))
    block_output = middle + sigma * kvals

    upstream = out_grad[0].astype(F32)
    grad_kvals = (upstream * sigma).astype(BF)
    grad_rpre = (upstream * kvals * sigma * (1.0 - sigma)).astype(BF)
    sum_fval = weight_grad(squared, grad_kvals, True)
    grad_kpre = (back_product(grad_kvals, fval) * (2.0 * positive)).astype(BF)
    sum_fkey = weight_grad(key_in, grad_kpre, False)
    sum_frec = weight_grad(rec_in, grad_rpre, False)
    grad_second, grad_inc_two, vec_one = pull_channel(
        (back_product(grad_kpre, fkey), back_product(grad_rpre, frec))
    )
    grad_second = back_rows(grad_inc_two, grad_second)
    grad_mid, vec_two = pull_norm_two(grad_second)
    grad_middle = upstream + grad_mid
    grad_attn = grad_middle.astype(BF)
    sum_out = weight_grad(gated, grad_attn, True)
    grad_gated = back_product(grad_attn, mix[4])
    grad_raw, grad_gate, direct, vec_head = head_back(
        keep, recept, logdec, raw, gate, grad_gated, vec3
    )
    later = prefix(carry, direct, True)
    sum_gate = weight_grad(xgate, grad_gate, False)
    grad_xgate = back_product(grad_gate, mix[3])
    grad_rec, grad_key, grad_val, grad_dec, vec_bonus = backward(
        keep, recept, keys, values, logdec, grad_raw, score, states, later, vec3
    )
    sum_rec = weight_grad(xrec, grad_rec, True)
    sum_key = weight_grad(xkey, grad_key, False)
    sum_val = weight_grad(xval, grad_val, True)
    grad_normed, grad_inc, vec_mix, gdown, gup, gddown, gdup = pull_mix(
        (
            back_product(grad_key, mix[0]),
            back_product(grad_val, mix[1]),
            back_product(grad_rec, mix[2]),
            grad_xgate,
            grad_dec,
        )
    )
    grad_normed = back_rows(grad_inc, grad_normed)
    grad_hidden, vec_three = pull_norm_one(grad_normed)
    input_grad = grad_middle + grad_hidden

    vec_all = vec_one + vec_two + vec_mix + vec_three
    vec_all = jnp.concatenate(
        [vec_all[:9], vec_all[9:10] + vec_bonus, vec_all[10:12] + vec_head, vec_all[12:]], axis=0
    )
    total = small_grad(jnp.concatenate([vec_all.T, gdown, gup.T, gddown, gdup.T], axis=1))
    gvec, gdown, gup, gddown, gdup = jnp.split(total, cuts[:-1], axis=1)
    grads = (
        gvec.T,
        jnp.stack([sum_key, sum_val, sum_rec, sum_gate, sum_out]),
        sum_fkey,
        sum_frec,
        sum_fval,
        gdown,
        gup.T.reshape(maa_up.shape),
        gddown,
        gdup.T,
    )
    results = [block_output[None], input_grad[None]]
    for param, moment, average, grad, factor in zip(params, moments, averages, grads, FACTORS):
        results.extend(renew(param, moment, average, grad, factor, tokens))
    return tuple(results)


def solution(mesh):
    vec, mix = P(None, BOTH), P(None, BOTH, None)
    rows, up = P(BOTH, None), P(None, None, BOTH)
    specs = [vec, mix, rows, rows, rows, rows, up, rows, vec]
    state = tuple(spec for spec in specs for _ in range(3))
    tokens = P("dp", "seq", None)
    return jax.shard_map(
        local,
        mesh=mesh,
        in_specs=(tokens, tokens, P("dp", None)) + state,
        out_specs=(tokens, tokens) + state,
        check_vma=False,
    )
```

time: 5350 us -> 1930 us (0.36)
  waiting for transfers between devices: 3100 us -> 1010 us
  other arithmetic: 948 us -> 154 us
  local copies, waits for them, and re-layouts: 425 us -> 70.8 us
  blocking collectives: 242 us -> 0 us
  matrix products: 549 us -> 335 us
  starting transfers between devices: 8.44 us -> 189 us
  Pallas kernels: 0 us -> 132 us
    reduce_scatter x13 -> x0, waiting for transfers between devices: 2410 us -> none  [the longest x1 562 us: local(): lax.psum_scatter(grad_mix, 'seq', scatter_dimension=1, tiled=True)]
    ppermute x4 -> x98, waiting for transfers between devices: 0.82 us -> 418 us  [the longest x40 310 us: swap(): lax.ppermute(value, axis, [(i, i ^ bit) for i in range(lax.axis_size(axis...]
    unnamed x31 -> x7, waiting for transfers between devices: 308 us -> 0.11 us
    another operation x38 -> x1, other arithmetic: 261 us -> 1.9 us  [local(): jnp.stack([sum_key, sum_val, sum_rec, sum_gate, sum_out])]
    all_gather x4 -> x0, blocking collectives: 242 us -> none  [the longest x1 87.2 us: local(): lax.all_gather(decay_up, ('seq', 'dp'), axis=1, tiled=True)]
    dot_general x119 -> x72, matrix products: 549 us -> 335 us  [the longest x32 117 us: product_t(): return lax.dot_general(left, right, TN, preferred_element_type=F32)]
    all_gather x8 -> x7, waiting for transfers between devices: 385 us -> 594 us  [the longest x1 201 us: local(): mix = lax.all_gather(mix_weights.astype(BF), BOTH, axis=1, tiled=True)]
    ppermute x4 -> x98, starting transfers between devices: 6.41 us -> 189 us  [the longest x54 148 us: climb(): return lax.ppermute(value, 'dp', pairs)]
  transfers between devices with their start and end apart: 30 -> 105, of which waited for: 19 -> 38; matrix products, arithmetic and copies ran while one was open for 9% -> 24% of each run, Pallas kernels for 0% -> 6%
where the time goes in v1:
time: 1930 us; the launch traced here: 1910 us
  waiting for transfers between devices  1010 us (52%)
  matrix products  335 us (17%)
  starting transfers between devices  189 us (10%)
  other arithmetic  154 us (8%)
  Pallas kernels  132 us (7%)
  local copies, waits for them, and re-layouts  70.8 us (4%)
    ppermute x40, waiting for transfers between devices, swap(): lax.ppermute(value, axis, [(i, i ^ bit) for i in range(lax.axis_size(axis...  310 us
    all_gather x1, waiting for transfers between devices, local(): mix = lax.all_gather(mix_weights.astype(BF), BOTH, axis=1, tiled=True)  201 us
    all_gather x1, waiting for transfers between devices, local(): fval = lax.all_gather(ffn_value.astype(BF), BOTH, axis=0, tiled=True)  159 us
    ppermute x54, starting transfers between devices, climb(): return lax.ppermute(value, 'dp', pairs)  148 us
    pallas_call x4, Pallas kernels, _call(): pl.pallas_call(kernel, grid=(width // LANES,), in_specs=[spec(kind) for k...  132 us
    dot_general x32, matrix products, product_t(): return lax.dot_general(left, right, TN, preferred_element_type=F32)  117 us
    ppermute x54, waiting for transfers between devices, climb(): return lax.ppermute(value, 'dp', pairs)  108 us
    all_gather x1, waiting for transfers between devices, local(): fkey = lax.all_gather(ffn_key.astype(BF), BOTH, axis=0, tiled=True)  108 us
  transfers between devices with their start and end apart: 105, of which 38 were waited for; matrix products, arithmetic and copies ran while one was open for 24% of the time, Pallas kernels for 6%

profile of v1, /device:TPU:0, one launch (start us, length us, event | category | flops | bytes accessed | tf_op | source)
XLA Modules:
  0.0 1911.7 jit_solution(17068609098803616081)
XLA Ops:
  16.2 60.9 %all-gather.12.cloned.1.call-done = f32[2048,464]{1,0:T(8,128)} async-done(((f32[64,464]{1,0:T(8,128)}), f32[2048,464]{1,0:T(8,128)}) %all-gather.12.cloned.1.call-update) | async-done | bytes 3801104 | tf_op jit(solution)/shard_map/all_gather | solution.py:548
  113.2 201.1 %all-gather.14.cloned.1.call-done = bf16[5,2048,2048]{2,1,0:T(8,128)(2,1)} async-done(((bf16[5,64,2048]{2,1,0:T(8,128)(2,1)}), bf16[5,2048,2048]{2,1,0:T(8,128)(2,1)}) %all-gather.14.cloned.1.call-update) | async-done | bytes 41943056 | tf_op jit(solution)/shard_map/all_gather | solution.py:553
  314.3 5.8 fusion.4.k_ref
  320.1 6.5 fusion.6.v_ref
  326.7 13.7 shard_map.599
  348.1 7.2 fusion.2.q_ref
  355.3 7.1 fusion.8.gate_ref
  367.0 51.0 %shard_map.600 = (f32[256,2048]{1,0:T(8,128)S(1)}, bf16[256,2048]{1,0:T(8,128)(2,1)S(1)}, f32[256,2048]{1,0:T(8,128)S(1)}, f32[256,2048]{1,0:T(8,128)}) custom-call(f32[4]{0:T(128)S(1)} %compare_convert_fusion.keep_ref, f32[256,2048]{1,0:T(8,128)} %fusion.2.q_ref, f32[256,2048]{1,0:T(8,128)} %copy-done.10, f32[256,2048]{1,0:T(8,128)} %copy-done.11, ...), custom_call_target="tpu_custom_call" | custom-call | flops 10485760000 | bytes 20971520 | tf_op jit(solution)/shard_map/pallas_call | solution.py:292
  418.1 7.4 fusion.303
  434.8 107.8 %all-gather.18.cloned.1.call-done = bf16[2048,7168]{1,0:T(8,128)(2,1)} async-done(((bf16[64,7168]{1,0:T(8,128)(2,1)}), bf16[2048,7168]{1,0:T(8,128)(2,1)}) %all-gather.18.cloned.1.call-update) | async-done | bytes 29360144 | tf_op jit(solution)/shard_map/all_gather | solution.py:554
  542.6 16.7 multiply_convert_fusion
  559.3 159.1 %all-gather.20.cloned.1.call-done = bf16[7168,2048]{1,0:T(8,128)(2,1)} async-done(((bf16[224,2048]{1,0:T(8,128)(2,1)}), bf16[7168,2048]{1,0:T(8,128)(2,1)}) %all-gather.20.cloned.1.call-update) | async-done | bytes 29360144 | tf_op jit(solution)/shard_map/all_gather | solution.py:555
  718.4 15.7 fusion.304
  734.1 63.2 %all-gather.16.cloned.1.call-done = bf16[2048,2048]{1,0:T(8,128)(2,1)} async-done(((bf16[64,2048]{1,0:T(8,128)(2,1)}), bf16[2048,2048]{1,0:T(8,128)(2,1)}) %all-gather.16.cloned.1.call-update) | async-done | bytes 8388624 | tf_op jit(solution)/shard_map/all_gather | solution.py:556
  797.3 9.2 fusion.34
  806.5 17.9 fusion
  824.4 7.4 convolution_convert_fusion
  831.8 6.3 convolution_convert_fusion.1
  842.2 14.8 fusion.305
  857.0 7.9 multiply_reduce_fusion.3
  872.7 7.3 fusion.103
  880.0 5.1 convolution_convert_fusion.3
  893.5 7.2 fusion.9.grad_ref
  900.7 24.8 %shard_map.601 = (f32[256,2048]{1,0:T(8,128)S(1)}, bf16[256,2048]{1,0:T(8,128)(2,1)S(1)}, f32[64,2048]{1,0:T(8,128)S(1)}, f32[2,2048]{1,0:T(2,128)S(1)}) custom-call(f32[4]{0:T(128)S(1)} %compare_convert_fusion.keep_ref, f32[256,2048]{1,0:T(8,128)S(1)} %copy-done, f32[256,2048]{1,0:T(8,128)} %get-tuple-element.357.ld_ref, f32[256,2048]{1,0:T(8,128)} %copy-done.1, ...), custom_call_target="tpu_custom_call" | custom-call | flops 2097152000 | bytes 20971520 | tf_op jit(solution)/shard_map/pallas_call | solution.py:292
  928.2 6.0 fusion.7
  969.7 6.5 collective-permute-done.80
  979.5 41.2 %collective-permute-done.48 = bf16[4,64,2048]{2,1,0:T(8,128)(2,1)S(1)} collective-permute-done((bf16[4,64,2048]{2,1,0:T(8,128)(2,1)S(1)}, bf16[4,64,2048]{2,1,0:T(8,128)(2,1)S(1)}, u32[]{:S(2)}, u32[]{:S(2)}) %collective-permute-start.48) | collective-permute-done | bytes 1048608 | tf_op jit(solution)/shard_map/ppermute | solution.py:443
  1024.7 42.8 %shard_map.602 = (bf16[256,2048]{1,0:T(8,128)(2,1)S(1)}, bf16[256,2048]{1,0:T(8,128)(2,1)S(1)}, bf16[256,2048]{1,0:T(8,128)(2,1)S(1)}, f32[256,2048]{1,0:T(8,128)S(1)}, f32[1,2048]{1,0:T(1,128)S(1)}) custom-call(f32[4]{0:T(128)S(1)} %compare_convert_fusion.keep_ref, f32[256,2048]{1,0:T(8,128)} %fusion.2.q_ref, f32[256,2048]{1,0:T(8,128)} %copy-done.10, ...), custom_call_target="tpu_custom_call" | custom-call | flops 15728640000 | bytes 20971520 | tf_op jit(solution)/shard_map/pallas_call | solution.py:292
  1076.3 5.9 fusion.3
  1086.9 5.9 fusion.5
  1097.2 5.9 fusion.1
  1124.2 13.1 multiply_reduce_fusion.10
  1143.2 6.8 fusion.297
  1174.6 19.3 %collective-permute-done.46 = bf16[4,64,2048]{2,1,0:T(8,128)(2,1)S(1)} collective-permute-done((bf16[4,64,2048]{2,1,0:T(8,128)(2,1)S(1)}, bf16[4,64,2048]{2,1,0:T(8,128)(2,1)S(1)}, u32[]{:S(2)}, u32[]{:S(2)}) %collective-permute-start.46) | collective-permute-done | bytes 1048608 | tf_op jit(solution)/shard_map/ppermute | solution.py:443
  1248.3 12.3 collective-permute-done.87
  1306.5 7.7 collective-permute-start.9
  1347.4 7.9 collective-permute-done.17
  1358.4 10.3 convert_add_fusion.1
  1369.3 5.2 convert_add_fusion.2
  1374.5 10.7 fusion.14
  1386.8 8.0 collective-permute-done.18
  1409.8 8.6 add_convert_fusion
  1420.1 19.7 %collective-permute-done.27 = bf16[512,2048]{1,0:T(8,128)(2,1)} collective-permute-done((bf16[512,2048]{1,0:T(8,128)(2,1)}, bf16[512,2048]{1,0:T(8,128)(2,1)}, u32[]{:S(2)}, u32[]{:S(2)}) %collective-permute-start.27) | collective-permute-done | bytes 2097184 | tf_op jit(solution)/shard_map/ppermute | solution.py:443
  1445.2 7.2 collective-permute-start.21
  1452.4 32.2 %collective-permute-done.37 = bf16[512,2048]{1,0:T(8,128)(2,1)S(1)} collective-permute-done((bf16[512,2048]{1,0:T(8,128)(2,1)S(1)}, bf16[512,2048]{1,0:T(8,128)(2,1)S(1)}, u32[]{:S(2)}, u32[]{:S(2)}) %collective-permute-start.37) | collective-permute-done | bytes 2097184 | tf_op jit(solution)/shard_map/ppermute | solution.py:443
  1498.7 93.1 %collective-permute-done.38 = bf16[4,64,2048]{2,1,0:T(8,128)(2,1)S(1)} collective-permute-done((bf16[4,64,2048]{2,1,0:T(8,128)(2,1)S(1)}, bf16[4,64,2048]{2,1,0:T(8,128)(2,1)S(1)}, u32[]{:S(2)}, u32[]{:S(2)}) %collective-permute-start.38) | collective-permute-done | bytes 1048608 | tf_op jit(solution)/shard_map/ppermute | solution.py:443
  1619.4 11.3 collective-permute-start.31
  1631.6 7.1 fusion.11
  1644.2 11.6 convert_add_fusion
  1655.8 5.5 fusion.15
  1665.6 6.5 collective-permute-start.52
  1675.3 21.4 %collective-permute-done.67 = bf16[4,64,7168]{2,1,0:T(8,128)(2,1)} collective-permute-done((bf16[4,64,7168]{2,1,0:T(8,128)(2,1)}, bf16[4,64,7168]{2,1,0:T(8,128)(2,1)}, u32[]{:S(2)}, u32[]{:S(2)}) %collective-permute-start.67) | collective-permute-done | bytes 3670048 | tf_op jit(solution)/shard_map/ppermute | solution.py:443
  1699.3 20.6 %collective-permute-done.70 = bf16[4,64,7168]{2,1,0:T(8,128)(2,1)S(1)} collective-permute-done((bf16[4,64,7168]{2,1,0:T(8,128)(2,1)}, bf16[4,64,7168]{2,1,0:T(8,128)(2,1)S(1)}, u32[]{:S(2)}, u32[]{:S(2)}) %collective-permute-start.70) | collective-permute-done | bytes 3670048 | tf_op jit(solution)/shard_map/ppermute | solution.py:443
  1723.1 6.7 fusion.12
  1730.9 39.2 %collective-permute-done.91 = bf16[4,224,2048]{2,1,0:T(8,128)(2,1)} collective-permute-done((bf16[4,224,2048]{2,1,0:T(8,128)(2,1)}, bf16[4,224,2048]{2,1,0:T(8,128)(2,1)}, u32[]{:S(2)}, u32[]{:S(2)}) %collective-permute-start.91) | collective-permute-done | bytes 3670048 | tf_op jit(solution)/shard_map/ppermute | solution.py:443
  1773.3 5.4 bitcast_add_fusion
  1778.9 9.8 collective-permute-done.71
  1798.7 15.2 collective-permute-done.92
  1819.3 14.2 collective-permute-done.72
  1837.5 6.1 collective-permute-start.73
  1843.7 9.5 collective-permute-done.93
  1859.3 7.9 multiply_add_fusion
  1867.2 6.0 collective-permute-start.94
  1885.9 13.7 collective-permute-done.97
  (686 shorter events, 468.5 us)
Async XLA Ops:
  7.2 70.0 %all-gather.12.cloned.1.call-start = ((), (), s32[]{:S(2)}) async-start(), calls=%async_computation | async-start | bytes 4325376 | tf_op jit(solution)/shard_map/all_gather | solution.py:548
  12.3 302.0 %all-gather.14.cloned.1.call-start = ((), (), s32[]{:S(2)}) async-start(), calls=%async_computation.1 | async-start | bytes 43253760 | tf_op jit(solution)/shard_map/all_gather | solution.py:553
  15.4 348.9 %all-gather.22.cloned.1.call-start = ((), (), s32[]{:S(2)}) async-start(), calls=%async_computation.5 | async-start | bytes 2949120 | tf_op jit(solution)/shard_map/all_gather | solution.py:421
  341.9 200.7 %all-gather.18.cloned.1.call-start = ((), (), s32[]{:S(2)}) async-start(), calls=%async_computation.3 | async-start | bytes 30277632 | tf_op jit(solution)/shard_map/all_gather | solution.py:554
  344.5 373.9 %all-gather.20.cloned.1.call-start = ((), (), s32[]{:S(2)}) async-start(), calls=%async_computation.4 | async-start | bytes 30277632 | tf_op jit(solution)/shard_map/all_gather | solution.py:555
  347.2 450.1 %all-gather.16.cloned.1.call-start = ((), (), s32[]{:S(2)}) async-start(), calls=%async_computation.2 | async-start | bytes 8650752 | tf_op jit(solution)/shard_map/all_gather | solution.py:556
  348.0 673.9 %all-gather.24.cloned.1.call-start = ((), (), s32[]{:S(2)}) async-start(), calls=%async_computation.6 | async-start | bytes 2949120 | tf_op jit(solution)/shard_map/all_gather | solution.py:421
  865.0 20.4 %collective-permute-start.2 = (f32[1,2048]{1,0:T(1,128)S(1)}, f32[1,2048]{1,0:T(1,128)S(1)}, u32[]{:S(2)}, u32[]{:S(2)}) collective-permute-start(f32[1,2048]{1,0:T(1,128)S(1)} %split.62), channel_id=1, source_target_pairs={{8,0},{16,8},{24,16},{9,1},{17,9},{25,17},{10,2},{18,10},{26,18},{... | collective-permute-start | bytes 24584 | tf_op jit(solution)/shard_map/ppermute | solution.py:414
  866.4 80.7 %collective-permute-start.79 = (bf16[512,2048]{1,0:T(8,128)(2,1)}, bf16[512,2048]{1,0:T(8,128)(2,1)}, u32[]{:S(2)}, u32[]{:S(2)}) collective-permute-start(bf16[512,2048]{1,0:T(8,128)(2,1)} %convolution_convert_fusion.4), channel_id=1, source_target_pairs={{0,8},{8,0},{16,24},{24,16},{1,9},{9,1},{17,25},{25,17},{2,10},{10... | collective-permute-start | bytes 6291464 | tf_op jit(solution)/shard_map/ppermute | solution.py:443
  867.6 82.6 %collective-permute-start.77 = (bf16[512,2048]{1,0:T(8,128)(2,1)}, bf16[512,2048]{1,0:T(8,128)(2,1)}, u32[]{:S(2)}, u32[]{:S(2)}) collective-permute-start(bf16[512,2048]{1,0:T(8,128)(2,1)} %convolution_convert_fusion.5), channel_id=1, source_target_pairs={{0,8},{8,0},{16,24},{24,16},{1,9},{9,1},{17,25},{25,17},{2,10},{10... | collective-permute-start | bytes 6291464 | tf_op jit(solution)/shard_map/ppermute | solution.py:443
  927.6 27.9 %collective-permute-start.47 = (bf16[512,2048]{1,0:T(8,128)(2,1)}, bf16[512,2048]{1,0:T(8,128)(2,1)}, u32[]{:S(2)}, u32[]{:S(2)}) collective-permute-start(bf16[512,2048]{1,0:T(8,128)(2,1)} %convolution_convert_fusion.8), channel_id=1, source_target_pairs={{0,8},{8,0},{16,24},{24,16},{1,9},{9,1},{17,25},{25,17},{2,10},{10... | collective-permute-start | bytes 6291464 | tf_op jit(solution)/shard_map/ppermute | solution.py:443
  928.1 31.0 %collective-permute-start.57 = (bf16[512,2048]{1,0:T(8,128)(2,1)}, bf16[512,2048]{1,0:T(8,128)(2,1)}, u32[]{:S(2)}, u32[]{:S(2)}) collective-permute-start(bf16[512,2048]{1,0:T(8,128)(2,1)} %convolution_convert_fusion.6), channel_id=1, source_target_pairs={{0,8},{8,0},{16,24},{24,16},{1,9},{9,1},{17,25},{25,17},{2,10},{10... | collective-permute-start | bytes 6291464 | tf_op jit(solution)/shard_map/ppermute | solution.py:443
  947.1 249.9 %collective-permute-start.56 = (bf16[512,2048]{1,0:T(8,128)(2,1)}, bf16[512,2048]{1,0:T(8,128)(2,1)}, u32[]{:S(2)}, u32[]{:S(2)}) collective-permute-start(bf16[512,2048]{1,0:T(8,128)(2,1)} %convolution_convert_fusion.7), channel_id=1, source_target_pairs={{0,8},{8,0},{16,24},{24,16},{1,9},{9,1},{17,25},{25,17},{2,10},{10... | collective-permute-start | bytes 6291464 | tf_op jit(solution)/shard_map/ppermute | solution.py:443
  950.2 26.1 %collective-permute-start.80 = (bf16[4,64,2048]{2,1,0:T(8,128)(2,1)S(1)}, bf16[4,64,2048]{2,1,0:T(8,128)(2,1)S(1)}, u32[]{:S(2)}, u32[]{:S(2)}) collective-permute-start(bf16[4,64,2048]{2,1,0:T(8,128)(2,1)S(1)} %fusion.70), channel_id=1, source_target_pairs={{0,1},{1,0},{2,3},{3,2},{4,5},{5,4},{6,7},{7,6},{8,9},{9,8},{10,11... | collective-permute-start | bytes 3145736 | tf_op jit(solution)/shard_map/ppermute | solution.py:443
  955.5 213.0 %collective-permute-start.78 = (bf16[4,64,2048]{2,1,0:T(8,128)(2,1)}, bf16[4,64,2048]{2,1,0:T(8,128)(2,1)}, u32[]{:S(2)}, u32[]{:S(2)}) collective-permute-start(bf16[4,64,2048]{2,1,0:T(8,128)(2,1)} %fusion.69), channel_id=1, source_target_pairs={{0,1},{1,0},{2,3},{3,2},{4,5},{5,4},{6,7},{7,6},{8,9},{9,8},{10,11... | collective-permute-start | bytes 3145736 | tf_op jit(solution)/shard_map/ppermute | solution.py:443
  959.0 61.6 %collective-permute-start.48 = (bf16[4,64,2048]{2,1,0:T(8,128)(2,1)S(1)}, bf16[4,64,2048]{2,1,0:T(8,128)(2,1)S(1)}, u32[]{:S(2)}, u32[]{:S(2)}) collective-permute-start(bf16[4,64,2048]{2,1,0:T(8,128)(2,1)S(1)} %fusion.67), channel_id=1, source_target_pairs={{0,1},{1,0},{2,3},{3,2},{4,5},{5,4},{6,7},{7,6},{8,9},{9,8},{10,11... | collective-permute-start | bytes 3145736 | tf_op jit(solution)/shard_map/ppermute | solution.py:443
  963.8 237.1 %collective-permute-start.58 = (bf16[512,2048]{1,0:T(8,128)(2,1)}, bf16[512,2048]{1,0:T(8,128)(2,1)}, u32[]{:S(2)}, u32[]{:S(2)}) collective-permute-start(bf16[512,2048]{1,0:T(8,128)(2,1)} %add_convert_fusion.1), channel_id=1, source_target_pairs={{0,16},{8,24},{16,0},{24,8},{1,17},{9,25},{17,1},{25,9},{2,18},{10... | collective-permute-start | bytes 6291464 | tf_op jit(solution)/shard_map/ppermute | solution.py:443
  977.6 194.5 %collective-permute-start.81 = (bf16[4,64,2048]{2,1,0:T(8,128)(2,1)}, bf16[4,64,2048]{2,1,0:T(8,128)(2,1)}, u32[]{:S(2)}, u32[]{:S(2)}) collective-permute-start(bf16[4,64,2048]{2,1,0:T(8,128)(2,1)} %fusion.38), channel_id=1, source_target_pairs={{0,16},{8,24},{16,0},{24,8},{1,17},{9,25},{17,1},{25,9},{2,18},{10... | collective-permute-start | bytes 3145736 | tf_op jit(solution)/shard_map/ppermute | solution.py:443
  1168.5 25.4 %collective-permute-start.46 = (bf16[4,64,2048]{2,1,0:T(8,128)(2,1)S(1)}, bf16[4,64,2048]{2,1,0:T(8,128)(2,1)S(1)}, u32[]{:S(2)}, u32[]{:S(2)}) collective-permute-start(bf16[4,64,2048]{2,1,0:T(8,128)(2,1)S(1)} %copy-done.105), channel_id=1, source_target_pairs={{0,1},{1,0},{2,3},{3,2},{4,5},{5,4},{6,7},{7,6},{8,9},{9,8},{10,11... | collective-permute-start | bytes 3145736 | tf_op jit(solution)/shard_map/ppermute | solution.py:443
  1170.0 25.1 %collective-permute-start.49 = (bf16[4,64,2048]{2,1,0:T(8,128)(2,1)S(1)}, bf16[4,64,2048]{2,1,0:T(8,128)(2,1)S(1)}, u32[]{:S(2)}, u32[]{:S(2)}) collective-permute-start(bf16[4,64,2048]{2,1,0:T(8,128)(2,1)S(1)} %copy-done.99), channel_id=1, source_target_pairs={{0,16},{8,24},{16,0},{24,8},{1,17},{9,25},{17,1},{25,9},{2,18},{10... | collective-permute-start | bytes 3145736 | tf_op jit(solution)/shard_map/ppermute | solution.py:443
  1172.1 90.1 %collective-permute-start.26 = (bf16[512,2048]{1,0:T(8,128)(2,1)}, bf16[512,2048]{1,0:T(8,128)(2,1)}, u32[]{:S(2)}, u32[]{:S(2)}) collective-permute-start(bf16[512,2048]{1,0:T(8,128)(2,1)} %convolution_convert_fusion.12), channel_id=1, source_target_pairs={{0,8},{8,0},{16,24},{24,16},{1,9},{9,1},{17,25},{25,17},{2,10},{10... | collective-permute-start | bytes 6291464 | tf_op jit(solution)/shard_map/ppermute | solution.py:443
  1193.9 38.0 %collective-permute-start.4 = (f32[512,464]{0,1:T(8,128)S(1)}, f32[512,464]{0,1:T(8,128)S(1)}, u32[]{:S(2)}, u32[]{:S(2)}) collective-permute-start(f32[512,464]{0,1:T(8,128)S(1)} %get-tuple-element.296), channel_id=1, source_target_pairs={{0,8},{8,0},{16,24},{24,16},{1,9},{9,1},{17,25},{25,17},{2,10},{10... | collective-permute-start | bytes 2850824 | tf_op jit(solution)/shard_map/ppermute | solution.py:443
  1195.1 47.0 %collective-permute-start.6 = (f32[512,464]{0,1:T(8,128)S(1)}, f32[512,464]{0,1:T(8,128)S(1)}, u32[]{:S(2)}, u32[]{:S(2)}) collective-permute-start(f32[512,464]{0,1:T(8,128)S(1)} %dynamic-slice_add_fusion), channel_id=1, source_target_pairs={{0,16},{8,24},{16,0},{24,8},{1,17},{9,25},{17,1},{25,9},{2,18},{10... | collective-permute-start | bytes 2850824 | tf_op jit(solution)/shard_map/ppermute | solution.py:443
  1226.7 35.0 %collective-permute-start.59 = (bf16[4,64,2048]{2,1,0:T(8,128)(2,1)}, bf16[4,64,2048]{2,1,0:T(8,128)(2,1)}, u32[]{:S(2)}, u32[]{:S(2)}) collective-permute-start(bf16[4,64,2048]{2,1,0:T(8,128)(2,1)} %fusion.68), channel_id=1, source_target_pairs={{0,1},{1,0},{2,3},{3,2},{4,5},{5,4},{6,7},{7,6},{8,9},{9,8},{10,11... | collective-permute-start | bytes 3145736 | tf_op jit(solution)/shard_map/ppermute | solution.py:443
  1240.8 116.5 %collective-permute-start.68 = (bf16[512,7168]{1,0:T(8,128)(2,1)}, bf16[512,7168]{1,0:T(8,128)(2,1)}, u32[]{:S(2)}, u32[]{:S(2)}) collective-permute-start(bf16[512,7168]{1,0:T(8,128)(2,1)} %convolution_convert_fusion), channel_id=1, source_target_pairs={{0,8},{8,0},{16,24},{24,16},{1,9},{9,1},{17,25},{25,17},{2,10},{10... | collective-permute-start | bytes 22020104 | tf_op jit(solution)/shard_map/ppermute | solution.py:443
  1240.8 31.3 %collective-permute-start.16 = (bf16[512,2048]{1,0:T(8,128)(2,1)}, bf16[512,2048]{1,0:T(8,128)(2,1)}, u32[]{:S(2)}, u32[]{:S(2)}) collective-permute-start(bf16[512,2048]{1,0:T(8,128)(2,1)} %convolution_convert_fusion.14), channel_id=1, source_target_pairs={{0,8},{8,0},{16,24},{24,16},{1,9},{9,1},{17,25},{25,17},{2,10},{10... | collective-permute-start | bytes 6291464 | tf_op jit(solution)/shard_map/ppermute | solution.py:443
  1261.7 107.1 %collective-permute-start.66 = (bf16[512,7168]{1,0:T(8,128)(2,1)}, bf16[512,7168]{1,0:T(8,128)(2,1)}, u32[]{:S(2)}, u32[]{:S(2)}) collective-permute-start(bf16[512,7168]{1,0:T(8,128)(2,1)} %convolution_convert_fusion.1), channel_id=1, source_target_pairs={{0,8},{8,0},{16,24},{24,16},{1,9},{9,1},{17,25},{25,17},{2,10},{10... | collective-permute-start | bytes 22020104 | tf_op jit(solution)/shard_map/ppermute | solution.py:443
  1262.3 22.5 %collective-permute-start.14 = (bf16[512,2048]{1,0:T(8,128)(2,1)}, bf16[512,2048]{1,0:T(8,128)(2,1)S(1)}, u32[]{:S(2)}, u32[]{:S(2)}) collective-permute-start(bf16[512,2048]{1,0:T(8,128)(2,1)} %convolution_convert_fusion.15), channel_id=1, source_target_pairs={{0,8},{8,0},{16,24},{24,16},{1,9},{9,1},{17,25},{25,17},{2,10},{10... | collective-permute-start | bytes 6291464 | tf_op jit(solution)/shard_map/ppermute | solution.py:443
  1284.7 35.4 %collective-permute-start.63 = (bf16[64,2048]{1,0:T(8,128)(2,1)}, bf16[64,2048]{1,0:T(8,128)(2,1)}, u32[]{:S(2)}, u32[]{:S(2)}) collective-permute-start(bf16[64,2048]{1,0:T(8,128)(2,1)} %get-tuple-element.318), channel_id=1, source_target_pairs={{6,4},{7,5},{14,12},{15,13},{22,20},{23,21},{30,28},{31,29}} | collective-permute-start | bytes 786440 | tf_op jit(solution)/shard_map/ppermute | solution.py:452
  1296.0 25.6 %collective-permute-start.61 = (bf16[64,2048]{1,0:T(8,128)(2,1)S(1)}, bf16[64,2048]{1,0:T(8,128)(2,1)}, u32[]{:S(2)}, u32[]{:S(2)}) collective-permute-start(bf16[64,2048]{1,0:T(8,128)(2,1)S(1)} %fusion.130), channel_id=1, source_target_pairs={{0,2},{1,3},{2,4},{3,5},{8,10},{9,11},{10,12},{11,13},{16,18},{17,... | collective-permute-start | bytes 786440 | tf_op jit(solution)/shard_map/ppermute | solution.py:452
  1319.0 85.7 %collective-permute-start.89 = (bf16[1792,2048]{1,0:T(8,128)(2,1)}, bf16[1792,2048]{1,0:T(8,128)(2,1)}, u32[]{:S(2)}, u32[]{:S(2)}) collective-permute-start(bf16[1792,2048]{1,0:T(8,128)(2,1)} %convolution_convert_fusion.2), channel_id=1, source_target_pairs={{0,8},{8,0},{16,24},{24,16},{1,9},{9,1},{17,25},{25,17},{2,10},{10... | collective-permute-start | bytes 22020104 | tf_op jit(solution)/shard_map/ppermute | solution.py:443
  1330.3 25.0 %collective-permute-start.17 = (bf16[4,64,2048]{2,1,0:T(8,128)(2,1)}, bf16[4,64,2048]{2,1,0:T(8,128)(2,1)S(1)}, u32[]{:S(2)}, u32[]{:S(2)}) collective-permute-start(bf16[4,64,2048]{2,1,0:T(8,128)(2,1)} %fusion.63), channel_id=1, source_target_pairs={{0,1},{1,0},{2,3},{3,2},{4,5},{5,4},{6,7},{7,6},{8,9},{9,8},{10,11... | collective-permute-start | bytes 3145736 | tf_op jit(solution)/shard_map/ppermute | solution.py:443
  1346.3 72.2 %collective-permute-start.25 = (bf16[512,2048]{1,0:T(8,128)(2,1)}, bf16[512,2048]{1,0:T(8,128)(2,1)}, u32[]{:S(2)}, u32[]{:S(2)}) collective-permute-start(bf16[512,2048]{1,0:T(8,128)(2,1)} %convolution_convert_fusion.13), channel_id=1, source_target_pairs={{0,8},{8,0},{16,24},{24,16},{1,9},{9,1},{17,25},{25,17},{2,10},{10... | collective-permute-start | bytes 6291464 | tf_op jit(solution)/shard_map/ppermute | solution.py:443
  1355.3 89.9 %collective-permute-start.35 = (bf16[512,2048]{1,0:T(8,128)(2,1)}, bf16[512,2048]{1,0:T(8,128)(2,1)}, u32[]{:S(2)}, u32[]{:S(2)}) collective-permute-start(bf16[512,2048]{1,0:T(8,128)(2,1)} %convolution_convert_fusion.11), channel_id=1, source_target_pairs={{0,8},{8,0},{16,24},{24,16},{1,9},{9,1},{17,25},{25,17},{2,10},{10... | collective-permute-start | bytes 6291464 | tf_op jit(solution)/shard_map/ppermute | solution.py:443
  1357.3 28.0 %collective-permute-start.15 = (bf16[4,64,2048]{2,1,0:T(8,128)(2,1)S(1)}, bf16[4,64,2048]{2,1,0:T(8,128)(2,1)S(1)}, u32[]{:S(2)}, u32[]{:S(2)}) collective-permute-start(bf16[4,64,2048]{2,1,0:T(8,128)(2,1)S(1)} %copy-done.106), channel_id=1, source_target_pairs={{0,1},{1,0},{2,3},{3,2},{4,5},{5,4},{6,7},{7,6},{8,9},{9,8},{10,11... | collective-permute-start | bytes 3145736 | tf_op jit(solution)/shard_map/ppermute | solution.py:443
  1368.7 26.0 %collective-permute-start.18 = (bf16[4,64,2048]{2,1,0:T(8,128)(2,1)S(1)}, bf16[4,64,2048]{2,1,0:T(8,128)(2,1)S(1)}, u32[]{:S(2)}, u32[]{:S(2)}) collective-permute-start(bf16[4,64,2048]{2,1,0:T(8,128)(2,1)S(1)} %fusion.42), channel_id=1, source_target_pairs={{0,16},{8,24},{16,0},{24,8},{1,17},{9,25},{17,1},{25,9},{2,18},{10... | collective-permute-start | bytes 3145736 | tf_op jit(solution)/shard_map/ppermute | solution.py:443
  1385.3 54.5 %collective-permute-start.27 = (bf16[512,2048]{1,0:T(8,128)(2,1)}, bf16[512,2048]{1,0:T(8,128)(2,1)}, u32[]{:S(2)}, u32[]{:S(2)}) collective-permute-start(bf16[512,2048]{1,0:T(8,128)(2,1)} %add_convert_fusion.3), channel_id=1, source_target_pairs={{0,16},{8,24},{16,0},{24,8},{1,17},{9,25},{17,1},{25,9},{2,18},{10... | collective-permute-start | bytes 6291464 | tf_op jit(solution)/shard_map/ppermute | solution.py:443
  1404.8 79.8 %collective-permute-start.37 = (bf16[512,2048]{1,0:T(8,128)(2,1)S(1)}, bf16[512,2048]{1,0:T(8,128)(2,1)S(1)}, u32[]{:S(2)}, u32[]{:S(2)}) collective-permute-start(bf16[512,2048]{1,0:T(8,128)(2,1)S(1)} %copy-done.92), channel_id=1, source_target_pairs={{0,16},{8,24},{16,0},{24,8},{1,17},{9,25},{17,1},{25,9},{2,18},{10... | collective-permute-start | bytes 6291464 | tf_op jit(solution)/shard_map/ppermute | solution.py:443
  1418.4 222.0 %collective-permute-start.88 = (bf16[1792,2048]{1,0:T(8,128)(2,1)}, bf16[1792,2048]{1,0:T(8,128)(2,1)}, u32[]{:S(2)}, u32[]{:S(2)}) collective-permute-start(bf16[1792,2048]{1,0:T(8,128)(2,1)} %convolution_convert_fusion.3), channel_id=1, source_target_pairs={{0,8},{8,0},{16,24},{24,16},{1,9},{9,1},{17,25},{25,17},{2,10},{10... | collective-permute-start | bytes 22020104 | tf_op jit(solution)/shard_map/ppermute | solution.py:443
  1418.5 224.4 %collective-permute-start.90 = (bf16[1792,2048]{1,0:T(8,128)(2,1)}, bf16[1792,2048]{1,0:T(8,128)(2,1)}, u32[]{:S(2)}, u32[]{:S(2)}) collective-permute-start(bf16[1792,2048]{1,0:T(8,128)(2,1)} %add_convert_fusion), channel_id=1, source_target_pairs={{0,16},{8,24},{16,0},{24,8},{1,17},{9,25},{17,1},{25,9},{2,18},{10... | collective-permute-start | bytes 22020104 | tf_op jit(solution)/shard_map/ppermute | solution.py:443
  1444.1 51.2 %collective-permute-start.28 = (bf16[4,64,2048]{2,1,0:T(8,128)(2,1)S(1)}, bf16[4,64,2048]{2,1,0:T(8,128)(2,1)S(1)}, u32[]{:S(2)}, u32[]{:S(2)}) collective-permute-start(bf16[4,64,2048]{2,1,0:T(8,128)(2,1)S(1)} %fusion.64), channel_id=1, source_target_pairs={{0,1},{1,0},{2,3},{3,2},{4,5},{5,4},{6,7},{7,6},{8,9},{9,8},{10,11... | collective-permute-start | bytes 3145736 | tf_op jit(solution)/shard_map/ppermute | solution.py:443
  1445.2 43.9 %collective-permute-start.21 = (bf16[64,2048]{1,0:T(8,128)(2,1)S(1)}, bf16[64,2048]{1,0:T(8,128)(2,1)S(1)}, u32[]{:S(2)}, u32[]{:S(2)}) collective-permute-start(bf16[64,2048]{1,0:T(8,128)(2,1)S(1)} %get-tuple-element.331), channel_id=1, source_target_pairs={{0,2},{1,3},{2,4},{3,5},{4,6},{5,7},{8,10},{9,11},{10,12},{11,13},... | collective-permute-start | bytes 786440 | tf_op jit(solution)/shard_map/ppermute | solution.py:452
  1489.1 141.7 %collective-permute-start.69 = (bf16[4,64,7168]{2,1,0:T(8,128)(2,1)}, bf16[4,64,7168]{2,1,0:T(8,128)(2,1)}, u32[]{:S(2)}, u32[]{:S(2)}) collective-permute-start(bf16[4,64,7168]{2,1,0:T(8,128)(2,1)} %fusion.14), channel_id=1, source_target_pairs={{0,1},{1,0},{2,3},{3,2},{4,5},{5,4},{6,7},{7,6},{8,9},{9,8},{10,11... | collective-permute-start | bytes 11010056 | tf_op jit(solution)/shard_map/ppermute | solution.py:443
  1493.4 98.4 %collective-permute-start.38 = (bf16[4,64,2048]{2,1,0:T(8,128)(2,1)S(1)}, bf16[4,64,2048]{2,1,0:T(8,128)(2,1)S(1)}, u32[]{:S(2)}, u32[]{:S(2)}) collective-permute-start(bf16[4,64,2048]{2,1,0:T(8,128)(2,1)S(1)} %fusion.65), channel_id=1, source_target_pairs={{0,1},{1,0},{2,3},{3,2},{4,5},{5,4},{6,7},{7,6},{8,9},{9,8},{10,11... | collective-permute-start | bytes 3145736 | tf_op jit(solution)/shard_map/ppermute | solution.py:443
  1495.7 97.3 %collective-permute-start.29 = (bf16[64,2048]{1,0:T(8,128)(2,1)S(1)}, bf16[64,2048]{1,0:T(8,128)(2,1)S(1)}, u32[]{:S(2)}, u32[]{:S(2)}) collective-permute-start(bf16[64,2048]{1,0:T(8,128)(2,1)S(1)} %get-tuple-element.329), channel_id=1, source_target_pairs={{0,2},{1,3},{8,10},{9,11},{16,18},{17,19},{24,26},{25,27}} | collective-permute-start | bytes 786440 | tf_op jit(solution)/shard_map/ppermute | solution.py:452
  1614.0 82.7 %collective-permute-start.67 = (bf16[4,64,7168]{2,1,0:T(8,128)(2,1)}, bf16[4,64,7168]{2,1,0:T(8,128)(2,1)}, u32[]{:S(2)}, u32[]{:S(2)}) collective-permute-start(bf16[4,64,7168]{2,1,0:T(8,128)(2,1)} %fusion.13), channel_id=1, source_target_pairs={{0,1},{1,0},{2,3},{3,2},{4,5},{5,4},{6,7},{7,6},{8,9},{9,8},{10,11... | collective-permute-start | bytes 11010056 | tf_op jit(solution)/shard_map/ppermute | solution.py:443
  1619.4 41.9 %collective-permute-start.31 = (bf16[64,2048]{1,0:T(8,128)(2,1)S(1)}, bf16[64,2048]{1,0:T(8,128)(2,1)S(1)}, u32[]{:S(2)}, u32[]{:S(2)}) collective-permute-start(bf16[64,2048]{1,0:T(8,128)(2,1)S(1)} %get-tuple-element.327), channel_id=1, source_target_pairs={{0,2},{1,3},{2,4},{3,5},{4,6},{5,7},{8,10},{9,11},{10,12},{11,13},... | collective-permute-start | bytes 786440 | tf_op jit(solution)/shard_map/ppermute | solution.py:452
  1638.7 81.2 %collective-permute-start.70 = (bf16[4,64,7168]{2,1,0:T(8,128)(2,1)}, bf16[4,64,7168]{2,1,0:T(8,128)(2,1)S(1)}, u32[]{:S(2)}, u32[]{:S(2)}) collective-permute-start(bf16[4,64,7168]{2,1,0:T(8,128)(2,1)} %fusion.11), channel_id=1, source_target_pairs={{0,16},{8,24},{16,0},{24,8},{1,17},{9,25},{17,1},{25,9},{2,18},{10... | collective-permute-start | bytes 11010056 | tf_op jit(solution)/shard_map/ppermute | solution.py:443
  1640.3 25.3 %collective-permute-start.41 = (bf16[64,2048]{1,0:T(8,128)(2,1)}, bf16[64,2048]{1,0:T(8,128)(2,1)S(1)}, u32[]{:S(2)}, u32[]{:S(2)}) collective-permute-start(bf16[64,2048]{1,0:T(8,128)(2,1)} %get-tuple-element.323), channel_id=1, source_target_pairs={{0,2},{1,3},{2,4},{3,5},{4,6},{5,7},{8,10},{9,11},{10,12},{11,13},... | collective-permute-start | bytes 786440 | tf_op jit(solution)/shard_map/ppermute | solution.py:452
  1642.9 19.7 %collective-permute-start.34 = (bf16[64,2048]{1,0:T(8,128)(2,1)S(1)}, bf16[64,2048]{1,0:T(8,128)(2,1)S(1)}, u32[]{:S(2)}, u32[]{:S(2)}) collective-permute-start(bf16[64,2048]{1,0:T(8,128)(2,1)S(1)} %fusion.144), channel_id=1, source_target_pairs={{2,0},{3,1},{4,2},{5,3},{6,4},{7,5},{10,8},{11,9},{12,10},{13,11},... | collective-permute-start | bytes 786440 | tf_op jit(solution)/shard_map/ppermute | solution.py:452
  1662.6 107.5 %collective-permute-start.91 = (bf16[4,224,2048]{2,1,0:T(8,128)(2,1)}, bf16[4,224,2048]{2,1,0:T(8,128)(2,1)}, u32[]{:S(2)}, u32[]{:S(2)}) collective-permute-start(bf16[4,224,2048]{2,1,0:T(8,128)(2,1)} %fusion.15), channel_id=1, source_target_pairs={{0,1},{1,0},{2,3},{3,2},{4,5},{5,4},{6,7},{7,6},{8,9},{9,8},{10,11... | collective-permute-start | bytes 11010056 | tf_op jit(solution)/shard_map/ppermute | solution.py:443
  1665.6 128.9 %collective-permute-start.52 = (bf16[64,2048]{1,0:T(8,128)(2,1)}, bf16[64,2048]{1,0:T(8,128)(2,1)}, u32[]{:S(2)}, u32[]{:S(2)}) collective-permute-start(bf16[64,2048]{1,0:T(8,128)(2,1)} %get-tuple-element.319), channel_id=1, source_target_pairs={{0,2},{1,3},{2,4},{3,5},{4,6},{5,7},{8,10},{9,11},{10,12},{11,13},... | collective-permute-start | bytes 786440 | tf_op jit(solution)/shard_map/ppermute | solution.py:452
  1672.1 123.1 %collective-permute-start.55 = (bf16[64,2048]{1,0:T(8,128)(2,1)S(1)}, bf16[64,2048]{1,0:T(8,128)(2,1)}, u32[]{:S(2)}, u32[]{:S(2)}) collective-permute-start(bf16[64,2048]{1,0:T(8,128)(2,1)S(1)} %copy-done.116), channel_id=1, source_target_pairs={{2,0},{3,1},{4,2},{5,3},{6,4},{7,5},{10,8},{11,9},{12,10},{13,11},... | collective-permute-start | bytes 786440 | tf_op jit(solution)/shard_map/ppermute | solution.py:452
  1696.7 138.9 %collective-permute-start.62 = (bf16[64,2048]{1,0:T(8,128)(2,1)}, bf16[64,2048]{1,0:T(8,128)(2,1)}, u32[]{:S(2)}, u32[]{:S(2)}) collective-permute-start(bf16[64,2048]{1,0:T(8,128)(2,1)} %get-tuple-element.315), channel_id=1, source_target_pairs={{0,2},{1,3},{2,4},{3,5},{4,6},{5,7},{8,10},{9,11},{10,12},{11,13},... | collective-permute-start | bytes 786440 | tf_op jit(solution)/shard_map/ppermute | solution.py:452
  1721.8 113.8 %collective-permute-start.65 = (bf16[64,2048]{1,0:T(8,128)(2,1)S(1)}, bf16[64,2048]{1,0:T(8,128)(2,1)}, u32[]{:S(2)}, u32[]{:S(2)}) collective-permute-start(bf16[64,2048]{1,0:T(8,128)(2,1)S(1)} %fusion.129), channel_id=1, source_target_pairs={{2,0},{3,1},{4,2},{5,3},{6,4},{7,5},{10,8},{11,9},{12,10},{13,11},... | collective-permute-start | bytes 786440 | tf_op jit(solution)/shard_map/ppermute | solution.py:452
  1788.7 25.2 %collective-permute-start.92 = (bf16[224,2048]{1,0:T(8,128)(2,1)S(1)}, bf16[224,2048]{1,0:T(8,128)(2,1)S(1)}, u32[]{:S(2)}, u32[]{:S(2)}) collective-permute-start(bf16[224,2048]{1,0:T(8,128)(2,1)S(1)} %get-tuple-element.285), channel_id=1, source_target_pairs={{0,2},{1,3},{8,10},{9,11},{16,18},{17,19},{24,26},{25,27}} | collective-permute-start | bytes 2752520 | tf_op jit(solution)/shard_map/ppermute | solution.py:452
  1794.5 20.3 %collective-permute-start.74 = (bf16[64,7168]{1,0:T(8,128)(2,1)S(1)}, bf16[64,7168]{1,0:T(8,128)(2,1)S(1)}, u32[]{:S(2)}, u32[]{:S(2)}) collective-permute-start(bf16[64,7168]{1,0:T(8,128)(2,1)S(1)} %get-tuple-element.290), channel_id=1, source_target_pairs={{6,4},{7,5},{14,12},{15,13},{22,20},{23,21},{30,28},{31,29}} | collective-permute-start | bytes 2752520 | tf_op jit(solution)/shard_map/ppermute | solution.py:452
  1795.2 38.3 %collective-permute-start.72 = (bf16[64,7168]{1,0:T(8,128)(2,1)S(1)}, bf16[64,7168]{1,0:T(8,128)(2,1)S(1)}, u32[]{:S(2)}, u32[]{:S(2)}) collective-permute-start(bf16[64,7168]{1,0:T(8,128)(2,1)S(1)} %fusion.55), channel_id=1, source_target_pairs={{0,2},{1,3},{2,4},{3,5},{8,10},{9,11},{10,12},{11,13},{16,18},{17,... | collective-permute-start | bytes 2752520 | tf_op jit(solution)/shard_map/ppermute | solution.py:452
  1813.8 29.8 %collective-permute-start.95 = (bf16[224,2048]{1,0:T(8,128)(2,1)S(1)}, bf16[224,2048]{1,0:T(8,128)(2,1)S(1)}, u32[]{:S(2)}, u32[]{:S(2)}) collective-permute-start(bf16[224,2048]{1,0:T(8,128)(2,1)S(1)} %get-tuple-element.286), channel_id=1, source_target_pairs={{6,4},{7,5},{14,12},{15,13},{22,20},{23,21},{30,28},{31,29}} | collective-permute-start | bytes 2752520 | tf_op jit(solution)/shard_map/ppermute | solution.py:452
  1814.8 38.3 %collective-permute-start.93 = (bf16[224,2048]{1,0:T(8,128)(2,1)S(1)}, bf16[224,2048]{1,0:T(8,128)(2,1)S(1)}, u32[]{:S(2)}, u32[]{:S(2)}) collective-permute-start(bf16[224,2048]{1,0:T(8,128)(2,1)S(1)} %fusion.50), channel_id=1, source_target_pairs={{0,2},{1,3},{2,4},{3,5},{8,10},{9,11},{10,12},{11,13},{16,18},{17,... | collective-permute-start | bytes 2752520 | tf_op jit(solution)/shard_map/ppermute | solution.py:452
  1834.9 22.0 %collective-permute-start.75 = (bf16[64,7168]{1,0:T(8,128)(2,1)S(1)}, bf16[64,7168]{1,0:T(8,128)(2,1)S(1)}, u32[]{:S(2)}, u32[]{:S(2)}) collective-permute-start(bf16[64,7168]{1,0:T(8,128)(2,1)S(1)} %get-tuple-element.288), channel_id=1, source_target_pairs={{4,2},{5,3},{6,4},{7,5},{12,10},{13,11},{14,12},{15,13},{20,18},{2... | collective-permute-start | bytes 2752520 | tf_op jit(solution)/shard_map/ppermute | solution.py:452
  1837.5 39.6 %collective-permute-start.73 = (bf16[64,7168]{1,0:T(8,128)(2,1)}, bf16[64,7168]{1,0:T(8,128)(2,1)}, u32[]{:S(2)}, u32[]{:S(2)}) collective-permute-start(bf16[64,7168]{1,0:T(8,128)(2,1)} %get-tuple-element.287), channel_id=1, source_target_pairs={{0,2},{1,3},{2,4},{3,5},{4,6},{5,7},{8,10},{9,11},{10,12},{11,13},... | collective-permute-start | bytes 2752520 | tf_op jit(solution)/shard_map/ppermute | solution.py:452
  1858.0 21.0 %collective-permute-start.76 = (bf16[64,7168]{1,0:T(8,128)(2,1)}, bf16[64,7168]{1,0:T(8,128)(2,1)}, u32[]{:S(2)}, u32[]{:S(2)}) collective-permute-start(bf16[64,7168]{1,0:T(8,128)(2,1)} %fusion.54), channel_id=1, source_target_pairs={{2,0},{3,1},{4,2},{5,3},{6,4},{7,5},{10,8},{11,9},{12,10},{13,11},... | collective-permute-start | bytes 2752520 | tf_op jit(solution)/shard_map/ppermute | solution.py:452
  1875.6 24.1 %collective-permute-start.97 = (bf16[224,2048]{1,0:T(8,128)(2,1)}, bf16[224,2048]{1,0:T(8,128)(2,1)}, u32[]{:S(2)}, u32[]{:S(2)}) collective-permute-start(bf16[224,2048]{1,0:T(8,128)(2,1)} %fusion.49), channel_id=1, source_target_pairs={{2,0},{3,1},{4,2},{5,3},{6,4},{7,5},{10,8},{11,9},{12,10},{13,11},... | collective-permute-start | bytes 2752520 | tf_op jit(solution)/shard_map/ppermute | solution.py:452
  (190 other events, 3438.9 us)
Sparse Core Ops, SparseCore 0:
  12.4 64.7 all-gather.11
  80.8 233.4 all-gather.13
  342.0 22.2 all-gather.21
  367.7 174.8 all-gather.17
  545.4 173.0 all-gather.19
  721.8 75.4 all-gather.15
  946.8 26.4 all-gather.23

commit v2 on v1

--- a/solution.py
+++ b/solution.py
@@ -418,13 +418,22 @@
 
 def prefix(carry, state, reverse):
     n, here = lax.axis_size("seq"), lax.axis_index("seq")
-    every = lax.all_gather(jnp.concatenate([state, carry], 0), "seq")
-    total = jnp.zeros_like(state)
-    for k in range(n):
-        at = n - 1 - k if reverse else k
-        reached = at > here if reverse else at < here
-        total = jnp.where(reached, every[at, -1:] * total + every[at, :-1], total)
-    return total
+    own = jnp.concatenate([state, carry], 0)
+    if not tuned():
+        every = lax.all_gather(own, "seq")
+        total = jnp.zeros_like(state)
+        for k in range(n):
+            at = n - 1 - k if reverse else k
+            reached = at > here if reverse else at < here
+            total = jnp.where(reached, every[at, -1:] * total + every[at, :-1], total)
+        return total
+    other = swap(own, "seq", 1)
+    other_state, other_carry = other[:-1], other[-1:]
+    second = (here % 2 == 1) != reverse
+    chip = jnp.where(second, carry * other_state + state, other_carry * state + other_state)
+    pairs = [(2, 0), (3, 1)] if reverse else [(0, 2), (1, 3)]
+    arrived = lax.ppermute(chip, "seq", pairs)
+    return jnp.where(second, other_carry * arrived + other_state, arrived)
 
 
 def product(left, right):
@@ -443,81 +452,143 @@
     return lax.ppermute(value, axis, [(i, i ^ bit) for i in range(lax.axis_size(axis))])
 
 
-def climb(value, step, count):
-    planes = lax.axis_size("dp") // 2
-    pairs = []
-    for z in range(planes):
-        if (step > 0 and z < count and z + 1 < planes) or (step < 0 and z >= planes - count and z > 0):
-            pairs += [(2 * z + y, 2 * (z + step) + y) for y in (0, 1)]
-    return lax.ppermute(value, "dp", pairs)
+def to_plane(value, step):
+    n = lax.axis_size("dp")
+    return lax.ppermute(value, "dp", [(i, (i + 2 * step) % n) for i in range(n)])
 
 
 def pick(value, index, axis=0):
     return lax.dynamic_index_in_dim(value, index, axis, keepdims=False)
 
 
-def down_z(whole, kind):
-    z = lax.axis_index("dp") // 2
-    planes = whole.shape[0]
-    ends = []
-    for step in (1, -1):
-        carried = None
-        for t in range(1, planes):
-            part = pick(whole, (z + step * (planes - t)) % planes)
-            carried = part if carried is None else part + carried
-            carried = climb(carried.astype(kind), step, t).astype(F32)
-        ends.append(carried)
-    return pick(whole, z) + ends[0] + ends[1]
-
-
-def scatter_sum(block, rows, kind, x_first):
+def tuned():
+    return (lax.axis_size("seq"), lax.axis_size("dp")) == (4, 8)
+
+
+class Steps:
+    def __init__(self):
+        self.units = []
+
+    def add(self, *units):
+        self.units.extend([unit, None, None] for unit in units)
+        return self.units[-len(units) :]
+
+    def tick(self, values=()):
+        live = [u for u in self.units if u[0] is not None]
+        waiting, values = lax.optimization_barrier(([u[1] for u in live], values))
+        for unit, arrived in zip(live, waiting):
+            try:
+                unit[1] = unit[0].send(arrived)
+            except StopIteration as stop:
+                unit[:] = [None, None, stop.value]
+        return values
+
+    def drain(self):
+        while any(u[0] is not None for u in self.units):
+            self.tick()
+
+
+def gather_unit(shard):
+    d = lax.axis_index("dp")
+    z, y = d // 2, d % 2
+    arrived = yield [to_plane(shard, t) for t in (1, 2, 3)]
+    column = jnp.stack([shard, *arrived])
+    (other,) = yield [swap(column, "dp", 1)]
+    both = jnp.concatenate([column, other], 0)
+    chunks = [pick(both, ((k ^ y) * 4) + (z - j) % 4) for j in range(4) for k in (0, 1)]
+    slab = jnp.concatenate(chunks, 0)
+    across, near = yield [swap(slab, "seq", 2), swap(slab, "seq", 1)]
+    (far,) = yield [swap(across, "seq", 1)]
+    return [slab, near, across, far]
+
+
+def plain_gather(shard):
+    return [lax.all_gather(shard, BOTH, axis=0, tiled=True)]
+    yield
+
+
+def gather(shard):
+    return gather_unit(shard) if tuned() else plain_gather(shard)
+
+
+def in_order(pieces):
+    if not tuned():
+        return pieces[0]
+    s, every = lax.axis_index("seq"), jnp.stack(pieces)
+    return jnp.concatenate([pick(every, s ^ j) for j in range(4)])
+
+
+def scatter_unit(first, second, rows, kind):
     s, d = lax.axis_index("seq"), lax.axis_index("dp")
-    y = d % 2
+    z, y = d // 2, d % 2
+    wide = rows * 8
 
     def parts(value):
-        return value.reshape(4, 2, rows, value.shape[-1])
-
-    far = swap(block(s ^ 3).astype(kind), "seq", 1)
-    near = swap(block(s ^ 1).astype(kind), "seq", 1)
-    if x_first:
-        across = swap((block(s ^ 2) + far.astype(F32)).astype(kind), "seq", 2)
-        own = parts(block(s) + near.astype(F32) + across.astype(F32))
-        other = swap(pick(own, 1 - y, 1).astype(kind), "dp", 1)
-        own = pick(own, y, 1) + other.astype(F32)
-    else:
-        across = parts(block(s ^ 2) + far.astype(F32))
-        own = parts(block(s) + near.astype(F32))
-        a = swap(pick(across, 1 - y, 1).astype(kind), "dp", 1)
-        b = swap(pick(own, 1 - y, 1).astype(kind), "dp", 1)
-        a = swap((pick(across, y, 1) + a.astype(F32)).astype(kind), "seq", 2)
-        own = pick(own, y, 1) + b.astype(F32) + a.astype(F32)
-    return down_z(own, kind)
-
-
-def weight_grad(left, grad, x_first):
-    n, m = lax.axis_size("seq"), lax.axis_size("dp")
-    wide = left.shape[1] // n
-    if (n, m) != (4, 8):
-        part = lax.psum_scatter(product_t(left, grad), "seq", scatter_dimension=0, tiled=True)
-        return lax.psum_scatter(part, "dp", scatter_dimension=0, tiled=True)
-
-    def block(i):
-        return product_t(lax.dynamic_slice_in_dim(left, i * wide, wide, 1), grad)
-
-    return scatter_sum(block, wide // m, BF, x_first)
-
-
-def small_grad(whole):
-    n, m = lax.axis_size("seq"), lax.axis_size("dp")
-    if (n, m) != (4, 8):
+        return value.reshape(-1, 4, 2, rows, value.shape[-1])
+
+    sends = [swap(f([s ^ 3, s ^ 1]).astype(kind), "seq", 1) for f in (first, second) if f]
+    one, *two = yield sends
+    sends = [swap((first([s ^ 2]) + one[:wide].astype(F32)).astype(kind), "seq", 2)]
+    if second:
+        both = parts((second([s ^ 2, s]) + two[0].astype(F32)).astype(kind))
+        sends.append(swap(pick(both, 1 - y, 2), "dp", 1))
+    across, *beside = yield sends
+    own = parts((first([s]) + one[wide:].astype(F32) + across.astype(F32)).astype(kind))
+    sends = [swap(pick(own, 1 - y, 2), "dp", 1)]
+    if second:
+        both = pick(both, y, 2).astype(F32) + beside[0].astype(F32)
+        sends.append(swap(both[0].astype(kind), "seq", 2))
+    beside, *across = yield sends
+    own = [(pick(own, y, 2)[0].astype(F32) + beside[0].astype(F32)).astype(kind)]
+    if second:
+        own.append((both[1] + across[0].astype(F32)).astype(kind))
+    own = jnp.stack(own, 1)
+    arrived = yield [to_plane(pick(own, (z + t) % 4), t) for t in (1, 2, 3)]
+    total = pick(own, z).astype(F32)
+    for part in arrived:
+        total = total + part.astype(F32)
+    return [total[i] for i in range(total.shape[0])]
+
+
+def plain_scatter(*wholes):
+    results = []
+    for whole in wholes:
         part = lax.psum_scatter(whole, "seq", scatter_dimension=0, tiled=True)
-        return lax.psum_scatter(part, "dp", scatter_dimension=0, tiled=True)
-    wide = whole.shape[0] // n
-
-    def block(i):
-        return lax.dynamic_slice_in_dim(whole, i * wide, wide, 0)
-
-    return scatter_sum(block, wide // m, F32, True)
+        results.append(lax.psum_scatter(part, "dp", scatter_dimension=0, tiled=True))
+    return results
+    yield
+
+
+def scatter(*pairs):
+    if not tuned():
+        return plain_scatter(*[product_t(left, grad) for left, grad in pairs])
+
+    def blocks(left, grad):
+        wide = left.shape[1] // 4
+
+        def block(shards):
+            taken = [lax.dynamic_slice_in_dim(left, i * wide, wide, 1) for i in shards]
+            return product_t(jnp.concatenate(taken, 1), grad)
+
+        return block
+
+    if len(pairs) == 1:
+        left, grad = pairs[0]
+        half = grad.shape[1] // 2
+        pairs = ((left, grad[:, :half]), (left, grad[:, half:]))
+    rows = pairs[0][0].shape[1] // 4 // lax.axis_size("dp")
+    return scatter_unit(*[blocks(*pair) for pair in pairs], rows, BF)
+
+
+def scatter_small(whole):
+    if not tuned():
+        return plain_scatter(whole)
+    wide = whole.shape[0] // 4
+
+    def block(shards):
+        return jnp.concatenate([lax.dynamic_slice_in_dim(whole, i * wide, wide, 0) for i in shards])
+
+    return scatter_unit(block, None, wide // 8, F32)
 
 
 def renew(weight, moment, average, grad, factor, tokens):
@@ -545,15 +616,17 @@
     small = jnp.concatenate(
         [vectors.T, maa_down, maa_up.reshape(5 * rank, -1).T, decay_down, decay_up.T], axis=1
     )
-    small = lax.all_gather(small, BOTH, axis=0, tiled=True)
-    cuts = np.cumsum([n_vec, n_down, 5 * rank, n_decay, n_decay])
-    vecs, down, up, ddown, dup = jnp.split(small, cuts[:-1], axis=1)
-    vecs, up, dup = vecs.T, up.T, dup.T
-
+    up_steps = Steps()
+    (small,) = up_steps.add(gather(small))
+    up_steps.drain()
     mix = lax.all_gather(mix_weights.astype(BF), BOTH, axis=1, tiled=True)
     fkey = lax.all_gather(ffn_key.astype(BF), BOTH, axis=0, tiled=True)
     fval = lax.all_gather(ffn_value.astype(BF), BOTH, axis=0, tiled=True)
     frec = lax.all_gather(ffn_recept.astype(BF), BOTH, axis=0, tiled=True)
+    small = in_order(small[-1])
+    cuts = np.cumsum([n_vec, n_down, 5 * rank, n_decay, n_decay])
+    vecs, down, up, ddown, dup = jnp.split(small, cuts[:-1], axis=1)
+    vecs, up, dup = vecs.T, up.T, dup.T
 
     hidden = block_input[0].astype(F32)
     normed, pull_norm_one = jax.vjp(norm_first, hidden, vecs)
@@ -584,13 +657,14 @@
     sigma = jax.nn.sigmoid(product(rec_in, frec))
     block_output = middle + sigma * kvals
 
+    steps = Steps()
     upstream = out_grad[0].astype(F32)
     grad_kvals = (upstream * sigma).astype(BF)
     grad_rpre = (upstream * kvals * sigma * (1.0 - sigma)).astype(BF)
-    sum_fval = weight_grad(squared, grad_kvals, True)
+    (sum_fval,) = steps.add(scatter((squared, grad_kvals)))
+    grad_kvals = steps.tick(grad_kvals)
     grad_kpre = (back_product(grad_kvals, fval) * (2.0 * positive)).astype(BF)
-    sum_fkey = weight_grad(key_in, grad_kpre, False)
-    sum_frec = weight_grad(rec_in, grad_rpre, False)
+    grad_kpre = steps.tick(grad_kpre)
     grad_second, grad_inc_two, vec_one = pull_channel(
         (back_product(grad_kpre, fkey), back_product(grad_rpre, frec))
     )
@@ -598,29 +672,31 @@
     grad_mid, vec_two = pull_norm_two(grad_second)
     grad_middle = upstream + grad_mid
     grad_attn = grad_middle.astype(BF)
-    sum_out = weight_grad(gated, grad_attn, True)
+    (sum_fkey,) = steps.add(scatter((key_in, grad_kpre)))
+    grad_attn = steps.tick(grad_attn)
     grad_gated = back_product(grad_attn, mix[4])
     grad_raw, grad_gate, direct, vec_head = head_back(
         keep, recept, logdec, raw, gate, grad_gated, vec3
     )
     later = prefix(carry, direct, True)
-    sum_gate = weight_grad(xgate, grad_gate, False)
+    later, grad_gate = steps.tick((later, grad_gate))
     grad_xgate = back_product(grad_gate, mix[3])
     grad_rec, grad_key, grad_val, grad_dec, vec_bonus = backward(
         keep, recept, keys, values, logdec, grad_raw, score, states, later, vec3
     )
-    sum_rec = weight_grad(xrec, grad_rec, True)
-    sum_key = weight_grad(xkey, grad_key, False)
-    sum_val = weight_grad(xval, grad_val, True)
-    grad_normed, grad_inc, vec_mix, gdown, gup, gddown, gdup = pull_mix(
-        (
-            back_product(grad_key, mix[0]),
-            back_product(grad_val, mix[1]),
-            back_product(grad_rec, mix[2]),
-            grad_xgate,
-            grad_dec,
-        )
-    )
+    (sum_rec_out,) = steps.add(scatter((rec_in, grad_rpre), (gated, grad_attn)))
+    grad_rec, grad_key, grad_val, grad_xgate = steps.tick(
+        (grad_rec, grad_key, grad_val, grad_xgate)
+    )
+    grad_x = (
+        back_product(grad_key, mix[0]),
+        back_product(grad_val, mix[1]),
+        back_product(grad_rec, mix[2]),
+        grad_xgate,
+        grad_dec,
+    )
+    grad_x = steps.tick(grad_x)
+    grad_normed, grad_inc, vec_mix, gdown, gup, gddown, gdup = pull_mix(grad_x)
     grad_normed = back_rows(grad_inc, grad_normed)
     grad_hidden, vec_three = pull_norm_one(grad_normed)
     input_grad = grad_middle + grad_hidden
@@ -629,14 +705,22 @@
     vec_all = jnp.concatenate(
         [vec_all[:9], vec_all[9:10] + vec_bonus, vec_all[10:12] + vec_head, vec_all[12:]], axis=0
     )
-    total = small_grad(jnp.concatenate([vec_all.T, gdown, gup.T, gddown, gdup.T], axis=1))
-    gvec, gdown, gup, gddown, gdup = jnp.split(total, cuts[:-1], axis=1)
+    total = jnp.concatenate([vec_all.T, gdown, gup.T, gddown, gdup.T], axis=1)
+    (sum_gate_rec,) = steps.add(scatter((xgate, grad_gate), (xrec, grad_rec)))
+    total, input_grad = steps.tick((total, input_grad))
+    (sum_small,) = steps.add(scatter_small(total))
+    steps.tick()
+    (sum_key_val,) = steps.add(scatter((xkey, grad_key), (xval, grad_val)))
+    steps.drain()
+
+    gvec, gdown, gup, gddown, gdup = jnp.split(sum_small[-1][0], cuts[:-1], axis=1)
+    grad_frec, grad_out = sum_rec_out[-1]
     grads = (
         gvec.T,
-        jnp.stack([sum_key, sum_val, sum_rec, sum_gate, sum_out]),
-        sum_fkey,
-        sum_frec,
-        sum_fval,
+        jnp.stack([*sum_key_val[-1], sum_gate_rec[-1][1], sum_gate_rec[-1][0], grad_out]),
+        jnp.concatenate(sum_fkey[-1], 1),
+        grad_frec,
+        jnp.concatenate(sum_fval[-1], 1),
         gdown,
         gup.T.reshape(maa_up.shape),
         gddown,

time: 1930 us -> 1630 us (0.84)
  waiting for transfers between devices: 1010 us -> 790 us
  starting transfers between devices: 189 us -> 111 us
  local copies, waits for them, and re-layouts: 70.8 us -> 97.9 us
  matrix products: 335 us -> 311 us
    ppermute x40 -> x39, waiting for transfers between devices: 310 us -> 193 us  [swap(): lax.ppermute(value, axis, [(i, i ^ bit) for i in range(lax.axis_size(axis...]
    ppermute x54 -> x23, waiting for transfers between devices: 108 us -> 187 us  [the longest x21 143 us: to_plane(): lax.ppermute(value, 'dp', [(i, (i + 2 * step) % n) for i in range(n)])]
    ppermute x54 -> x23, starting transfers between devices: 148 us -> 72.6 us  [the longest x21 67.4 us: to_plane(): lax.ppermute(value, 'dp', [(i, (i + 2 * step) % n) for i in range(n)])]
    all_gather x1, waiting for transfers between devices: 201 us -> 131 us  [local(): mix = lax.all_gather(mix_weights.astype(BF), BOTH, axis=1, tiled=True)]
    all_gather x3 -> x0, waiting for transfers between devices: 62.8 us -> none  [the longest x1 60.9 us: local(): small = lax.all_gather(small, BOTH, axis=0, tiled=True)]
    all_gather x1, waiting for transfers between devices: 108 us -> 56.4 us  [local(): fkey = lax.all_gather(ffn_key.astype(BF), BOTH, axis=0, tiled=True)]
    convert_element_type x20 -> x5, local copies, waits for them, and re-layouts: 30.8 us -> 8.65 us  [scatter_unit(): sends.append(swap(both[0].astype(kind), 'seq', 2))]
    dot_general x32 -> x25, matrix products: 117 us -> 104 us  [product_t(): return lax.dot_general(left, right, TN, preferred_element_type=F32)]
  transfers between devices with their start and end apart: 105 -> 70, of which waited for: 38 -> 34; matrix products, arithmetic and copies ran while one was open for 24% -> 27% of each run, Pallas kernels for 6% -> 8%
where the time goes in v2:
time: 1630 us; the launch traced here: 1610 us
  waiting for transfers between devices  790 us (48%)
  matrix products  311 us (19%)
  other arithmetic  152 us (9%)
  Pallas kernels  132 us (8%)
  starting transfers between devices  111 us (7%)
  local copies, waits for them, and re-layouts  97.9 us (6%)
  between operations  17.4 us (1%)
    ppermute x39, waiting for transfers between devices, swap(): lax.ppermute(value, axis, [(i, i ^ bit) for i in range(lax.axis_size(axis...  193 us
    all_gather x1, waiting for transfers between devices, local(): fval = lax.all_gather(ffn_value.astype(BF), BOTH, axis=0, tiled=True)  158 us
    ppermute x21, waiting for transfers between devices, to_plane(): lax.ppermute(value, 'dp', [(i, (i + 2 * step) % n) for i in range(n)])  143 us
    pallas_call x4, Pallas kernels, _call(): pl.pallas_call(kernel, grid=(width // LANES,), in_specs=[spec(kind) for k...  132 us
    all_gather x1, waiting for transfers between devices, local(): mix = lax.all_gather(mix_weights.astype(BF), BOTH, axis=1, tiled=True)  131 us
    dot_general x25, matrix products, product_t(): return lax.dot_general(left, right, TN, preferred_element_type=F32)  104 us
    dot_general x8, matrix products, product(): return jnp.dot(left, right, preferred_element_type=F32)  75.4 us
    dot_general x8, matrix products, back_product(): return lax.dot_general(grad, weight, NT, preferred_element_type=F32)  68.9 us
  transfers between devices with their start and end apart: 70, of which 34 were waited for; matrix products, arithmetic and copies ran while one was open for 27% of the time, Pallas kernels for 8%

profile of v2, /device:TPU:0, one launch (start us, length us, event | category | flops | bytes accessed | tf_op | source)
XLA Modules:
  0.0 1611.1 jit_solution(7372122239254519032)
XLA Ops:
  26.4 20.4 %collective-permute-done.1 = f32[64,464]{0,1:T(8,128)S(1)} collective-permute-done((f32[64,464]{0,1:T(8,128)S(1)}, f32[64,464]{0,1:T(8,128)S(1)}, u32[]{:S(2)}, u32[]{:S(2)}) %collective-permute-start.1) | collective-permute-done | bytes 118816 | tf_op jit(solution)/shard_map/ppermute | solution.py:457
  49.3 11.5 collective-permute-done.3
  68.0 36.2 %collective-permute-done.4 = f32[512,464]{0,1:T(8,128)} collective-permute-done((f32[512,464]{0,1:T(8,128)}, f32[512,464]{0,1:T(8,128)}, u32[]{:S(2)}, u32[]{:S(2)}) %collective-permute-start.4) | collective-permute-done | bytes 950304 | tf_op jit(solution)/shard_map/ppermute | solution.py:452
  151.6 131.0 %all-gather.5.cloned.1.call-done = bf16[5,2048,2048]{2,1,0:T(8,128)(2,1)} async-done(((bf16[5,64,2048]{2,1,0:T(8,128)(2,1)}), bf16[5,2048,2048]{2,1,0:T(8,128)(2,1)}) %all-gather.5.cloned.1.call-update) | async-done | bytes 41943056 | tf_op jit(solution)/shard_map/all_gather | solution.py:622
  282.6 5.8 fusion.4.k_ref
  288.5 6.7 fusion.6.v_ref
  295.2 14.0 shard_map.599
  309.7 7.1 fusion.2.q_ref
  320.7 7.9 fusion.8.gate_ref
  328.6 13.7 collective-permute-done.9
  342.4 50.9 %shard_map.600 = (f32[256,2048]{1,0:T(8,128)S(1)}, bf16[256,2048]{1,0:T(8,128)(2,1)S(1)}, f32[256,2048]{1,0:T(8,128)S(1)}, f32[256,2048]{1,0:T(8,128)}) custom-call(f32[4]{0:T(128)S(1)} %compare_convert_fusion.keep_ref, f32[256,2048]{1,0:T(8,128)} %fusion.2.q_ref, f32[256,2048]{1,0:T(8,128)} %copy-done.10, f32[256,2048]{1,0:T(8,128)} %copy-done.11, ...), custom_call_target="tpu_custom_call" | custom-call | flops 10485760000 | bytes 20971520 | tf_op jit(solution)/shard_map/pallas_call | solution.py:292
  393.2 7.5 fusion.252
  409.9 56.4 %all-gather.9.cloned.1.call-done = bf16[2048,7168]{1,0:T(8,128)(2,1)} async-done(((bf16[64,7168]{1,0:T(8,128)(2,1)}), bf16[2048,7168]{1,0:T(8,128)(2,1)}) %all-gather.9.cloned.1.call-update) | async-done | bytes 29360144 | tf_op jit(solution)/shard_map/all_gather | solution.py:623
  466.3 15.2 multiply_convert_fusion
  485.0 157.9 %all-gather.11.cloned.1.call-done = bf16[7168,2048]{1,0:T(8,128)(2,1)} async-done(((bf16[224,2048]{1,0:T(8,128)(2,1)}), bf16[7168,2048]{1,0:T(8,128)(2,1)}) %all-gather.11.cloned.1.call-update) | async-done | bytes 29360144 | tf_op jit(solution)/shard_map/all_gather | solution.py:624
  642.9 15.7 fusion.253
  658.5 63.4 %all-gather.7.cloned.1.call-done = bf16[2048,2048]{1,0:T(8,128)(2,1)} async-done(((bf16[64,2048]{1,0:T(8,128)(2,1)}), bf16[2048,2048]{1,0:T(8,128)(2,1)}) %all-gather.7.cloned.1.call-update) | async-done | bytes 8388624 | tf_op jit(solution)/shard_map/all_gather | solution.py:625
  721.9 9.6 fusion.36
  731.6 5.1 convolution_convert_fusion.2
  736.8 5.1 convolution_convert_fusion.3
  759.5 7.3 fusion.52
  766.8 17.5 %fusion = bf16[256,7168]{1,0:T(8,128)(2,1)} fusion(bf16[256,2048]{1,0:T(8,128)(2,1)} %copy-done.114, bf16[7168,2048]{1,0:T(8,128)(2,1)} %all-gather.11.cloned.1.call-done, f32[256,7168]{1,0:T(8,128)} %get-tuple-element.515), kind=kOutput, calls=%fused_computation.4 | convolution fusion | flops 7521697792 | bytes 41418752 | tf_op jit(solution)/shard_map/dot_general | solution.py:448
  784.4 8.4 add_convert_fusion.1
  804.2 12.7 fusion.254
  817.0 7.3 multiply_reduce_fusion.3
  831.7 5.2 convolution_convert_fusion.1
  843.5 35.2 %collective-permute-done.14 = bf16[2,4,224,1024]{3,2,1,0:T(8,128)(2,1)} collective-permute-done((bf16[2,4,224,1024]{3,2,1,0:T(8,128)(2,1)}, bf16[2,4,224,1024]{3,2,1,0:T(8,128)(2,1)}, u32[]{:S(2)}, u32[]{:S(2)}) %collective-permute-start.14) | collective-permute-done | bytes 3670048 | tf_op jit(solution)/shard_map/ppermute | solution.py:452
  878.7 6.2 collective-permute-done.13
  884.9 7.1 fusion.9.grad_ref
  892.0 24.3 %shard_map.601 = (f32[256,2048]{1,0:T(8,128)S(1)}, bf16[256,2048]{1,0:T(8,128)(2,1)S(1)}, f32[64,2048]{1,0:T(8,128)S(1)}, f32[2,2048]{1,0:T(2,128)S(1)}) custom-call(f32[4]{0:T(128)S(1)} %compare_convert_fusion.keep_ref, f32[256,2048]{1,0:T(8,128)S(1)} %copy-done, f32[256,2048]{1,0:T(8,128)} %get-tuple-element.510.ld_ref, f32[256,2048]{1,0:T(8,128)} %copy-done.1, ...), custom_call_target="tpu_custom_call" | custom-call | flops 2097152000 | bytes 20971520 | tf_op jit(solution)/shard_map/pallas_call | solution.py:292
  916.3 5.6 collective-permute-start.20
  930.4 9.1 add_convert_fusion.7
  954.4 30.0 %collective-permute-done.21 = f32[64,2048]{1,0:T(8,128)S(1)} collective-permute-done((f32[64,2048]{1,0:T(8,128)S(1)}, f32[64,2048]{1,0:T(8,128)S(1)}, u32[]{:S(2)}, u32[]{:S(2)}) %collective-permute-start.21) | collective-permute-done | bytes 524320 | tf_op jit(solution)/shard_map/ppermute | solution.py:435
  984.5 6.4 add_convert_fusion
  997.1 5.7 add_convert_fusion.6
  1015.2 42.9 %shard_map.602 = (bf16[256,2048]{1,0:T(8,128)(2,1)S(1)}, bf16[256,2048]{1,0:T(8,128)(2,1)S(1)}, bf16[256,2048]{1,0:T(8,128)(2,1)S(1)}, f32[256,2048]{1,0:T(8,128)S(1)}, f32[1,2048]{1,0:T(1,128)S(1)}) custom-call(f32[4]{0:T(128)S(1)} %compare_convert_fusion.keep_ref, f32[256,2048]{1,0:T(8,128)} %fusion.2.q_ref, f32[256,2048]{1,0:T(8,128)} %copy-done.10, ...), custom_call_target="tpu_custom_call" | custom-call | flops 15728640000 | bytes 20971520 | tf_op jit(solution)/shard_map/pallas_call | solution.py:292
  1061.4 5.9 fusion.7
  1069.9 7.9 collective-permute-done.26
  1077.8 6.0 collective-permute-done.25
  1083.8 6.1 convert_add_fusion
  1093.7 8.5 add_convert_fusion.5
  1120.0 6.1 fusion.1
  1128.0 5.7 fusion.3
  1133.8 6.5 fusion.5
  1159.6 10.2 multiply_reduce_fusion.10
  1206.4 7.7 collective-permute-start.31
  1216.6 8.6 fusion.32
  1236.5 39.0 %collective-permute-done.32 = bf16[2,64,3584]{2,1,0:T(8,128)(2,1)} collective-permute-done((bf16[2,64,3584]{2,1,0:T(8,128)(2,1)}, bf16[2,64,3584]{2,1,0:T(8,128)(2,1)}, u32[]{:S(2)}, u32[]{:S(2)}) %collective-permute-start.32) | collective-permute-done | bytes 917536 | tf_op jit(solution)/shard_map/ppermute | solution.py:457
  1289.6 5.9 multiply_add_fusion.7
  1297.2 10.8 collective-permute-done.38
  1308.0 5.2 collective-permute-done.37
  1323.9 18.3 %collective-permute-start.41 = (bf16[2,64,2048]{2,1,0:T(8,128)(2,1)S(1)}, bf16[2,64,2048]{2,1,0:T(8,128)(2,1)S(1)}, u32[]{:S(2)}, u32[]{:S(2)}) collective-permute-start(bf16[2,64,2048]{2,1,0:T(8,128)(2,1)S(1)} %get-tuple-element.460), channel_id=1, source_target_pairs={{0,2},{1,3},{2,4},{3,5},{4,6},{5,7},{6,0},{7,1},{8,10},{9,11},{10,... | collective-permute-start | bytes 1572872 | tf_op jit(solution)/shard_map/ppermute | solution.py:457
  1348.1 9.9 collective-permute-done.41
  1360.3 18.2 %collective-permute-done.42 = bf16[2,64,2048]{2,1,0:T(8,128)(2,1)S(1)} collective-permute-done((bf16[2,64,2048]{2,1,0:T(8,128)(2,1)S(1)}, bf16[2,64,2048]{2,1,0:T(8,128)(2,1)S(1)}, u32[]{:S(2)}, u32[]{:S(2)}) %collective-permute-start.42) | collective-permute-done | bytes 524320 | tf_op jit(solution)/shard_map/ppermute | solution.py:457
  1378.5 5.6 collective-permute-done.43
  1398.1 5.2 multiply_add_fusion.9
  1403.7 7.7 collective-permute-done.49
  1411.4 22.1 %collective-permute-done.48 = bf16[4,64,2048]{2,1,0:T(8,128)(2,1)} collective-permute-done((bf16[4,64,2048]{2,1,0:T(8,128)(2,1)}, bf16[4,64,2048]{2,1,0:T(8,128)(2,1)}, u32[]{:S(2)}, u32[]{:S(2)}) %collective-permute-start.48) | collective-permute-done | bytes 1048608 | tf_op jit(solution)/shard_map/ppermute | solution.py:452
  1454.0 6.1 collective-permute-start.52
  1460.1 38.5 %collective-permute-done.55 = f32[1,4,64,464]{3,2,1,0:T(8,128)S(1)} collective-permute-done((f32[1,4,64,464]{3,2,1,0:T(8,128)S(1)}, f32[1,4,64,464]{3,2,1,0:T(8,128)S(1)}, u32[]{:S(2)}, u32[]{:S(2)}) %collective-permute-start.55) | collective-permute-done | bytes 475168 | tf_op jit(solution)/shard_map/ppermute | solution.py:452
  1506.0 9.9 collective-permute-done.54
  1544.5 6.9 collective-permute-done.59
  1575.3 19.1 %collective-permute-done.64 = bf16[2,64,2048]{2,1,0:T(8,128)(2,1)} collective-permute-done((bf16[2,64,2048]{2,1,0:T(8,128)(2,1)}, bf16[2,64,2048]{2,1,0:T(8,128)(2,1)}, u32[]{:S(2)}, u32[]{:S(2)}) %collective-permute-start.64) | collective-permute-done | bytes 524320 | tf_op jit(solution)/shard_map/ppermute | solution.py:457
  1597.3 6.7 multiply_add_fusion
  (734 shorter events, 407.6 us)
Async XLA Ops:
  7.2 275.4 %all-gather.5.cloned.1.call-start = ((), (), s32[]{:S(2)}) async-start(), calls=%async_computation | async-start | bytes 43253760 | tf_op jit(solution)/shard_map/all_gather | solution.py:622
  10.3 456.0 %all-gather.9.cloned.1.call-start = ((), (), s32[]{:S(2)}) async-start(), calls=%async_computation.2 | async-start | bytes 30277632 | tf_op jit(solution)/shard_map/all_gather | solution.py:623
  13.0 629.8 %all-gather.11.cloned.1.call-start = ((), (), s32[]{:S(2)}) async-start(), calls=%async_computation.3 | async-start | bytes 30277632 | tf_op jit(solution)/shard_map/all_gather | solution.py:624
  14.2 707.8 %all-gather.7.cloned.1.call-start = ((), (), s32[]{:S(2)}) async-start(), calls=%async_computation.1 | async-start | bytes 8650752 | tf_op jit(solution)/shard_map/all_gather | solution.py:625
  17.6 29.1 %collective-permute-start.1 = (f32[64,464]{0,1:T(8,128)S(1)}, f32[64,464]{0,1:T(8,128)S(1)}, u32[]{:S(2)}, u32[]{:S(2)}) collective-permute-start(f32[64,464]{0,1:T(8,128)S(1)} %constant_dynamic-update-slice_fusion), channel_id=1, source_target_pairs={{0,4},{1,5},{2,6},{3,7},{4,0},{5,1},{6,2},{7,3},{8,12},{9,13},{10,... | collective-permute-start | bytes 356360 | tf_op jit(solution)/shard_map/ppermute | solution.py:457
  20.2 26.6 %collective-permute-start.2 = (f32[64,464]{0,1:T(8,128)S(1)}, f32[64,464]{0,1:T(8,128)S(1)}, u32[]{:S(2)}, u32[]{:S(2)}) collective-permute-start(f32[64,464]{0,1:T(8,128)S(1)} %constant_dynamic-update-slice_fusion), channel_id=1, source_target_pairs={{0,6},{1,7},{2,0},{3,1},{4,2},{5,3},{6,4},{7,5},{8,14},{9,15},{10,... | collective-permute-start | bytes 356360 | tf_op jit(solution)/shard_map/ppermute | solution.py:457
  47.1 13.7 collective-permute-start.3
  66.9 37.3 %collective-permute-start.4 = (f32[512,464]{0,1:T(8,128)}, f32[512,464]{0,1:T(8,128)}, u32[]{:S(2)}, u32[]{:S(2)}) collective-permute-start(f32[512,464]{0,1:T(8,128)} %copy.254), channel_id=1, source_target_pairs={{0,16},{8,24},{16,0},{24,8},{1,17},{9,25},{17,1},{25,9},{2,18},{10... | collective-permute-start | bytes 2850824 | tf_op jit(solution)/shard_map/ppermute | solution.py:452
  67.2 37.0 %collective-permute-start.5 = (f32[512,464]{0,1:T(8,128)}, f32[512,464]{0,1:T(8,128)}, u32[]{:S(2)}, u32[]{:S(2)}) collective-permute-start(f32[512,464]{0,1:T(8,128)} %copy.254), channel_id=1, source_target_pairs={{0,8},{8,0},{16,24},{24,16},{1,9},{9,1},{17,25},{25,17},{2,10},{10... | collective-permute-start | bytes 2850824 | tf_op jit(solution)/shard_map/ppermute | solution.py:452
  316.9 25.4 %collective-permute-start.9 = (f32[64,2048]{1,0:T(8,128)S(1)}, f32[64,2048]{1,0:T(8,128)S(1)}, u32[]{:S(2)}, u32[]{:S(2)}) collective-permute-start(f32[64,2048]{1,0:T(8,128)S(1)} %add_select_fusion.3), channel_id=1, source_target_pairs={{0,16},{8,24},{1,17},{9,25},{2,18},{10,26},{3,19},{11,27},{4,20},{... | collective-permute-start | bytes 1572872 | tf_op jit(solution)/shard_map/ppermute | solution.py:435
  741.8 42.5 %collective-permute-start.12 = (bf16[3584,1024]{1,0:T(8,128)(2,1)}, bf16[3584,1024]{1,0:T(8,128)(2,1)}, u32[]{:S(2)}, u32[]{:S(2)}) collective-permute-start(bf16[3584,1024]{1,0:T(8,128)(2,1)} %convolution_convert_fusion.2), channel_id=1, source_target_pairs={{0,8},{8,0},{16,24},{24,16},{1,9},{9,1},{17,25},{25,17},{2,10},{10... | collective-permute-start | bytes 22020104 | tf_op jit(solution)/shard_map/ppermute | solution.py:452
  742.1 42.3 %collective-permute-start.11 = (bf16[3584,1024]{1,0:T(8,128)(2,1)}, bf16[3584,1024]{1,0:T(8,128)(2,1)}, u32[]{:S(2)}, u32[]{:S(2)}) collective-permute-start(bf16[3584,1024]{1,0:T(8,128)(2,1)} %convolution_convert_fusion.3), channel_id=1, source_target_pairs={{0,8},{8,0},{16,24},{24,16},{1,9},{9,1},{17,25},{25,17},{2,10},{10... | collective-permute-start | bytes 22020104 | tf_op jit(solution)/shard_map/ppermute | solution.py:452
  796.9 81.8 %collective-permute-start.14 = (bf16[2,4,224,1024]{3,2,1,0:T(8,128)(2,1)}, bf16[2,4,224,1024]{3,2,1,0:T(8,128)(2,1)}, u32[]{:S(2)}, u32[]{:S(2)}) collective-permute-start(bf16[2,4,224,1024]{3,2,1,0:T(8,128)(2,1)} %dynamic-slice_bitcast_fusion.1), channel_id=1, source_target_pairs={{0,1},{1,0},{2,3},{3,2},{4,5},{5,4},{6,7},{7,6},{8,9},{9,8},{10,11... | collective-permute-start | bytes 11010056 | tf_op jit(solution)/shard_map/ppermute | solution.py:452
  803.3 81.5 %collective-permute-start.13 = (bf16[1792,1024]{1,0:T(8,128)(2,1)}, bf16[1792,1024]{1,0:T(8,128)(2,1)}, u32[]{:S(2)}, u32[]{:S(2)}) collective-permute-start(bf16[1792,1024]{1,0:T(8,128)(2,1)} %add_convert_fusion.8), channel_id=1, source_target_pairs={{0,16},{8,24},{16,0},{24,8},{1,17},{9,25},{17,1},{25,9},{2,18},{10... | collective-permute-start | bytes 11010056 | tf_op jit(solution)/shard_map/ppermute | solution.py:452
  824.2 13.0 collective-permute-start.15
  830.6 153.9 %collective-permute-start.19 = (bf16[1024,3584]{1,0:T(8,128)(2,1)}, bf16[1024,3584]{1,0:T(8,128)(2,1)}, u32[]{:S(2)}, u32[]{:S(2)}) collective-permute-start(bf16[1024,3584]{1,0:T(8,128)(2,1)} %convolution_convert_fusion), channel_id=1, source_target_pairs={{0,8},{8,0},{16,24},{24,16},{1,9},{9,1},{17,25},{25,17},{2,10},{10... | collective-permute-start | bytes 22020104 | tf_op jit(solution)/shard_map/ppermute | solution.py:452
  836.9 147.6 %collective-permute-start.18 = (bf16[1024,3584]{1,0:T(8,128)(2,1)}, bf16[1024,3584]{1,0:T(8,128)(2,1)}, u32[]{:S(2)}, u32[]{:S(2)}) collective-permute-start(bf16[1024,3584]{1,0:T(8,128)(2,1)} %convolution_convert_fusion.1), channel_id=1, source_target_pairs={{0,8},{8,0},{16,24},{24,16},{1,9},{9,1},{17,25},{25,17},{2,10},{10... | collective-permute-start | bytes 22020104 | tf_op jit(solution)/shard_map/ppermute | solution.py:452
  916.3 28.9 %collective-permute-start.20 = (f32[65,2048]{1,0:T(8,128)S(1)}, f32[65,2048]{1,0:T(8,128)S(1)}, u32[]{:S(2)}, u32[]{:S(2)}) collective-permute-start(f32[65,2048]{1,0:T(8,128)S(1)} %pad_maximum_fusion.10), channel_id=1, source_target_pairs={{0,8},{8,0},{16,24},{24,16},{1,9},{9,1},{17,25},{25,17},{2,10},{10... | collective-permute-start | bytes 1597448 | tf_op jit(solution)/shard_map/ppermute | solution.py:452
  930.4 54.0 %collective-permute-start.17 = (bf16[4,224,1024]{2,1,0:T(8,128)(2,1)}, bf16[4,224,1024]{2,1,0:T(8,128)(2,1)S(1)}, u32[]{:S(2)}, u32[]{:S(2)}) collective-permute-start(bf16[4,224,1024]{2,1,0:T(8,128)(2,1)} %fusion.48), channel_id=1, source_target_pairs={{0,16},{8,24},{16,0},{24,8},{1,17},{9,25},{17,1},{25,9},{2,18},{10... | collective-permute-start | bytes 5505032 | tf_op jit(solution)/shard_map/ppermute | solution.py:452
  941.1 43.3 %collective-permute-start.16 = (bf16[1,4,224,1024]{3,2,1,0:T(8,128)(2,1)S(1)}, bf16[1,4,224,1024]{3,2,1,0:T(8,128)(2,1)S(1)}, u32[]{:S(2)}, u32[]{:S(2)}) collective-permute-start(bf16[1,4,224,1024]{3,2,1,0:T(8,128)(2,1)S(1)} %dynamic-slice_bitcast_fusion.6), channel_id=1, source_target_pairs={{0,1},{1,0},{2,3},{3,2},{4,5},{5,4},{6,7},{7,6},{8,9},{9,8},{10,11... | collective-permute-start | bytes 5505032 | tf_op jit(solution)/shard_map/ppermute | solution.py:452
  945.3 39.0 %collective-permute-start.21 = (f32[64,2048]{1,0:T(8,128)S(1)}, f32[64,2048]{1,0:T(8,128)S(1)}, u32[]{:S(2)}, u32[]{:S(2)}) collective-permute-start(f32[64,2048]{1,0:T(8,128)S(1)} %add_select_fusion.1), channel_id=1, source_target_pairs={{16,0},{24,8},{17,1},{25,9},{18,2},{26,10},{19,3},{27,11},{20,4},{... | collective-permute-start | bytes 1572872 | tf_op jit(solution)/shard_map/ppermute | solution.py:435
  996.4 81.4 %collective-permute-start.26 = (bf16[2,4,64,3584]{3,2,1,0:T(8,128)(2,1)}, bf16[2,4,64,3584]{3,2,1,0:T(8,128)(2,1)}, u32[]{:S(2)}, u32[]{:S(2)}) collective-permute-start(bf16[2,4,64,3584]{3,2,1,0:T(8,128)(2,1)} %dynamic-slice_bitcast_fusion), channel_id=1, source_target_pairs={{0,1},{1,0},{2,3},{3,2},{4,5},{5,4},{6,7},{7,6},{8,9},{9,8},{10,11... | collective-permute-start | bytes 11010056 | tf_op jit(solution)/shard_map/ppermute | solution.py:452
  1002.8 81.0 %collective-permute-start.25 = (bf16[512,3584]{1,0:T(8,128)(2,1)}, bf16[512,3584]{1,0:T(8,128)(2,1)}, u32[]{:S(2)}, u32[]{:S(2)}) collective-permute-start(bf16[512,3584]{1,0:T(8,128)(2,1)} %add_convert_fusion.6), channel_id=1, source_target_pairs={{0,16},{8,24},{16,0},{24,8},{1,17},{9,25},{17,1},{25,9},{2,18},{10... | collective-permute-start | bytes 11010056 | tf_op jit(solution)/shard_map/ppermute | solution.py:452
  1006.7 60.6 %collective-permute-start.22 = (bf16[2,224,1024]{2,1,0:T(8,128)(2,1)}, bf16[2,224,1024]{2,1,0:T(8,128)(2,1)S(1)}, u32[]{:S(2)}, u32[]{:S(2)}) collective-permute-start(bf16[2,224,1024]{2,1,0:T(8,128)(2,1)} %get-tuple-element.442), channel_id=1, source_target_pairs={{0,2},{1,3},{2,4},{3,5},{4,6},{5,7},{6,0},{7,1},{8,10},{9,11},{10,... | collective-permute-start | bytes 2752520 | tf_op jit(solution)/shard_map/ppermute | solution.py:457
  1008.2 61.6 %collective-permute-start.23 = (bf16[2,224,1024]{2,1,0:T(8,128)(2,1)S(1)}, bf16[2,224,1024]{2,1,0:T(8,128)(2,1)S(1)}, u32[]{:S(2)}, u32[]{:S(2)}) collective-permute-start(bf16[2,224,1024]{2,1,0:T(8,128)(2,1)S(1)} %get-tuple-element.443), channel_id=1, source_target_pairs={{0,4},{1,5},{2,6},{3,7},{4,0},{5,1},{6,2},{7,3},{8,12},{9,13},{10,... | collective-permute-start | bytes 2752520 | tf_op jit(solution)/shard_map/ppermute | solution.py:457
  1009.2 60.7 %collective-permute-start.24 = (bf16[2,224,1024]{2,1,0:T(8,128)(2,1)S(1)}, bf16[2,224,1024]{2,1,0:T(8,128)(2,1)S(1)}, u32[]{:S(2)}, u32[]{:S(2)}) collective-permute-start(bf16[2,224,1024]{2,1,0:T(8,128)(2,1)S(1)} %get-tuple-element.441), channel_id=1, source_target_pairs={{0,6},{1,7},{2,0},{3,1},{4,2},{5,3},{6,4},{7,5},{8,14},{9,15},{10,... | collective-permute-start | bytes 2752520 | tf_op jit(solution)/shard_map/ppermute | solution.py:457
  1067.4 73.0 %collective-permute-start.29 = (bf16[1024,2048]{1,0:T(8,128)(2,1)}, bf16[1024,2048]{1,0:T(8,128)(2,1)}, u32[]{:S(2)}, u32[]{:S(2)}) collective-permute-start(bf16[1024,2048]{1,0:T(8,128)(2,1)} %convolution_convert_fusion.9), channel_id=1, source_target_pairs={{0,8},{8,0},{16,24},{24,16},{1,9},{9,1},{17,25},{25,17},{2,10},{10... | collective-permute-start | bytes 12582920 | tf_op jit(solution)/shard_map/ppermute | solution.py:452
  1069.9 70.5 %collective-permute-start.30 = (bf16[1024,2048]{1,0:T(8,128)(2,1)}, bf16[1024,2048]{1,0:T(8,128)(2,1)}, u32[]{:S(2)}, u32[]{:S(2)}) collective-permute-start(bf16[1024,2048]{1,0:T(8,128)(2,1)} %convolution_convert_fusion.8), channel_id=1, source_target_pairs={{0,8},{8,0},{16,24},{24,16},{1,9},{9,1},{17,25},{25,17},{2,10},{10... | collective-permute-start | bytes 12582920 | tf_op jit(solution)/shard_map/ppermute | solution.py:452
  1093.4 47.0 %collective-permute-start.28 = (bf16[4,64,3584]{2,1,0:T(8,128)(2,1)}, bf16[4,64,3584]{2,1,0:T(8,128)(2,1)}, u32[]{:S(2)}, u32[]{:S(2)}) collective-permute-start(bf16[4,64,3584]{2,1,0:T(8,128)(2,1)} %fusion.50), channel_id=1, source_target_pairs={{0,16},{8,24},{16,0},{24,8},{1,17},{9,25},{17,1},{25,9},{2,18},{10... | collective-permute-start | bytes 5505032 | tf_op jit(solution)/shard_map/ppermute | solution.py:452
  1105.0 40.4 %collective-permute-start.27 = (bf16[1,4,64,3584]{3,2,1,0:T(8,128)(2,1)}, bf16[1,4,64,3584]{3,2,1,0:T(8,128)(2,1)S(1)}, u32[]{:S(2)}, u32[]{:S(2)}) collective-permute-start(bf16[1,4,64,3584]{3,2,1,0:T(8,128)(2,1)} %dynamic-slice_bitcast_fusion.5), channel_id=1, source_target_pairs={{0,1},{1,0},{2,3},{3,2},{4,5},{5,4},{6,7},{7,6},{8,9},{9,8},{10,11... | collective-permute-start | bytes 5505032 | tf_op jit(solution)/shard_map/ppermute | solution.py:452
  1185.4 30.1 %collective-permute-start.36 = (f32[1,2048]{1,0:T(1,128)S(1)}, f32[1,2048]{1,0:T(1,128)S(1)}, u32[]{:S(2)}, u32[]{:S(2)}) collective-permute-start(f32[1,2048]{1,0:T(1,128)S(1)} %split.61), channel_id=1, source_target_pairs={{8,0},{16,8},{24,16},{9,1},{17,9},{25,17},{10,2},{18,10},{26,18},{... | collective-permute-start | bytes 24584 | tf_op jit(solution)/shard_map/ppermute | solution.py:414
  1193.1 84.8 %collective-permute-start.35 = (bf16[2,4,64,2048]{3,2,1,0:T(8,128)(2,1)}, bf16[2,4,64,2048]{3,2,1,0:T(8,128)(2,1)}, u32[]{:S(2)}, u32[]{:S(2)}) collective-permute-start(bf16[2,4,64,2048]{3,2,1,0:T(8,128)(2,1)} %dynamic-slice_bitcast_fusion.4), channel_id=1, source_target_pairs={{0,1},{1,0},{2,3},{3,2},{4,5},{5,4},{6,7},{7,6},{8,9},{9,8},{10,11... | collective-permute-start | bytes 6291464 | tf_op jit(solution)/shard_map/ppermute | solution.py:452
  1198.6 79.3 %collective-permute-start.34 = (bf16[512,2048]{1,0:T(8,128)(2,1)}, bf16[512,2048]{1,0:T(8,128)(2,1)}, u32[]{:S(2)}, u32[]{:S(2)}) collective-permute-start(bf16[512,2048]{1,0:T(8,128)(2,1)} %add_convert_fusion.14), channel_id=1, source_target_pairs={{0,16},{8,24},{16,0},{24,8},{1,17},{9,25},{17,1},{25,9},{2,18},{10... | collective-permute-start | bytes 6291464 | tf_op jit(solution)/shard_map/ppermute | solution.py:452
  1206.4 30.1 %collective-permute-start.31 = (bf16[2,64,3584]{2,1,0:T(8,128)(2,1)}, bf16[2,64,3584]{2,1,0:T(8,128)(2,1)}, u32[]{:S(2)}, u32[]{:S(2)}) collective-permute-start(bf16[2,64,3584]{2,1,0:T(8,128)(2,1)} %get-tuple-element.439), channel_id=1, source_target_pairs={{0,2},{1,3},{2,4},{3,5},{4,6},{5,7},{6,0},{7,1},{8,10},{9,11},{10,... | collective-permute-start | bytes 2752520 | tf_op jit(solution)/shard_map/ppermute | solution.py:457
  1214.0 61.5 %collective-permute-start.32 = (bf16[2,64,3584]{2,1,0:T(8,128)(2,1)}, bf16[2,64,3584]{2,1,0:T(8,128)(2,1)}, u32[]{:S(2)}, u32[]{:S(2)}) collective-permute-start(bf16[2,64,3584]{2,1,0:T(8,128)(2,1)} %get-tuple-element.440), channel_id=1, source_target_pairs={{0,4},{1,5},{2,6},{3,7},{4,0},{5,1},{6,2},{7,3},{8,12},{9,13},{10,... | collective-permute-start | bytes 2752520 | tf_op jit(solution)/shard_map/ppermute | solution.py:457
  1215.5 62.4 %collective-permute-start.33 = (bf16[2,64,3584]{2,1,0:T(8,128)(2,1)}, bf16[2,64,3584]{2,1,0:T(8,128)(2,1)}, u32[]{:S(2)}, u32[]{:S(2)}) collective-permute-start(bf16[2,64,3584]{2,1,0:T(8,128)(2,1)} %get-tuple-element.438), channel_id=1, source_target_pairs={{0,6},{1,7},{2,0},{3,1},{4,2},{5,3},{6,4},{7,5},{8,14},{9,15},{10,... | collective-permute-start | bytes 2752520 | tf_op jit(solution)/shard_map/ppermute | solution.py:457
  1236.5 60.7 %collective-permute-start.39 = (bf16[1024,2048]{1,0:T(8,128)(2,1)S(1)}, bf16[1024,2048]{1,0:T(8,128)(2,1)S(1)}, u32[]{:S(2)}, u32[]{:S(2)}) collective-permute-start(bf16[1024,2048]{1,0:T(8,128)(2,1)S(1)} %copy-done.70), channel_id=1, source_target_pairs={{0,8},{8,0},{16,24},{24,16},{1,9},{9,1},{17,25},{25,17},{2,10},{10... | collective-permute-start | bytes 12582920 | tf_op jit(solution)/shard_map/ppermute | solution.py:452
  1275.6 21.6 %collective-permute-start.40 = (bf16[1024,2048]{1,0:T(8,128)(2,1)}, bf16[1024,2048]{1,0:T(8,128)(2,1)}, u32[]{:S(2)}, u32[]{:S(2)}) collective-permute-start(bf16[1024,2048]{1,0:T(8,128)(2,1)} %convolution_convert_fusion.6), channel_id=1, source_target_pairs={{0,8},{8,0},{16,24},{24,16},{1,9},{9,1},{17,25},{25,17},{2,10},{10... | collective-permute-start | bytes 12582920 | tf_op jit(solution)/shard_map/ppermute | solution.py:452
  1282.1 25.9 %collective-permute-start.38 = (bf16[4,64,2048]{2,1,0:T(8,128)(2,1)}, bf16[4,64,2048]{2,1,0:T(8,128)(2,1)}, u32[]{:S(2)}, u32[]{:S(2)}) collective-permute-start(bf16[4,64,2048]{2,1,0:T(8,128)(2,1)} %fusion.74), channel_id=1, source_target_pairs={{0,16},{8,24},{16,0},{24,8},{1,17},{9,25},{17,1},{25,9},{2,18},{10... | collective-permute-start | bytes 3145736 | tf_op jit(solution)/shard_map/ppermute | solution.py:452
  1287.6 25.6 %collective-permute-start.37 = (bf16[1,4,64,2048]{3,2,1,0:T(8,128)(2,1)}, bf16[1,4,64,2048]{3,2,1,0:T(8,128)(2,1)}, u32[]{:S(2)}, u32[]{:S(2)}) collective-permute-start(bf16[1,4,64,2048]{3,2,1,0:T(8,128)(2,1)} %dynamic-slice_bitcast_fusion.9), channel_id=1, source_target_pairs={{0,1},{1,0},{2,3},{3,2},{4,5},{5,4},{6,7},{7,6},{8,9},{9,8},{10,11... | collective-permute-start | bytes 3145736 | tf_op jit(solution)/shard_map/ppermute | solution.py:452
  1297.0 87.1 %collective-permute-start.46 = (f32[1024,464]{0,1:T(8,128)}, f32[1024,464]{0,1:T(8,128)}, u32[]{:S(2)}, u32[]{:S(2)}) collective-permute-start(f32[1024,464]{0,1:T(8,128)} %pad_maximum_fusion.3), channel_id=1, source_target_pairs={{0,8},{8,0},{16,24},{24,16},{1,9},{9,1},{17,25},{25,17},{2,10},{10... | collective-permute-start | bytes 5701640 | tf_op jit(solution)/shard_map/ppermute | solution.py:452
  1317.0 67.2 %collective-permute-start.45 = (bf16[2,4,64,2048]{3,2,1,0:T(8,128)(2,1)S(1)}, bf16[2,4,64,2048]{3,2,1,0:T(8,128)(2,1)}, u32[]{:S(2)}, u32[]{:S(2)}) collective-permute-start(bf16[2,4,64,2048]{3,2,1,0:T(8,128)(2,1)S(1)} %dynamic-slice_bitcast_fusion.3), channel_id=1, source_target_pairs={{0,1},{1,0},{2,3},{3,2},{4,5},{5,4},{6,7},{7,6},{8,9},{9,8},{10,11... | collective-permute-start | bytes 6291464 | tf_op jit(solution)/shard_map/ppermute | solution.py:452
  1319.5 64.6 %collective-permute-start.44 = (bf16[512,2048]{1,0:T(8,128)(2,1)S(1)}, bf16[512,2048]{1,0:T(8,128)(2,1)S(1)}, u32[]{:S(2)}, u32[]{:S(2)}) collective-permute-start(bf16[512,2048]{1,0:T(8,128)(2,1)S(1)} %add_convert_fusion.12), channel_id=1, source_target_pairs={{0,16},{8,24},{16,0},{24,8},{1,17},{9,25},{17,1},{25,9},{2,18},{10... | collective-permute-start | bytes 6291464 | tf_op jit(solution)/shard_map/ppermute | solution.py:452
  1323.9 34.0 %collective-permute-start.41 = (bf16[2,64,2048]{2,1,0:T(8,128)(2,1)S(1)}, bf16[2,64,2048]{2,1,0:T(8,128)(2,1)S(1)}, u32[]{:S(2)}, u32[]{:S(2)}) collective-permute-start(bf16[2,64,2048]{2,1,0:T(8,128)(2,1)S(1)} %get-tuple-element.460), channel_id=1, source_target_pairs={{0,2},{1,3},{2,4},{3,5},{4,6},{5,7},{6,0},{7,1},{8,10},{9,11},{10,... | collective-permute-start | bytes 1572872 | tf_op jit(solution)/shard_map/ppermute | solution.py:457
  1344.6 33.9 %collective-permute-start.42 = (bf16[2,64,2048]{2,1,0:T(8,128)(2,1)S(1)}, bf16[2,64,2048]{2,1,0:T(8,128)(2,1)S(1)}, u32[]{:S(2)}, u32[]{:S(2)}) collective-permute-start(bf16[2,64,2048]{2,1,0:T(8,128)(2,1)S(1)} %get-tuple-element.461), channel_id=1, source_target_pairs={{0,4},{1,5},{2,6},{3,7},{4,0},{5,1},{6,2},{7,3},{8,12},{9,13},{10,... | collective-permute-start | bytes 1572872 | tf_op jit(solution)/shard_map/ppermute | solution.py:457
  1358.0 26.1 %collective-permute-start.43 = (bf16[2,64,2048]{2,1,0:T(8,128)(2,1)S(1)}, bf16[2,64,2048]{2,1,0:T(8,128)(2,1)S(1)}, u32[]{:S(2)}, u32[]{:S(2)}) collective-permute-start(bf16[2,64,2048]{2,1,0:T(8,128)(2,1)S(1)} %get-tuple-element.459), channel_id=1, source_target_pairs={{0,6},{1,7},{2,0},{3,1},{4,2},{5,3},{6,4},{7,5},{8,14},{9,15},{10,... | collective-permute-start | bytes 1572872 | tf_op jit(solution)/shard_map/ppermute | solution.py:457
  1378.5 25.1 %collective-permute-start.51 = (bf16[1024,2048]{1,0:T(8,128)(2,1)S(1)}, bf16[1024,2048]{1,0:T(8,128)(2,1)}, u32[]{:S(2)}, u32[]{:S(2)}) collective-permute-start(bf16[1024,2048]{1,0:T(8,128)(2,1)S(1)} %copy-done.69), channel_id=1, source_target_pairs={{0,8},{8,0},{16,24},{24,16},{1,9},{9,1},{17,25},{25,17},{2,10},{10... | collective-permute-start | bytes 12582920 | tf_op jit(solution)/shard_map/ppermute | solution.py:452
  1384.1 19.6 %collective-permute-start.50 = (bf16[1024,2048]{1,0:T(8,128)(2,1)S(1)}, bf16[1024,2048]{1,0:T(8,128)(2,1)}, u32[]{:S(2)}, u32[]{:S(2)}) collective-permute-start(bf16[1024,2048]{1,0:T(8,128)(2,1)S(1)} %copy-done.68), channel_id=1, source_target_pairs={{0,8},{8,0},{16,24},{24,16},{1,9},{9,1},{17,25},{25,17},{2,10},{10... | collective-permute-start | bytes 12582920 | tf_op jit(solution)/shard_map/ppermute | solution.py:452
  1387.2 24.2 %collective-permute-start.49 = (f32[512,464]{0,1:T(8,128)}, f32[512,464]{0,1:T(8,128)}, u32[]{:S(2)}, u32[]{:S(2)}) collective-permute-start(f32[512,464]{0,1:T(8,128)} %slice_add_fusion), channel_id=1, source_target_pairs={{0,16},{8,24},{16,0},{24,8},{1,17},{9,25},{17,1},{25,9},{2,18},{10... | collective-permute-start | bytes 2850824 | tf_op jit(solution)/shard_map/ppermute | solution.py:452
  1392.0 41.4 %collective-permute-start.48 = (bf16[4,64,2048]{2,1,0:T(8,128)(2,1)}, bf16[4,64,2048]{2,1,0:T(8,128)(2,1)}, u32[]{:S(2)}, u32[]{:S(2)}) collective-permute-start(bf16[4,64,2048]{2,1,0:T(8,128)(2,1)} %fusion.76), channel_id=1, source_target_pairs={{0,16},{8,24},{16,0},{24,8},{1,17},{9,25},{17,1},{25,9},{2,18},{10... | collective-permute-start | bytes 3145736 | tf_op jit(solution)/shard_map/ppermute | solution.py:452
  1396.0 37.4 %collective-permute-start.47 = (bf16[1,4,64,2048]{3,2,1,0:T(8,128)(2,1)S(1)}, bf16[1,4,64,2048]{3,2,1,0:T(8,128)(2,1)S(1)}, u32[]{:S(2)}, u32[]{:S(2)}) collective-permute-start(bf16[1,4,64,2048]{3,2,1,0:T(8,128)(2,1)S(1)} %dynamic-slice_bitcast_fusion.8), channel_id=1, source_target_pairs={{0,1},{1,0},{2,3},{3,2},{4,5},{5,4},{6,7},{7,6},{8,9},{9,8},{10,11... | collective-permute-start | bytes 3145736 | tf_op jit(solution)/shard_map/ppermute | solution.py:452
  1439.9 76.0 %collective-permute-start.57 = (bf16[2,4,64,2048]{3,2,1,0:T(8,128)(2,1)}, bf16[2,4,64,2048]{3,2,1,0:T(8,128)(2,1)}, u32[]{:S(2)}, u32[]{:S(2)}) collective-permute-start(bf16[2,4,64,2048]{3,2,1,0:T(8,128)(2,1)} %dynamic-slice_bitcast_fusion.2), channel_id=1, source_target_pairs={{0,1},{1,0},{2,3},{3,2},{4,5},{5,4},{6,7},{7,6},{8,9},{9,8},{10,11... | collective-permute-start | bytes 6291464 | tf_op jit(solution)/shard_map/ppermute | solution.py:452
  1444.8 71.1 %collective-permute-start.56 = (bf16[512,2048]{1,0:T(8,128)(2,1)}, bf16[512,2048]{1,0:T(8,128)(2,1)}, u32[]{:S(2)}, u32[]{:S(2)}) collective-permute-start(bf16[512,2048]{1,0:T(8,128)(2,1)} %add_convert_fusion.10), channel_id=1, source_target_pairs={{0,16},{8,24},{16,0},{24,8},{1,17},{9,25},{17,1},{25,9},{2,18},{10... | collective-permute-start | bytes 6291464 | tf_op jit(solution)/shard_map/ppermute | solution.py:452
  1449.2 49.4 %collective-permute-start.55 = (f32[1,4,64,464]{3,2,1,0:T(8,128)S(1)}, f32[1,4,64,464]{3,2,1,0:T(8,128)S(1)}, u32[]{:S(2)}, u32[]{:S(2)}) collective-permute-start(f32[1,4,64,464]{3,2,1,0:T(8,128)S(1)} %get-tuple-element.472), channel_id=1, source_target_pairs={{0,1},{1,0},{2,3},{3,2},{4,5},{5,4},{6,7},{7,6},{8,9},{9,8},{10,11... | collective-permute-start | bytes 1425416 | tf_op jit(solution)/shard_map/ppermute | solution.py:452
  1454.0 52.0 %collective-permute-start.52 = (bf16[2,64,2048]{2,1,0:T(8,128)(2,1)}, bf16[2,64,2048]{2,1,0:T(8,128)(2,1)}, u32[]{:S(2)}, u32[]{:S(2)}) collective-permute-start(bf16[2,64,2048]{2,1,0:T(8,128)(2,1)} %get-tuple-element.457), channel_id=1, source_target_pairs={{0,2},{1,3},{2,4},{3,5},{4,6},{5,7},{6,0},{7,1},{8,10},{9,11},{10,... | collective-permute-start | bytes 1572872 | tf_op jit(solution)/shard_map/ppermute | solution.py:457
  1460.1 45.9 %collective-permute-start.53 = (bf16[2,64,2048]{2,1,0:T(8,128)(2,1)}, bf16[2,64,2048]{2,1,0:T(8,128)(2,1)}, u32[]{:S(2)}, u32[]{:S(2)}) collective-permute-start(bf16[2,64,2048]{2,1,0:T(8,128)(2,1)} %get-tuple-element.458), channel_id=1, source_target_pairs={{0,4},{1,5},{2,6},{3,7},{4,0},{5,1},{6,2},{7,3},{8,12},{9,13},{10,... | collective-permute-start | bytes 1572872 | tf_op jit(solution)/shard_map/ppermute | solution.py:457
  1498.6 17.3 %collective-permute-start.54 = (bf16[2,64,2048]{2,1,0:T(8,128)(2,1)}, bf16[2,64,2048]{2,1,0:T(8,128)(2,1)}, u32[]{:S(2)}, u32[]{:S(2)}) collective-permute-start(bf16[2,64,2048]{2,1,0:T(8,128)(2,1)} %get-tuple-element.456), channel_id=1, source_target_pairs={{0,6},{1,7},{2,0},{3,1},{4,2},{5,3},{6,4},{7,5},{8,14},{9,15},{10,... | collective-permute-start | bytes 1572872 | tf_op jit(solution)/shard_map/ppermute | solution.py:457
  1522.2 29.2 %collective-permute-start.62 = (bf16[4,64,2048]{2,1,0:T(8,128)(2,1)}, bf16[4,64,2048]{2,1,0:T(8,128)(2,1)}, u32[]{:S(2)}, u32[]{:S(2)}) collective-permute-start(bf16[4,64,2048]{2,1,0:T(8,128)(2,1)} %fusion.78), channel_id=1, source_target_pairs={{0,16},{8,24},{16,0},{24,8},{1,17},{9,25},{17,1},{25,9},{2,18},{10... | collective-permute-start | bytes 3145736 | tf_op jit(solution)/shard_map/ppermute | solution.py:452
  1529.0 23.3 %collective-permute-start.61 = (bf16[1,4,64,2048]{3,2,1,0:T(8,128)(2,1)}, bf16[1,4,64,2048]{3,2,1,0:T(8,128)(2,1)}, u32[]{:S(2)}, u32[]{:S(2)}) collective-permute-start(bf16[1,4,64,2048]{3,2,1,0:T(8,128)(2,1)} %dynamic-slice_bitcast_fusion.7), channel_id=1, source_target_pairs={{0,1},{1,0},{2,3},{3,2},{4,5},{5,4},{6,7},{7,6},{8,9},{9,8},{10,11... | collective-permute-start | bytes 3145736 | tf_op jit(solution)/shard_map/ppermute | solution.py:452
  1535.7 15.7 collective-permute-start.59
  1536.1 15.3 collective-permute-start.60
  1556.7 18.6 %collective-permute-start.63 = (bf16[2,64,2048]{2,1,0:T(8,128)(2,1)}, bf16[2,64,2048]{2,1,0:T(8,128)(2,1)}, u32[]{:S(2)}, u32[]{:S(2)}) collective-permute-start(bf16[2,64,2048]{2,1,0:T(8,128)(2,1)} %get-tuple-element.454), channel_id=1, source_target_pairs={{0,2},{1,3},{2,4},{3,5},{4,6},{5,7},{6,0},{7,1},{8,10},{9,11},{10,... | collective-permute-start | bytes 1572872 | tf_op jit(solution)/shard_map/ppermute | solution.py:457
  1561.5 32.9 %collective-permute-start.64 = (bf16[2,64,2048]{2,1,0:T(8,128)(2,1)}, bf16[2,64,2048]{2,1,0:T(8,128)(2,1)}, u32[]{:S(2)}, u32[]{:S(2)}) collective-permute-start(bf16[2,64,2048]{2,1,0:T(8,128)(2,1)} %get-tuple-element.455), channel_id=1, source_target_pairs={{0,4},{1,5},{2,6},{3,7},{4,0},{5,1},{6,2},{7,3},{8,12},{9,13},{10,... | collective-permute-start | bytes 1572872 | tf_op jit(solution)/shard_map/ppermute | solution.py:457
  1561.7 34.0 %collective-permute-start.65 = (bf16[2,64,2048]{2,1,0:T(8,128)(2,1)}, bf16[2,64,2048]{2,1,0:T(8,128)(2,1)}, u32[]{:S(2)}, u32[]{:S(2)}) collective-permute-start(bf16[2,64,2048]{2,1,0:T(8,128)(2,1)} %get-tuple-element.453), channel_id=1, source_target_pairs={{0,6},{1,7},{2,0},{3,1},{4,2},{5,3},{6,4},{7,5},{8,14},{9,15},{10,... | collective-permute-start | bytes 1572872 | tf_op jit(solution)/shard_map/ppermute | solution.py:457
  (210 other events, 3179.5 us)
Sparse Core Ops, SparseCore 0:
  11.7 270.8 all-gather.4
  286.1 180.1 all-gather.8
  469.8 172.9 all-gather.10
  646.3 75.6 all-gather.6

commit v3 on v2

--- a/solution.py
+++ b/solution.py
@@ -296,7 +296,7 @@
         out_specs=[spec(("r", rows)) for rows, _ in outs],
         out_shape=[jax.ShapeDtypeStruct((rows, width), dt) for rows, dt in outs],
         compiler_params=pltpu.CompilerParams(vmem_limit_bytes=48 * 2**20),
-        cost_estimate=pl.CostEstimate(flops=flops, bytes_accessed=10 * tokens * width * 4, transcendentals=8 * tokens * width),
+        cost_estimate=pl.CostEstimate(flops=0, bytes_accessed=0, transcendentals=0),
     )(*[value for _, value in ins])
 
 
@@ -355,6 +355,198 @@
     )
 
 
+def dot3s(left, right, dims):
+    lh, ll = left
+    rh, rl = right
+
+    def one(a, b):
+        return lax.dot_general(a, b, dims, preferred_element_type=F32)
+
+    return one(lh, rh) + one(lh, rl) + one(ll, rh)
+
+
+def mix_back_kernel(
+    g1_ref, g2_ref, g3_ref, g4_ref, gld_ref, ld_ref, n_ref, p_ref, f_ref, vec_ref, lora_ref, tan_ref,
+    down_ref, up_ref, ddown_ref, dup_ref,
+    gn_ref, ginc_ref, gvec_ref, gdown_ref, gup_ref, gddown_ref, gdup_ref,
+    gdl_ref, flat_ref,
+):
+    tokens, width = n_ref.shape
+    rank, block = lora_ref.shape[2], 256
+    tan = tan_ref[...]
+    tan2 = two(tan)
+    lora2 = [two(lora_ref[c]) for c in range(5)]
+
+    def columns(j):
+        return pl.ds(pl.multiple_of(j * block, block), block)
+
+    def total(value):
+        return jnp.sum(value, 0, keepdims=True)
+
+    def first(j, carry):
+        gtan, glora = carry
+        at = columns(j)
+        n = n_ref[:, at]
+        d = p_ref[:, at] - n
+        gdec = gld_ref[:, at] * ld_ref[:, at]
+        gvec_ref[6:7, at] = total(gdec)
+        gdec2 = two(gdec)
+        gtan = gtan + dot3(gdec2, two(dup_ref[:, at]), NT)
+        gdup_ref[:, at] = dot3(tan2, gdec2, TN)
+        gn = jnp.zeros_like(n)
+        gdl = jnp.zeros_like(n)
+        new = []
+        for c, ref in enumerate((g1_ref, g2_ref, g3_ref, g4_ref), 1):
+            g = ref[:, at]
+            up2 = two(up_ref[c, :, at])
+            m = vec_ref[3 + c : 4 + c, at] + dot3s(lora2[c], up2, NN)
+            gm = g * d
+            gm2 = two(gm)
+            gvec_ref[1 + c : 2 + c, at] = total(gm)
+            gup_ref[c, :, at] = dot3(lora2[c], gm2, TN)
+            new.append(glora[c - 1] + dot3(gm2, up2, NT))
+            gn = gn + g
+            gdl = gdl + g * m
+        gn_ref[:, at] = gn
+        gdl_ref[:, at] = gdl
+        return gtan, tuple(new)
+
+    blank = jnp.zeros((tokens, rank), F32)
+    gtan, glora = lax.fori_loop(0, width // block, first, (jnp.zeros_like(tan), (blank,) * 4))
+    gtan2 = two(gtan * (1.0 - tan * tan))
+
+    def second(j, glora):
+        at = columns(j)
+        n = n_ref[:, at]
+        d = p_ref[:, at] - n
+        g = dot3s(gtan2, two(ddown_ref[at, :]), NT)
+        up2 = two(up_ref[0, :, at])
+        m = vec_ref[3:4, at] + dot3s(lora2[0], up2, NN)
+        gddown_ref[at, :] = dot3(two(n + d * m), gtan2, TN)
+        gm = g * d
+        gm2 = two(gm)
+        gvec_ref[1:2, at] = total(gm)
+        gup_ref[0, :, at] = dot3(lora2[0], gm2, TN)
+        gn_ref[:, at] += g
+        gdl_ref[:, at] += g * m
+        return glora + dot3(gm2, up2, NT)
+
+    glora = (lax.fori_loop(0, width // block, second, blank), *glora)
+    for c in range(5):
+        lora = lora_ref[c]
+        flat_ref[:, c * rank : (c + 1) * rank] = glora[c] * (1.0 - lora * lora)
+    flat2 = two(flat_ref[...])
+    last = lax.broadcasted_iota(jnp.int32, (tokens, block), 0) == tokens - 1
+
+    def third(j, carry):
+        at = columns(j)
+        n = n_ref[:, at]
+        d = p_ref[:, at] - n
+        shift = vec_ref[2:3, at]
+        g = dot3s(flat2, two(down_ref[at, :]), NT)
+        gdown_ref[at, :] = dot3(two(n + d * shift), flat2, TN)
+        gvec_ref[0:1, at] = total(g * d)
+        gdl = gdl_ref[:, at] + g * shift
+        passed = gdl * f_ref[...]
+        ginc_ref[:, at] = passed[0:1]
+        passed = jnp.where(last, 0.0, pltpu.roll(passed, tokens - 1, 0))
+        gn_ref[:, at] = gn_ref[:, at] + g - gdl + passed
+        return carry
+
+    lax.fori_loop(0, width // block, third, 0)
+    gvec_ref[7:8, :] = jnp.zeros((1, width), F32)
+
+
+def mix_back(grads, grad_dec, logdec, normed, prior, follows, vecs, lora, tan, down, up, ddown, dup):
+    tokens, width = normed.shape
+    rank = up.shape[1]
+    lora = jnp.stack([lora[:, c * rank : (c + 1) * rank] for c in range(5)])
+    shapes = [
+        (tokens, width), (1, width), (8, width), down.shape, up.shape, ddown.shape, dup.shape,
+    ]
+    return pl.pallas_call(
+        mix_back_kernel,
+        in_specs=[pl.BlockSpec(memory_space=pltpu.VMEM)] * 16,
+        out_specs=[pl.BlockSpec(memory_space=pltpu.VMEM)] * 7,
+        out_shape=[jax.ShapeDtypeStruct(shape, F32) for shape in shapes],
+        scratch_shapes=[pltpu.VMEM((tokens, width), F32), pltpu.VMEM((tokens, 5 * rank), F32)],
+        compiler_params=pltpu.CompilerParams(vmem_limit_bytes=56 * 2**20),
+        cost_estimate=pl.CostEstimate(flops=0, bytes_accessed=0, transcendentals=0),
+    )(*grads, grad_dec, logdec, normed, prior, follows, vecs, lora, tan, down, up, ddown, dup)
+
+
+FREE = pl.CostEstimate(flops=0, bytes_accessed=0, transcendentals=0)
+
+
+def tile_of(size, largest):
+    return max(t for t in range(128, largest + 1, 128) if size % t == 0)
+
+
+def slab_kernel(index_ref, left_ref, grad_ref, *refs):
+    total = lax.dot_general(left_ref[...], grad_ref[...], TN, preferred_element_type=F32)
+    for ref in refs[:-1]:
+        total = total + ref[...].astype(F32)
+    refs[-1][...] = total.astype(refs[-1].dtype)
+
+
+def slab_grad(left, grad, wide, start, width, shards, added=()):
+    tokens = left.shape[0]
+    tr, tc = tile_of(wide, 1024), tile_of(width, 2048)
+    steps = wide // tr
+    grid = (len(shards), steps, width // tc)
+    return pl.pallas_call(
+        slab_kernel,
+        grid_spec=pltpu.PrefetchScalarGridSpec(
+            num_scalar_prefetch=1,
+            grid=grid,
+            in_specs=[
+                pl.BlockSpec((tokens, tr), lambda i, a, b, index: (0, index[i] * steps + a)),
+                pl.BlockSpec((tokens, tc), lambda i, a, b, index: (0, start // tc + b)),
+            ]
+            + [
+                pl.BlockSpec((tr, tc), functools.partial(_row_block, row // tr, steps))
+                for _, row in added
+            ],
+            out_specs=pl.BlockSpec((tr, tc), functools.partial(_row_block, 0, steps)),
+        ),
+        out_shape=jax.ShapeDtypeStruct((len(shards) * wide, width), BF),
+        compiler_params=pltpu.CompilerParams(vmem_limit_bytes=56 * 2**20),
+        cost_estimate=FREE,
+    )(jnp.stack(shards).astype(jnp.int32), left, grad, *[value for value, _ in added])
+
+
+def _row_block(first, steps, i, a, b, index):
+    return (first + i * steps + a, b)
+
+
+def back_kernel(grad_ref, weight_ref, *refs):
+    total = lax.dot_general(grad_ref[...], weight_ref[...], NT, preferred_element_type=F32)
+    if len(refs) == 2:
+        total = total * (2.0 * refs[0][...])
+    refs[-1][...] = total.astype(refs[-1].dtype)
+
+
+def back_dot(grad, weight, place=None, positive=None):
+    tokens, width = grad.shape
+    rows = weight.shape[-2]
+    tile = tile_of(rows, 512 if width <= 4096 else 256)
+    if place is None:
+        spec = pl.BlockSpec((tile, width), lambda a: (a, 0))
+    else:
+        spec = pl.BlockSpec((None, tile, width), lambda a: (place, a, 0))
+    column = pl.BlockSpec((tokens, tile), lambda a: (0, a))
+    return pl.pallas_call(
+        back_kernel,
+        grid=(rows // tile,),
+        in_specs=[pl.BlockSpec((tokens, width), lambda a: (0, 0)), spec]
+        + [column] * (positive is not None),
+        out_specs=column,
+        out_shape=jax.ShapeDtypeStruct((tokens, rows), F32 if positive is None else BF),
+        compiler_params=pltpu.CompilerParams(vmem_limit_bytes=56 * 2**20),
+        cost_estimate=FREE,
+    )(grad, weight, *([] if positive is None else [positive]))
+
+
 HIGHEST = lax.Precision.HIGHEST
 FACTORS = (0.2, 0.03, 0.03, 0.03, 0.03, 0.03, 0.03, 0.03, 0.03)
 BOTH = ("seq", "dp")
@@ -378,25 +570,22 @@
     return jnp.concatenate([incoming, field[:-1]], axis=0) * follows
 
 
-def mix_inputs(normed, incoming, vecs, down, up, ddown, dup, follows):
-    delta = shifted(normed, incoming, follows) - normed
+def mix_inputs(normed, prior, vecs, down, up, ddown, dup):
+    delta = prior - normed
     lora = jnp.tanh(jnp.dot(normed + delta * vecs[2], down, precision=HIGHEST))
-    rank = lora.shape[1] // 5
+    rank = up.shape[1]
     inputs = [
         normed
         + delta
         * (
             vecs[3 + c]
-            + jnp.dot(
-                lora[:, c * rank : (c + 1) * rank], up[c * rank : (c + 1) * rank], precision=HIGHEST
-            )
+            + jnp.dot(lora[:, c * rank : (c + 1) * rank], up[c], precision=HIGHEST)
         )
         for c in range(5)
     ]
-    decay = vecs[8] + jnp.dot(
-        jnp.tanh(jnp.dot(inputs[0], ddown, precision=HIGHEST)), dup, precision=HIGHEST
-    )
-    return (inputs[1], inputs[2], inputs[3], inputs[4], -jnp.exp(decay))
+    tan = jnp.tanh(jnp.dot(inputs[0], ddown, precision=HIGHEST))
+    logdec = -jnp.exp(vecs[8] + jnp.dot(tan, dup, precision=HIGHEST))
+    return [v.astype(BF) for v in inputs[1:]], logdec, lora, tan
 
 
 def channel_inputs(second, incoming, vecs, follows):
@@ -473,6 +662,14 @@
         self.units.extend([unit, None, None] for unit in units)
         return self.units[-len(units) :]
 
+    def start(self, unit):
+        (entry,) = self.add(unit)
+        try:
+            entry[1] = unit.send(None)
+        except StopIteration as stop:
+            entry[:] = [None, None, stop.value]
+        return entry
+
     def tick(self, values=()):
         live = [u for u in self.units if u[0] is not None]
         waiting, values = lax.optimization_barrier(([u[1] for u in live], values))
@@ -497,7 +694,7 @@
     both = jnp.concatenate([column, other], 0)
     chunks = [pick(both, ((k ^ y) * 4) + (z - j) % 4) for j in range(4) for k in (0, 1)]
     slab = jnp.concatenate(chunks, 0)
-    across, near = yield [swap(slab, "seq", 2), swap(slab, "seq", 1)]
+    near, across = yield [swap(slab, "seq", j) for j in (1, 2)]
     (far,) = yield [swap(across, "seq", 1)]
     return [slab, near, across, far]
 
@@ -518,36 +715,53 @@
     return jnp.concatenate([pick(every, s ^ j) for j in range(4)])
 
 
-def scatter_unit(first, second, rows, kind):
+def scatter_unit(first, second, rows, waits):
     s, d = lax.axis_index("seq"), lax.axis_index("dp")
-    z, y = d // 2, d % 2
-    wide = rows * 8
-
-    def parts(value):
-        return value.reshape(-1, 4, 2, rows, value.shape[-1])
-
-    sends = [swap(f([s ^ 3, s ^ 1]).astype(kind), "seq", 1) for f in (first, second) if f]
-    one, *two = yield sends
-    sends = [swap((first([s ^ 2]) + one[:wide].astype(F32)).astype(kind), "seq", 2)]
-    if second:
-        both = parts((second([s ^ 2, s]) + two[0].astype(F32)).astype(kind))
-        sends.append(swap(pick(both, 1 - y, 2), "dp", 1))
-    across, *beside = yield sends
-    own = parts((first([s]) + one[wide:].astype(F32) + across.astype(F32)).astype(kind))
-    sends = [swap(pick(own, 1 - y, 2), "dp", 1)]
-    if second:
-        both = pick(both, y, 2).astype(F32) + beside[0].astype(F32)
-        sends.append(swap(both[0].astype(kind), "seq", 2))
-    beside, *across = yield sends
-    own = [(pick(own, y, 2)[0].astype(F32) + beside[0].astype(F32)).astype(kind)]
-    if second:
-        own.append((both[1] + across[0].astype(F32)).astype(kind))
-    own = jnp.stack(own, 1)
-    arrived = yield [to_plane(pick(own, (z + t) % 4), t) for t in (1, 2, 3)]
-    total = pick(own, z).astype(F32)
-    for part in arrived:
-        total = total + part.astype(F32)
-    return [total[i] for i in range(total.shape[0])]
+    high, low, y = d // 4, d // 2 % 2, d % 2
+    wide, kind = rows * 8, BF
+
+    def half(value, index):
+        return pick(value.reshape(-1, 4, 2, rows, value.shape[-1]), index, 2).astype(F32)
+
+    both = [f([s ^ 3, s ^ 1]) for f in (first, second)]
+    ahead = [first([s ^ 2]), second([s ^ 2, s]), first([s])]
+    if "join" in waits:
+        both, *ahead = yield [swap(jnp.stack(both), "seq", 1), *ahead]
+        one, two = both[0], both[1]
+    else:
+        one, two, *ahead = yield [*[swap(v, "seq", 1) for v in both], *ahead]
+    for _ in range(waits.get("a", 0)):
+        one, two, *ahead = yield [one, two, *ahead]
+    across = (ahead[0].astype(F32) + one[:wide].astype(F32)).astype(kind)
+    other = (half(ahead[1], 1 - y) + half(two, 1 - y)).astype(kind)
+    sends = [swap(across, "seq", 2), swap(other, "dp", 1)]
+    ahead = [
+        (ahead[2].astype(F32) + one[wide:].astype(F32)).astype(kind),
+        (half(ahead[1], y) + half(two, y)).astype(kind),
+    ]
+    across, beside, *ahead = yield [*sends, *ahead]
+    for _ in range(waits.get("b", 0)):
+        across, beside, *ahead = yield [across, beside, *ahead]
+    other = (half(ahead[0], 1 - y) + half(across, 1 - y))[0].astype(kind)
+    first_out = (ahead[1][0].astype(F32) + beside[0].astype(F32)).astype(kind)
+    sends = [swap(other, "dp", 1), swap(first_out, "seq", 2)]
+    ahead = [
+        (half(ahead[0], y) + half(across, y))[0].astype(kind),
+        (ahead[1][1].astype(F32) + beside[1].astype(F32)).astype(kind),
+    ]
+    *arrived, one, two = yield [*sends, *ahead]
+    mine = [(a.astype(F32) + b.astype(F32)) for a, b in zip((one, two), arrived)]
+    mine = [v.reshape(2, 2, *v.shape[1:]) for v in mine]
+    other = jnp.stack([pick(v, 1 - low, 1) for v in mine], 1).astype(kind)
+    own = jnp.stack([pick(v, low, 1) for v in mine], 1).astype(kind)
+    far, own = yield [swap(other, "dp", 2), own]
+    for _ in range(waits.get("high", 0)):
+        far, own = yield [far, own]
+    other = (pick(own, 1 - high).astype(F32) + pick(far, 1 - high).astype(F32)).astype(kind)
+    own = pick(own, high).astype(F32) + pick(far, high).astype(F32)
+    far, own = yield [swap(other, "dp", 4), own]
+    total = own + far.astype(F32)
+    return [total[0], total[1]]
 
 
 def plain_scatter(*wholes):
@@ -559,36 +773,24 @@
     yield
 
 
-def scatter(*pairs):
+def scatter(*pairs, waits={}):
     if not tuned():
         return plain_scatter(*[product_t(left, grad) for left, grad in pairs])
 
-    def blocks(left, grad):
-        wide = left.shape[1] // 4
-
-        def block(shards):
-            taken = [lax.dynamic_slice_in_dim(left, i * wide, wide, 1) for i in shards]
-            return product_t(jnp.concatenate(taken, 1), grad)
+    def blocks(left, grad, start, width):
+        def block(shards, *added):
+            return slab_grad(left, grad, left.shape[1] // 4, start, width, shards, added)
 
         return block
 
     if len(pairs) == 1:
         left, grad = pairs[0]
         half = grad.shape[1] // 2
-        pairs = ((left, grad[:, :half]), (left, grad[:, half:]))
+        pairs = ((left, grad, 0, half), (left, grad, half, half))
+    else:
+        pairs = [(left, grad, 0, grad.shape[1]) for left, grad in pairs]
     rows = pairs[0][0].shape[1] // 4 // lax.axis_size("dp")
-    return scatter_unit(*[blocks(*pair) for pair in pairs], rows, BF)
-
-
-def scatter_small(whole):
-    if not tuned():
-        return plain_scatter(whole)
-    wide = whole.shape[0] // 4
-
-    def block(shards):
-        return jnp.concatenate([lax.dynamic_slice_in_dim(whole, i * wide, wide, 0) for i in shards])
-
-    return scatter_unit(block, None, wide // 8, F32)
+    return scatter_unit(*[blocks(*pair) for pair in pairs], rows, waits)
 
 
 def renew(weight, moment, average, grad, factor, tokens):
@@ -616,13 +818,14 @@
     small = jnp.concatenate(
         [vectors.T, maa_down, maa_up.reshape(5 * rank, -1).T, decay_down, decay_up.T], axis=1
     )
-    up_steps = Steps()
-    (small,) = up_steps.add(gather(small))
-    up_steps.drain()
-    mix = lax.all_gather(mix_weights.astype(BF), BOTH, axis=1, tiled=True)
+    ups = Steps()
+    (small,) = ups.add(gather(small))
+    square = jnp.concatenate([mix_weights, ffn_recept[None]]).astype(BF)
+    square = lax.all_gather(square, BOTH, axis=1, tiled=True)
     fkey = lax.all_gather(ffn_key.astype(BF), BOTH, axis=0, tiled=True)
     fval = lax.all_gather(ffn_value.astype(BF), BOTH, axis=0, tiled=True)
-    frec = lax.all_gather(ffn_recept.astype(BF), BOTH, axis=0, tiled=True)
+    mix, wout, frec = square[:4], square[4], square[5]
+    ups.drain()
     small = in_order(small[-1])
     cuts = np.cumsum([n_vec, n_down, 5 * rank, n_decay, n_decay])
     vecs, down, up, ddown, dup = jnp.split(small, cuts[:-1], axis=1)
@@ -631,10 +834,11 @@
     hidden = block_input[0].astype(F32)
     normed, pull_norm_one = jax.vjp(norm_first, hidden, vecs)
     incoming = send_rows(normed)
-    (xkey, xval, xrec, xgate, logdec), pull_mix = jax.vjp(
-        functools.partial(mix_inputs, follows=follows), normed, incoming, vecs, down, up, ddown, dup
-    )
-    xkey, xval, xrec, xgate = (v.astype(BF) for v in (xkey, xval, xrec, xgate))
+    up = up.reshape(5, rank, width)
+    prior = shifted(normed, incoming, follows)
+    (xkey, xval, xrec, xgate), logdec, lora, tan = mix_inputs(
+        normed, prior, vecs, down, up, ddown, dup
+    )
     keys = product(xkey, mix[0])
     values = product(xval, mix[1])
     closing, carry = close(keep, keys, values, logdec)
@@ -643,7 +847,7 @@
     gate = product(xgate, mix[3])
     vec3 = vecs[9:12]
     raw, gated, score, states = forward(keep, recept, keys, values, logdec, gate, vec3, before)
-    middle = hidden + product(gated, mix[4])
+    middle = hidden + product(gated, wout)
 
     second, pull_norm_two = jax.vjp(norm_second, middle, vecs)
     incoming_two = send_rows(second)
@@ -653,67 +857,76 @@
     key_in, rec_in = key_in.astype(BF), rec_in.astype(BF)
     positive = jnp.maximum(product(key_in, fkey), 0.0)
     squared = (positive * positive).astype(BF)
+    sigma = jax.nn.sigmoid(product(rec_in, frec))
+    squared, positive, sigma = lax.optimization_barrier((squared, positive, sigma))
     kvals = product(squared, fval)
-    sigma = jax.nn.sigmoid(product(rec_in, frec))
     block_output = middle + sigma * kvals
 
     steps = Steps()
     upstream = out_grad[0].astype(F32)
     grad_kvals = (upstream * sigma).astype(BF)
     grad_rpre = (upstream * kvals * sigma * (1.0 - sigma)).astype(BF)
-    (sum_fval,) = steps.add(scatter((squared, grad_kvals)))
+    (sum_fval,) = steps.add(scatter((squared, grad_kvals), waits={"b": 1, "high": 1}))
     grad_kvals = steps.tick(grad_kvals)
-    grad_kpre = (back_product(grad_kvals, fval) * (2.0 * positive)).astype(BF)
+    grad_kpre = back_dot(grad_kvals, fval, positive=positive)
     grad_kpre = steps.tick(grad_kpre)
     grad_second, grad_inc_two, vec_one = pull_channel(
-        (back_product(grad_kpre, fkey), back_product(grad_rpre, frec))
+        (back_dot(grad_kpre, fkey), back_dot(grad_rpre, square, 5))
     )
     grad_second = back_rows(grad_inc_two, grad_second)
     grad_mid, vec_two = pull_norm_two(grad_second)
     grad_middle = upstream + grad_mid
     grad_attn = grad_middle.astype(BF)
-    (sum_fkey,) = steps.add(scatter((key_in, grad_kpre)))
-    grad_attn = steps.tick(grad_attn)
-    grad_gated = back_product(grad_attn, mix[4])
+    grad_attn, key_in, grad_kpre = lax.optimization_barrier((grad_attn, key_in, grad_kpre))
+    (sum_fkey,) = steps.add(scatter((key_in, grad_kpre), waits={"a": 1}))
+    grad_attn, rec_in, grad_rpre = steps.tick((grad_attn, rec_in, grad_rpre))
+    sum_rec_out = steps.start(
+        scatter((rec_in, grad_rpre), (gated, grad_attn), waits={"high": 2})
+    )
+    grad_gated = back_dot(grad_attn, square, 4)
     grad_raw, grad_gate, direct, vec_head = head_back(
         keep, recept, logdec, raw, gate, grad_gated, vec3
     )
     later = prefix(carry, direct, True)
     later, grad_gate = steps.tick((later, grad_gate))
-    grad_xgate = back_product(grad_gate, mix[3])
     grad_rec, grad_key, grad_val, grad_dec, vec_bonus = backward(
         keep, recept, keys, values, logdec, grad_raw, score, states, later, vec3
     )
-    (sum_rec_out,) = steps.add(scatter((rec_in, grad_rpre), (gated, grad_attn)))
-    grad_rec, grad_key, grad_val, grad_xgate = steps.tick(
-        (grad_rec, grad_key, grad_val, grad_xgate)
-    )
-    grad_x = (
-        back_product(grad_key, mix[0]),
-        back_product(grad_val, mix[1]),
-        back_product(grad_rec, mix[2]),
-        grad_xgate,
-        grad_dec,
-    )
-    grad_x = steps.tick(grad_x)
-    grad_normed, grad_inc, vec_mix, gdown, gup, gddown, gdup = pull_mix(grad_x)
+    grads = (grad_key, grad_val, grad_rec, grad_gate)
+    grads, grad_dec = steps.tick((grads, grad_dec))
+    grad_key, grad_val, grad_rec, grad_gate = grads
+    mixed = mix_back(
+        [back_dot(grad, square, i) for i, grad in enumerate(grads)],
+        grad_dec, logdec, normed, prior, follows, vecs, lora, tan, down, up, ddown, dup,
+    )
+    mixed, grads = steps.tick((mixed, grads))
+    grad_key, grad_val, grad_rec, grad_gate = grads
+    sum_gate_rec = steps.start(
+        scatter((xgate, grad_gate), (xrec, grad_rec), waits={"join": 1})
+    )
+    sum_key_val = steps.start(
+        scatter((xkey, grad_key), (xval, grad_val), waits={"join": 1, "a": 1})
+    )
+    mixed = steps.tick(mixed)
+    grad_normed, grad_inc, vec_mix, gdown, gup, gddown, gdup = mixed
     grad_normed = back_rows(grad_inc, grad_normed)
     grad_hidden, vec_three = pull_norm_one(grad_normed)
     input_grad = grad_middle + grad_hidden
 
-    vec_all = vec_one + vec_two + vec_mix + vec_three
+    vec_all = vec_one + vec_two + vec_three
     vec_all = jnp.concatenate(
-        [vec_all[:9], vec_all[9:10] + vec_bonus, vec_all[10:12] + vec_head, vec_all[12:]], axis=0
-    )
-    total = jnp.concatenate([vec_all.T, gdown, gup.T, gddown, gdup.T], axis=1)
-    (sum_gate_rec,) = steps.add(scatter((xgate, grad_gate), (xrec, grad_rec)))
+        [vec_all[:2], vec_mix[:7], vec_bonus, vec_head, vec_all[12:]], axis=0
+    )
+    total = jnp.concatenate(
+        [vec_all.T, gdown, gup.reshape(5 * rank, width).T, gddown, gdup.T], axis=1
+    )
     total, input_grad = steps.tick((total, input_grad))
-    (sum_small,) = steps.add(scatter_small(total))
-    steps.tick()
-    (sum_key_val,) = steps.add(scatter((xkey, grad_key), (xval, grad_val)))
+    total = lax.psum_scatter(total, "seq", scatter_dimension=0, tiled=True)
+    total = steps.tick(total)
+    total = lax.psum_scatter(total, "dp", scatter_dimension=0, tiled=True)
     steps.drain()
 
-    gvec, gdown, gup, gddown, gdup = jnp.split(sum_small[-1][0], cuts[:-1], axis=1)
+    gvec, gdown, gup, gddown, gdup = jnp.split(total, cuts[:-1], axis=1)
     grad_frec, grad_out = sum_rec_out[-1]
     grads = (
         gvec.T,

time: 1630 us -> 1600 us (0.982)
  Pallas kernels: 132 us -> 368 us
  matrix products: 311 us -> 98.5 us
  other arithmetic: 152 us -> 230 us
  starting transfers between devices: 111 us -> 57.5 us
  waiting for transfers between devices: 790 us -> 740 us
  local copies, waits for them, and re-layouts: 97.9 us -> 75.8 us
    pallas_call x0 -> x34, Pallas kernels: none -> 236 us  [the longest x25 123 us: slab_grad(): pl.pallas_call(slab_kernel, grid_spec=pltpu.PrefetchScalarGridSpec(num_sc...]
    dot_general x54 -> x7, matrix products: 220 us -> 19.7 us  [the longest x5 14.6 us: mix_inputs(): jnp.dot(lora[:, c * rank:(c + 1) * rank], up[c], precision=HIGHEST)]
    ppermute x21 -> x3, waiting for transfers between devices: 143 us -> 24.9 us  [to_plane(): lax.ppermute(value, 'dp', [(i, (i + 2 * step) % n) for i in range(n)])]
    ppermute x39 -> x44, waiting for transfers between devices: 193 us -> 289 us  [swap(): lax.ppermute(value, axis, [(i, i ^ bit) for i in range(lax.axis_size(axis...]
    convert_element_type x13 -> x30, other arithmetic: 44.1 us -> 119 us  [the longest x5 29.6 us: scatter_unit(): (ahead[2].astype(F32) + one[wide:].astype(F32)).astype(kind)]
    ppermute x21 -> x3, starting transfers between devices: 67.4 us -> 6.96 us  [to_plane(): lax.ppermute(value, 'dp', [(i, (i + 2 * step) % n) for i in range(n)])]
    ppermute x2, waiting for transfers between devices: 43.7 us -> 14.8 us  [prefix(): arrived = lax.ppermute(chip, 'seq', pairs)]
    another operation x5 -> x15, other arithmetic: 8.15 us -> 28.4 us  [the longest x2 14.9 us: scatter_unit(): both, *ahead = (yield [swap(jnp.stack(both), 'seq', 1), *ahead])]
  transfers between devices with their start and end apart: 70 -> 58, of which waited for: 34 -> 25; matrix products, arithmetic and copies ran while one was open for 27% -> 21% of each run, Pallas kernels for 8% -> 21%
where the time goes in v3:
time: 1600 us; the launch traced here: 1590 us
  waiting for transfers between devices  740 us (46%)
  Pallas kernels  368 us (23%)
  other arithmetic  230 us (14%)
  matrix products  98.5 us (6%)
  local copies, waits for them, and re-layouts  75.8 us (5%)
  starting transfers between devices  57.5 us (4%)
  between operations  16.9 us (1%)
    ppermute x44, waiting for transfers between devices, swap(): lax.ppermute(value, axis, [(i, i ^ bit) for i in range(lax.axis_size(axis...  289 us
    all_gather x1, waiting for transfers between devices, local(): square = lax.all_gather(square, BOTH, axis=1, tiled=True)  181 us
    all_gather x1, waiting for transfers between devices, local(): fval = lax.all_gather(ffn_value.astype(BF), BOTH, axis=0, tiled=True)  160 us
    pallas_call x4, Pallas kernels, _call(): pl.pallas_call(kernel, grid=(width // LANES,), in_specs=[spec(kind) for k...  132 us
    pallas_call x25, Pallas kernels, slab_grad(): pl.pallas_call(slab_kernel, grid_spec=pltpu.PrefetchScalarGridSpec(num_sc...  123 us
    pallas_call x8, Pallas kernels, back_dot(): pl.pallas_call(back_kernel, grid=(rows // tile,), in_specs=[pl.BlockSpec(...  80.3 us
    dot_general x8, matrix products, product(): return jnp.dot(left, right, preferred_element_type=F32)  76 us
    all_gather x1, waiting for transfers between devices, local(): fkey = lax.all_gather(ffn_key.astype(BF), BOTH, axis=0, tiled=True)  52.2 us
  transfers between devices with their start and end apart: 58, of which 25 were waited for; matrix products, arithmetic and copies ran while one was open for 21% of the time, Pallas kernels for 21%

profile of v3, /device:TPU:0, one launch (start us, length us, event | category | flops | bytes accessed | tf_op | source)
XLA Modules:
  0.0 1586.1 jit_solution(2567964806393373889)
XLA Ops:
  27.1 20.0 %collective-permute-done.1 = f32[64,464]{0,1:T(8,128)S(1)} collective-permute-done((f32[64,464]{0,1:T(8,128)S(1)}, f32[64,464]{0,1:T(8,128)S(1)}, u32[]{:S(2)}, u32[]{:S(2)}) %collective-permute-start.1) | collective-permute-done | bytes 118816 | tf_op jit(solution)/shard_map/ppermute | solution.py:646
  50.6 11.7 collective-permute-done.3
  66.5 26.4 %collective-permute-done.5 = f32[512,464]{0,1:T(8,128)} collective-permute-done((f32[512,464]{0,1:T(8,128)}, f32[512,464]{0,1:T(8,128)}, u32[]{:S(2)}, u32[]{:S(2)}) %collective-permute-start.5) | collective-permute-done | bytes 950304 | tf_op jit(solution)/shard_map/ppermute | solution.py:641
  140.8 180.7 %all-gather.4.cloned.1.call-done.weight_ref = bf16[6,2048,2048]{2,1,0:T(8,128)(2,1)} async-done(((bf16[6,64,2048]{2,1,0:T(8,128)(2,1)}), bf16[6,2048,2048]{2,1,0:T(8,128)(2,1)}) %all-gather.4.cloned.1.call-update) | async-done | bytes 50331664 | tf_op jit(solution)/shard_map/all_gather | solution.py:824
  321.6 6.0 fusion.3.v_ref
  327.6 7.1 fusion.4.k_ref
  334.8 13.7 shard_map.599
  348.9 7.1 fusion.2.gate_ref
  359.6 7.8 fusion.5.q_ref
  367.4 14.8 collective-permute-done.9
  382.3 50.9 %shard_map.600 = (f32[256,2048]{1,0:T(8,128)S(1)}, bf16[256,2048]{1,0:T(8,128)(2,1)S(1)}, f32[256,2048]{1,0:T(8,128)S(1)}, f32[256,2048]{1,0:T(8,128)}) custom-call(f32[4]{0:T(128)S(1)} %compare_convert_fusion.keep_ref, f32[256,2048]{1,0:T(8,128)} %fusion.5.q_ref, f32[256,2048]{1,0:T(8,128)} %copy-done.1, f32[256,2048]{1,0:T(8,128)} %copy-done, ...), custom_call_target="tpu_custom_call" | custom-call | tf_op jit(solution)/shard_map/pallas_call | solution.py:292
  433.2 7.7 fusion.116
  446.0 7.4 fusion.39
  453.4 52.2 %all-gather.6.cloned.1.call-done.weight_ref = bf16[2048,7168]{1,0:T(8,128)(2,1)} async-done(((bf16[64,7168]{1,0:T(8,128)(2,1)}), bf16[2048,7168]{1,0:T(8,128)(2,1)}) %all-gather.6.cloned.1.call-update) | async-done | bytes 29360144 | tf_op jit(solution)/shard_map/all_gather | solution.py:825
  505.6 16.3 %multiply_convert_fusion = (bf16[256,7168]{1,0:T(8,128)(2,1)}, f32[256,7168]{1,0:T(8,128)}) fusion(bf16[256,2048]{1,0:T(8,128)(2,1)S(1)} %get-tuple-element.219.left_ref, bf16[2048,7168]{1,0:T(8,128)(2,1)} %all-gather.6.cloned.1.call-done.weight_ref), kind=kOutput, calls=%fused_computation.23 | convolution fusion | flops 7521697792 | bytes 41418752 | tf_op jit(solution)/shard_map/dot_general | solution.py:629
  521.8 159.7 %all-gather.8.cloned.1.call-done.weight_ref = bf16[7168,2048]{1,0:T(8,128)(2,1)} async-done(((bf16[224,2048]{1,0:T(8,128)(2,1)}), bf16[7168,2048]{1,0:T(8,128)(2,1)}) %all-gather.8.cloned.1.call-update) | async-done | bytes 29360144 | tf_op jit(solution)/shard_map/all_gather | solution.py:826
  681.6 16.6 %fusion.47 = (bf16[256,2048]{1,0:T(8,128)(2,1)}, f32[1,256,2048]{2,1,0:T(8,128)}, bf16[256,2048]{1,0:T(8,128)(2,1)}) fusion(f32[256,2048]{1,0:T(8,128)} %fusion.39, bf16[1,256,2048]{2,1,0:T(8,128)(2,1)} %param.41, f32[256,2048]{1,0:T(8,128)S(1)} %get-tuple-element.638, bf16[256,7168]{1,0:T(8,128)(2,1)} %get-tuple-element.206.left_ref, ...), kind=kOutput, calls=%fused_computation.110 | convolution fusion | flops 7521435648 | bytes 42467328 | tf_op jit(solution)/shard_map/dot_general | solution.py:629
  698.2 6.9 shard_map.602
  705.1 6.9 shard_map.601
  720.7 6.9 shard_map.604
  727.6 6.9 shard_map.607
  734.6 21.2 %shard_map.606.grad_ref = bf16[256,7168]{1,0:T(8,128)(2,1)} custom-call(bf16[256,2048]{1,0:T(8,128)(2,1)} %get-tuple-element.589.grad_ref, bf16[7168,2048]{1,0:T(8,128)(2,1)} %all-gather.8.cloned.1.call-done.weight_ref, f32[256,7168]{1,0:T(8,128)} %get-tuple-element.207.refs_0_), custom_call_target="tpu_custom_call" | custom-call | tf_op jit(solution)/shard_map/pallas_call | solution.py:538
  755.8 17.3 %shard_map.608 = f32[256,2048]{1,0:T(8,128)} custom-call(bf16[256,7168]{1,0:T(8,128)(2,1)} %shard_map.606.grad_ref, bf16[2048,7168]{1,0:T(8,128)(2,1)} %all-gather.6.cloned.1.call-done.weight_ref), custom_call_target="tpu_custom_call" | custom-call | tf_op jit(solution)/shard_map/pallas_call | solution.py:538
  779.1 7.2 fusion.8
  787.8 7.8 add_convert_fusion.5
  804.1 7.6 shard_map.610
  811.7 7.6 shard_map.609
  819.8 7.0 fusion.9
  826.8 41.9 %collective-permute-done.14 = bf16[2,4,224,1024]{3,2,1,0:T(8,128)(2,1)} collective-permute-done((bf16[2,4,224,1024]{3,2,1,0:T(8,128)(2,1)}, bf16[2,4,224,1024]{3,2,1,0:T(8,128)(2,1)}, u32[]{:S(2)}, u32[]{:S(2)}) %collective-permute-start.14) | collective-permute-done | bytes 3670048 | tf_op jit(solution)/shard_map/ppermute | solution.py:641
  868.7 9.4 collective-permute-done.13
  882.9 4.8 shard_map.614
  888.4 7.0 shard_map.619.grad_ref
  895.4 24.3 %shard_map.620 = (f32[256,2048]{1,0:T(8,128)S(1)}, bf16[256,2048]{1,0:T(8,128)(2,1)S(1)}, f32[64,2048]{1,0:T(8,128)S(1)}, f32[2,2048]{1,0:T(2,128)S(1)}) custom-call(f32[4]{0:T(128)S(1)} %copy-done.24, f32[256,2048]{1,0:T(8,128)S(1)} %copy-done.2, f32[256,2048]{1,0:T(8,128)} %fusion.23.ld_ref, f32[256,2048]{1,0:T(8,128)} %copy-done.9, ...), custom_call_target="tpu_custom_call" | custom-call | tf_op jit(solution)/shard_map/pallas_call | solution.py:292
  929.6 7.5 shard_map.612
  944.5 4.9 shard_map.617
  957.8 5.7 add_convert_fusion.15
  966.1 5.8 fusion.61
  981.9 43.0 %shard_map.621 = (bf16[256,2048]{1,0:T(8,128)(2,1)S(1)}, bf16[256,2048]{1,0:T(8,128)(2,1)S(1)}, bf16[256,2048]{1,0:T(8,128)(2,1)S(1)}, f32[256,2048]{1,0:T(8,128)S(1)}, f32[1,2048]{1,0:T(1,128)S(1)}) custom-call(f32[4]{0:T(128)S(1)} %copy-done.24, f32[256,2048]{1,0:T(8,128)} %fusion.5.q_ref, f32[256,2048]{1,0:T(8,128)} %copy-done.1, f32[256,2048]{1,0:T(8,128)} %copy-done, ...), custom_call_target="tpu_custom_call" | custom-call | tf_op jit(solution)/shard_map/pallas_call | solution.py:292
  1024.9 6.0 fusion.60
  1033.4 17.8 %collective-permute-done.23 = bf16[4,224,1024]{2,1,0:T(8,128)(2,1)} collective-permute-done((bf16[4,224,1024]{2,1,0:T(8,128)(2,1)}, bf16[4,224,1024]{2,1,0:T(8,128)(2,1)}, u32[]{:S(2)}, u32[]{:S(2)}) %collective-permute-start.23) | collective-permute-done | bytes 1835040 | tf_op jit(solution)/shard_map/ppermute | solution.py:641
  1051.2 5.0 fusion.10
  1057.5 5.9 add_convert_fusion.1
  1081.6 6.9 shard_map.622.g1_ref
  1088.4 6.9 shard_map.623.g2_ref
  1095.3 6.9 shard_map.624.g3_ref
  1102.2 7.3 shard_map.625.g4_ref
  1109.4 32.3 %shard_map.626 = (f32[256,2048]{1,0:T(8,128)}, f32[1,2048]{1,0:T(1,128)}, f32[8,2048]{1,0:T(8,128)}, f32[2048,160]{1,0:T(8,128)}, f32[5,32,2048]{2,1,0:T(8,128)}...) custom-call(f32[256,2048]{1,0:T(8,128)} %shard_map.622.g1_ref, f32[256,2048]{1,0:T(8,128)} %shard_map.623.g2_ref, ...), custom_call_target="tpu_custom_call" | custom-call | tf_op jit(solution)/shard_map/pallas_call | solution.py:467
  1144.7 6.0 fusion.11
  1150.7 15.6 collective-permute-done.30
  1175.9 7.4 pad_maximum_fusion.1
  1192.9 7.5 pad_maximum_fusion
  1201.0 6.2 fusion.65
  1216.0 5.0 shard_map.635
  1243.5 5.8 collective-permute-done.32
  1264.2 6.8 fusion.6
  1279.3 6.2 slice_bitcast_fusion.12
  1300.1 7.3 concatenate.51
  1310.8 28.1 %collective-permute-done.36 = bf16[2,224,1024]{2,1,0:T(8,128)(2,1)} collective-permute-done((bf16[2,224,1024]{2,1,0:T(8,128)(2,1)}, bf16[2,224,1024]{2,1,0:T(8,128)(2,1)}, u32[]{:S(2)}, u32[]{:S(2)}) %collective-permute-start.36) | collective-permute-done | bytes 917536 | tf_op jit(solution)/shard_map/ppermute | solution.py:641
  1373.1 36.1 %collective-permute-done.41 = bf16[2,64,3584]{2,1,0:T(8,128)(2,1)S(1)} collective-permute-done((bf16[2,64,3584]{2,1,0:T(8,128)(2,1)S(1)}, bf16[2,64,3584]{2,1,0:T(8,128)(2,1)S(1)}, u32[]{:S(2)}, u32[]{:S(2)}) %collective-permute-start.41) | collective-permute-done | bytes 917536 | tf_op jit(solution)/shard_map/ppermute | solution.py:641
  1409.1 34.2 %collective-permute-done.43 = bf16[4,64,2048]{2,1,0:T(8,128)(2,1)S(1)} collective-permute-done((bf16[4,64,2048]{2,1,0:T(8,128)(2,1)S(1)}, bf16[4,64,2048]{2,1,0:T(8,128)(2,1)S(1)}, u32[]{:S(2)}, u32[]{:S(2)}) %collective-permute-start.43) | collective-permute-done | bytes 1048608 | tf_op jit(solution)/shard_map/ppermute | solution.py:641
  1464.7 5.7 multiply_add_fusion.6
  1472.6 30.6 %collective-permute-done.46 = bf16[2,64,2048]{2,1,0:T(8,128)(2,1)} collective-permute-done((bf16[2,64,2048]{2,1,0:T(8,128)(2,1)}, bf16[2,64,2048]{2,1,0:T(8,128)(2,1)}, u32[]{:S(2)}, u32[]{:S(2)}) %collective-permute-start.46) | collective-permute-done | bytes 524320 | tf_op jit(solution)/shard_map/ppermute | solution.py:641
  1517.8 18.2 %reduce-scatter.5.cloned.1.call-done = f32[64,464]{1,0:T(8,128)} async-done(((f32[512,464]{1,0:T(8,128)}), f32[64,464]{1,0:T(8,128)}) %reduce-scatter.5.cloned.1.call-update) | async-done | bytes 118800 | tf_op jit(solution)/shard_map/reduce_scatter | solution.py:926
  1552.5 22.2 %collective-permute-done.52 = bf16[2,64,2048]{2,1,0:T(8,128)(2,1)S(1)} collective-permute-done((bf16[2,64,2048]{2,1,0:T(8,128)(2,1)S(1)}, bf16[2,64,2048]{2,1,0:T(8,128)(2,1)S(1)}, u32[]{:S(2)}, u32[]{:S(2)}) %collective-permute-start.52) | collective-permute-done | bytes 524320 | tf_op jit(solution)/shard_map/ppermute | solution.py:641
  (621 shorter events, 361.7 us)
Async XLA Ops:
  7.2 314.3 %all-gather.4.cloned.1.call-start = ((), (), s32[]{:S(2)}) async-start(), calls=%async_computation.2 | async-start | bytes 51904512 | tf_op jit(solution)/shard_map/all_gather | solution.py:824
  10.6 495.0 %all-gather.6.cloned.1.call-start = ((), (), s32[]{:S(2)}) async-start(), calls=%async_computation.3 | async-start | bytes 30277632 | tf_op jit(solution)/shard_map/all_gather | solution.py:825
  13.4 668.1 %all-gather.8.cloned.1.call-start = ((), (), s32[]{:S(2)}) async-start(), calls=%async_computation.4 | async-start | bytes 30277632 | tf_op jit(solution)/shard_map/all_gather | solution.py:826
  14.6 1430.1 %reduce-scatter.3.cloned.1.call-start = ((), (), s32[]{:S(2)}) async-start(), calls=%async_computation.5 | async-start | bytes 5242880 | tf_op jit(solution)/shard_map/reduce_scatter | solution.py:924
  15.3 11.8 collective-permute-start
  18.4 28.8 %collective-permute-start.1 = (f32[64,464]{0,1:T(8,128)S(1)}, f32[64,464]{0,1:T(8,128)S(1)}, u32[]{:S(2)}, u32[]{:S(2)}) collective-permute-start(f32[64,464]{0,1:T(8,128)S(1)} %constant_dynamic-update-slice_fusion), channel_id=1, source_target_pairs={{0,4},{1,5},{2,6},{3,7},{4,0},{5,1},{6,2},{7,3},{8,12},{9,13},{10,... | collective-permute-start | bytes 356360 | tf_op jit(solution)/shard_map/ppermute | solution.py:646
  21.0 26.2 %collective-permute-start.2 = (f32[64,464]{0,1:T(8,128)S(1)}, f32[64,464]{0,1:T(8,128)S(1)}, u32[]{:S(2)}, u32[]{:S(2)}) collective-permute-start(f32[64,464]{0,1:T(8,128)S(1)} %constant_dynamic-update-slice_fusion), channel_id=1, source_target_pairs={{0,6},{1,7},{2,0},{3,1},{4,2},{5,3},{6,4},{7,5},{8,14},{9,15},{10,... | collective-permute-start | bytes 356360 | tf_op jit(solution)/shard_map/ppermute | solution.py:646
  48.4 13.9 collective-permute-start.3
  63.8 2.7 collective-permute-start.4
  63.8 29.2 %collective-permute-start.5 = (f32[512,464]{0,1:T(8,128)}, f32[512,464]{0,1:T(8,128)}, u32[]{:S(2)}, u32[]{:S(2)}) collective-permute-start(f32[512,464]{0,1:T(8,128)} %copy.323), channel_id=1, source_target_pairs={{0,16},{8,24},{16,0},{24,8},{1,17},{9,25},{17,1},{25,9},{2,18},{10... | collective-permute-start | bytes 2850824 | tf_op jit(solution)/shard_map/ppermute | solution.py:641
  92.9 5.4 collective-permute-start.6
  92.9 289.3 %copy-start.23 = (f32[4]{0:T(128)}, f32[4]{0:T(128)S(1)}, u32[]{:S(2)}) copy-start(f32[4]{0:T(128)S(1)} %compare_convert_fusion.keep_ref) | copy-start | bytes 52
  112.9 5.1 collective-permute-start.7
  117.9 264.4 %copy-start.14 = (f32[3,2048]{1,0:T(4,128)}, f32[3,2048]{1,0:T(4,128)S(1)}, u32[]{:S(2)}) copy-start(f32[3,2048]{1,0:T(4,128)S(1)} %slice.380.vec_ref) | copy-start | bytes 73732
  134.9 192.7 %copy-start.55 = (bf16[256,2048]{1,0:T(8,128)(2,1)}, bf16[256,2048]{1,0:T(8,128)(2,1)S(1)}, u32[]{:S(2)}) copy-start(bf16[256,2048]{1,0:T(8,128)(2,1)S(1)} %fusion.35.left_ref) | copy-start | bytes 3145732
  137.3 211.6 %copy-start.54 = (bf16[256,2048]{1,0:T(8,128)(2,1)}, bf16[256,2048]{1,0:T(8,128)(2,1)S(1)}, u32[]{:S(2)}) copy-start(bf16[256,2048]{1,0:T(8,128)(2,1)S(1)} %fusion.33.left_ref) | copy-start | bytes 3145732
  348.6 7.4 collective-permute-start.8
  356.2 26.0 %collective-permute-start.9 = (f32[64,2048]{1,0:T(8,128)S(1)}, f32[64,2048]{1,0:T(8,128)S(1)}, u32[]{:S(2)}, u32[]{:S(2)}) collective-permute-start(f32[64,2048]{1,0:T(8,128)S(1)} %add_select_fusion.3), channel_id=1, source_target_pairs={{0,16},{8,24},{1,17},{9,25},{2,18},{10,26},{3,19},{11,27},{4,20},{... | collective-permute-start | bytes 1572872 | tf_op jit(solution)/shard_map/ppermute | solution.py:624
  441.8 2.1 collective-permute-start.10
  712.0 43.8 %collective-permute-start.12 = (bf16[3584,1024]{1,0:T(8,128)(2,1)}, bf16[3584,1024]{1,0:T(8,128)(2,1)}, u32[]{:S(2)}, u32[]{:S(2)}) collective-permute-start(bf16[3584,1024]{1,0:T(8,128)(2,1)} %shard_map.602), channel_id=1, source_target_pairs={{0,8},{8,0},{16,24},{24,16},{1,9},{9,1},{17,25},{25,17},{2,10},{10... | collective-permute-start | bytes 22020104 | tf_op jit(solution)/shard_map/ppermute | solution.py:641
  712.3 43.5 %collective-permute-start.11 = (bf16[3584,1024]{1,0:T(8,128)(2,1)}, bf16[3584,1024]{1,0:T(8,128)(2,1)}, u32[]{:S(2)}, u32[]{:S(2)}) collective-permute-start(bf16[3584,1024]{1,0:T(8,128)(2,1)} %shard_map.601), channel_id=1, source_target_pairs={{0,8},{8,0},{16,24},{24,16},{1,9},{9,1},{17,25},{25,17},{2,10},{10... | collective-permute-start | bytes 22020104 | tf_op jit(solution)/shard_map/ppermute | solution.py:641
  712.5 85.7 %copy-start.144 = (pred[256]{0:T(512)(128)(4,1)}, pred[256]{0:T(512)(128)(4,1)S(1)}, u32[]{:S(2)}) copy-start(pred[256]{0:T(512)(128)(4,1)S(1)} %iota_compare_fusion.2) | copy-start | bytes 772
  777.8 20.4 %collective-permute-start.15 = (f32[1,2048]{1,0:T(1,128)S(1)}, f32[1,2048]{1,0:T(1,128)S(1)}, u32[]{:S(2)}, u32[]{:S(2)}) collective-permute-start(f32[1,2048]{1,0:T(1,128)S(1)} %split.51), channel_id=1, source_target_pairs={{8,0},{16,8},{24,16},{9,1},{17,9},{25,17},{10,2},{18,10},{26,18},{... | collective-permute-start | bytes 24584 | tf_op jit(solution)/shard_map/ppermute | solution.py:603
  786.3 82.4 %collective-permute-start.14 = (bf16[2,4,224,1024]{3,2,1,0:T(8,128)(2,1)}, bf16[2,4,224,1024]{3,2,1,0:T(8,128)(2,1)}, u32[]{:S(2)}, u32[]{:S(2)}) collective-permute-start(bf16[2,4,224,1024]{3,2,1,0:T(8,128)(2,1)} %fusion.8), channel_id=1, source_target_pairs={{0,1},{1,0},{2,3},{3,2},{4,5},{5,4},{6,7},{7,6},{8,9},{9,8},{10,11... | collective-permute-start | bytes 11010056 | tf_op jit(solution)/shard_map/ppermute | solution.py:641
  795.7 82.4 %collective-permute-start.13 = (bf16[1792,1024]{1,0:T(8,128)(2,1)}, bf16[1792,1024]{1,0:T(8,128)(2,1)}, u32[]{:S(2)}, u32[]{:S(2)}) collective-permute-start(bf16[1792,1024]{1,0:T(8,128)(2,1)} %get-tuple-element.560), channel_id=1, source_target_pairs={{0,16},{8,24},{16,0},{24,8},{1,17},{9,25},{17,1},{25,9},{2,18},{10... | collective-permute-start | bytes 11010056 | tf_op jit(solution)/shard_map/ppermute | solution.py:641
  819.3 133.8 %collective-permute-start.17 = (bf16[1024,3584]{1,0:T(8,128)(2,1)}, bf16[1024,3584]{1,0:T(8,128)(2,1)}, u32[]{:S(2)}, u32[]{:S(2)}) collective-permute-start(bf16[1024,3584]{1,0:T(8,128)(2,1)} %shard_map.610), channel_id=1, source_target_pairs={{0,8},{8,0},{16,24},{24,16},{1,9},{9,1},{17,25},{25,17},{2,10},{10... | collective-permute-start | bytes 22020104 | tf_op jit(solution)/shard_map/ppermute | solution.py:641
  819.3 133.8 %collective-permute-start.16 = (bf16[1024,3584]{1,0:T(8,128)(2,1)}, bf16[1024,3584]{1,0:T(8,128)(2,1)}, u32[]{:S(2)}, u32[]{:S(2)}) collective-permute-start(bf16[1024,3584]{1,0:T(8,128)(2,1)} %shard_map.609), channel_id=1, source_target_pairs={{0,8},{8,0},{16,24},{24,16},{1,9},{9,1},{17,25},{25,17},{2,10},{10... | collective-permute-start | bytes 22020104 | tf_op jit(solution)/shard_map/ppermute | solution.py:641
  882.9 70.2 %collective-permute-start.19 = (bf16[1024,2048]{1,0:T(8,128)(2,1)}, bf16[1024,2048]{1,0:T(8,128)(2,1)}, u32[]{:S(2)}, u32[]{:S(2)}) collective-permute-start(bf16[1024,2048]{1,0:T(8,128)(2,1)} %shard_map.615), channel_id=1, source_target_pairs={{0,8},{8,0},{16,24},{24,16},{1,9},{9,1},{17,25},{25,17},{2,10},{10... | collective-permute-start | bytes 12582920 | tf_op jit(solution)/shard_map/ppermute | solution.py:641
  887.8 65.3 %collective-permute-start.18 = (bf16[1024,2048]{1,0:T(8,128)(2,1)}, bf16[1024,2048]{1,0:T(8,128)(2,1)}, u32[]{:S(2)}, u32[]{:S(2)}) collective-permute-start(bf16[1024,2048]{1,0:T(8,128)(2,1)} %shard_map.614), channel_id=1, source_target_pairs={{0,8},{8,0},{16,24},{24,16},{1,9},{9,1},{17,25},{25,17},{2,10},{10... | collective-permute-start | bytes 12582920 | tf_op jit(solution)/shard_map/ppermute | solution.py:641
  922.1 2.1 collective-permute-start.20
  924.2 28.7 %collective-permute-start.21 = (f32[64,2048]{1,0:T(8,128)S(1)}, f32[64,2048]{1,0:T(8,128)S(1)}, u32[]{:S(2)}, u32[]{:S(2)}) collective-permute-start(f32[64,2048]{1,0:T(8,128)S(1)} %add_select_fusion.1), channel_id=1, source_target_pairs={{16,0},{24,8},{17,1},{25,9},{18,2},{26,10},{19,3},{27,11},{20,4},{... | collective-permute-start | bytes 1572872 | tf_op jit(solution)/shard_map/ppermute | solution.py:624
  957.1 94.1 %collective-permute-start.25 = (bf16[2,4,64,2048]{3,2,1,0:T(8,128)(2,1)}, bf16[2,4,64,2048]{3,2,1,0:T(8,128)(2,1)}, u32[]{:S(2)}, u32[]{:S(2)}) collective-permute-start(bf16[2,4,64,2048]{3,2,1,0:T(8,128)(2,1)} %fusion.48), channel_id=1, source_target_pairs={{0,1},{1,0},{2,3},{3,2},{4,5},{5,4},{6,7},{7,6},{8,9},{9,8},{10,11... | collective-permute-start | bytes 6291464 | tf_op jit(solution)/shard_map/ppermute | solution.py:641
  963.5 87.7 %collective-permute-start.24 = (bf16[512,2048]{1,0:T(8,128)(2,1)}, bf16[512,2048]{1,0:T(8,128)(2,1)}, u32[]{:S(2)}, u32[]{:S(2)}) collective-permute-start(bf16[512,2048]{1,0:T(8,128)(2,1)} %get-tuple-element.573), channel_id=1, source_target_pairs={{0,16},{8,24},{16,0},{24,8},{1,17},{9,25},{17,1},{25,9},{2,18},{10... | collective-permute-start | bytes 6291464 | tf_op jit(solution)/shard_map/ppermute | solution.py:641
  971.9 79.2 %collective-permute-start.23 = (bf16[4,224,1024]{2,1,0:T(8,128)(2,1)}, bf16[4,224,1024]{2,1,0:T(8,128)(2,1)}, u32[]{:S(2)}, u32[]{:S(2)}) collective-permute-start(bf16[4,224,1024]{2,1,0:T(8,128)(2,1)} %get-tuple-element.558), channel_id=1, source_target_pairs={{0,16},{8,24},{16,0},{24,8},{1,17},{9,25},{17,1},{25,9},{2,18},{10... | collective-permute-start | bytes 5505032 | tf_op jit(solution)/shard_map/ppermute | solution.py:641
  975.7 75.4 %collective-permute-start.22 = (bf16[4,224,1024]{2,1,0:T(8,128)(2,1)}, bf16[4,224,1024]{2,1,0:T(8,128)(2,1)}, u32[]{:S(2)}, u32[]{:S(2)}) collective-permute-start(bf16[4,224,1024]{2,1,0:T(8,128)(2,1)} %fusion.58), channel_id=1, source_target_pairs={{0,1},{1,0},{2,3},{3,2},{4,5},{5,4},{6,7},{7,6},{8,9},{9,8},{10,11... | collective-permute-start | bytes 5505032 | tf_op jit(solution)/shard_map/ppermute | solution.py:641
  981.8 69.3 %slice-start = ((s8[7340032]{0:T(1024)(128)(4,1)}), s8[4194304]{0:T(1024)(128)(4,1)S(1)}, s32[]{:S(2)}) async-start(s8[7340032]{0:T(1024)(128)(4,1)} %bitcast.403), calls=%async_computation.7 | async-start | bytes 8388608
  1056.2 110.1 %collective-permute-start.28 = (bf16[2,4,64,3584]{3,2,1,0:T(8,128)(2,1)}, bf16[2,4,64,3584]{3,2,1,0:T(8,128)(2,1)}, u32[]{:S(2)}, u32[]{:S(2)}) collective-permute-start(bf16[2,4,64,3584]{3,2,1,0:T(8,128)(2,1)} %fusion.10), channel_id=1, source_target_pairs={{0,1},{1,0},{2,3},{3,2},{4,5},{5,4},{6,7},{7,6},{8,9},{9,8},{10,11... | collective-permute-start | bytes 11010056 | tf_op jit(solution)/shard_map/ppermute | solution.py:641
  1063.4 102.9 %collective-permute-start.27 = (bf16[512,3584]{1,0:T(8,128)(2,1)}, bf16[512,3584]{1,0:T(8,128)(2,1)}, u32[]{:S(2)}, u32[]{:S(2)}) collective-permute-start(bf16[512,3584]{1,0:T(8,128)(2,1)} %get-tuple-element.556), channel_id=1, source_target_pairs={{0,16},{8,24},{16,0},{24,8},{1,17},{9,25},{17,1},{25,9},{2,18},{10... | collective-permute-start | bytes 11010056 | tf_op jit(solution)/shard_map/ppermute | solution.py:641
  1072.6 93.6 %collective-permute-start.26 = (bf16[2,2,224,1024]{3,2,1,0:T(8,128)(2,1)}, bf16[2,2,224,1024]{3,2,1,0:T(8,128)(2,1)}, u32[]{:S(2)}, u32[]{:S(2)}) collective-permute-start(bf16[2,2,224,1024]{3,2,1,0:T(8,128)(2,1)} %pad_maximum_fusion.5), channel_id=1, source_target_pairs={{0,2},{1,3},{2,0},{3,1},{4,6},{5,7},{6,4},{7,5},{8,10},{9,11},{10,... | collective-permute-start | bytes 5505032 | tf_op jit(solution)/shard_map/ppermute | solution.py:641
  1076.4 89.9 %collective-permute-start.30 = (bf16[4,64,2048]{2,1,0:T(8,128)(2,1)}, bf16[4,64,2048]{2,1,0:T(8,128)(2,1)}, u32[]{:S(2)}, u32[]{:S(2)}) collective-permute-start(bf16[4,64,2048]{2,1,0:T(8,128)(2,1)} %get-tuple-element.571), channel_id=1, source_target_pairs={{0,16},{8,24},{16,0},{24,8},{1,17},{9,25},{17,1},{25,9},{2,18},{10... | collective-permute-start | bytes 3145736 | tf_op jit(solution)/shard_map/ppermute | solution.py:641
  1079.4 86.9 %collective-permute-start.29 = (bf16[4,64,2048]{2,1,0:T(8,128)(2,1)}, bf16[4,64,2048]{2,1,0:T(8,128)(2,1)}, u32[]{:S(2)}, u32[]{:S(2)}) collective-permute-start(bf16[4,64,2048]{2,1,0:T(8,128)(2,1)} %fusion.71), channel_id=1, source_target_pairs={{0,1},{1,0},{2,3},{3,2},{4,5},{5,4},{6,7},{7,6},{8,9},{9,8},{10,11... | collective-permute-start | bytes 3145736 | tf_op jit(solution)/shard_map/ppermute | solution.py:641
  1183.3 68.9 %collective-permute-start.35 = (bf16[2,1024,2048]{2,1,0:T(8,128)(2,1)}, bf16[2,1024,2048]{2,1,0:T(8,128)(2,1)}, u32[]{:S(2)}, u32[]{:S(2)}) collective-permute-start(bf16[2,1024,2048]{2,1,0:T(8,128)(2,1)} %pad_maximum_fusion.1), channel_id=1, source_target_pairs={{0,8},{8,0},{16,24},{24,16},{1,9},{9,1},{17,25},{25,17},{2,10},{10... | collective-permute-start | bytes 25165832 | tf_op jit(solution)/shard_map/ppermute | solution.py:641
  1200.4 51.8 %collective-permute-start.34 = (bf16[2,1024,2048]{2,1,0:T(8,128)(2,1)}, bf16[2,1024,2048]{2,1,0:T(8,128)(2,1)}, u32[]{:S(2)}, u32[]{:S(2)}) collective-permute-start(bf16[2,1024,2048]{2,1,0:T(8,128)(2,1)} %pad_maximum_fusion), channel_id=1, source_target_pairs={{0,8},{8,0},{16,24},{24,16},{1,9},{9,1},{17,25},{25,17},{2,10},{10... | collective-permute-start | bytes 25165832 | tf_op jit(solution)/shard_map/ppermute | solution.py:641
  1207.2 42.1 %collective-permute-start.32 = (bf16[4,64,3584]{2,1,0:T(8,128)(2,1)}, bf16[4,64,3584]{2,1,0:T(8,128)(2,1)}, u32[]{:S(2)}, u32[]{:S(2)}) collective-permute-start(bf16[4,64,3584]{2,1,0:T(8,128)(2,1)} %get-tuple-element.554), channel_id=1, source_target_pairs={{0,16},{8,24},{16,0},{24,8},{1,17},{9,25},{17,1},{25,9},{2,18},{10... | collective-permute-start | bytes 5505032 | tf_op jit(solution)/shard_map/ppermute | solution.py:641
  1210.5 41.7 %collective-permute-start.31 = (bf16[4,64,3584]{2,1,0:T(8,128)(2,1)S(1)}, bf16[4,64,3584]{2,1,0:T(8,128)(2,1)}, u32[]{:S(2)}, u32[]{:S(2)}) collective-permute-start(bf16[4,64,3584]{2,1,0:T(8,128)(2,1)S(1)} %fusion.62), channel_id=1, source_target_pairs={{0,1},{1,0},{2,3},{3,2},{4,5},{5,4},{6,7},{7,6},{8,9},{9,8},{10,11... | collective-permute-start | bytes 5505032 | tf_op jit(solution)/shard_map/ppermute | solution.py:641
  1215.9 27.6 %collective-permute-start.33 = (bf16[2,2,64,2048]{3,2,1,0:T(8,128)(2,1)}, bf16[2,2,64,2048]{3,2,1,0:T(8,128)(2,1)}, u32[]{:S(2)}, u32[]{:S(2)}) collective-permute-start(bf16[2,2,64,2048]{3,2,1,0:T(8,128)(2,1)} %pad_maximum_fusion.12), channel_id=1, source_target_pairs={{0,2},{1,3},{2,0},{3,1},{4,6},{5,7},{6,4},{7,5},{8,10},{9,11},{10,... | collective-permute-start | bytes 3145736 | tf_op jit(solution)/shard_map/ppermute | solution.py:641
  1260.0 35.1 %collective-permute-start.40 = (f32[1,2048]{1,0:T(1,128)S(1)}, f32[1,2048]{1,0:T(1,128)S(1)}, u32[]{:S(2)}, u32[]{:S(2)}) collective-permute-start(f32[1,2048]{1,0:T(1,128)S(1)} %copy-done.146), channel_id=1, source_target_pairs={{8,0},{16,8},{24,16},{9,1},{17,9},{25,17},{10,2},{18,10},{26,18},{... | collective-permute-start | bytes 24584 | tf_op jit(solution)/shard_map/ppermute | solution.py:603
  1263.4 77.7 %collective-permute-start.39 = (bf16[2,4,64,2048]{3,2,1,0:T(8,128)(2,1)}, bf16[2,4,64,2048]{3,2,1,0:T(8,128)(2,1)}, u32[]{:S(2)}, u32[]{:S(2)}) collective-permute-start(bf16[2,4,64,2048]{3,2,1,0:T(8,128)(2,1)} %fusion.50), channel_id=1, source_target_pairs={{0,1},{1,0},{2,3},{3,2},{4,5},{5,4},{6,7},{7,6},{8,9},{9,8},{10,11... | collective-permute-start | bytes 6291464 | tf_op jit(solution)/shard_map/ppermute | solution.py:641
  1271.1 70.0 %collective-permute-start.38 = (bf16[512,2048]{1,0:T(8,128)(2,1)}, bf16[512,2048]{1,0:T(8,128)(2,1)}, u32[]{:S(2)}, u32[]{:S(2)}) collective-permute-start(bf16[512,2048]{1,0:T(8,128)(2,1)} %get-tuple-element.552), channel_id=1, source_target_pairs={{0,16},{8,24},{16,0},{24,8},{1,17},{9,25},{17,1},{25,9},{2,18},{10... | collective-permute-start | bytes 6291464 | tf_op jit(solution)/shard_map/ppermute | solution.py:641
  1279.3 61.8 %collective-permute-start.37 = (bf16[2,2,64,3584]{3,2,1,0:T(8,128)(2,1)}, bf16[2,2,64,3584]{3,2,1,0:T(8,128)(2,1)}, u32[]{:S(2)}, u32[]{:S(2)}) collective-permute-start(bf16[2,2,64,3584]{3,2,1,0:T(8,128)(2,1)} %pad_maximum_fusion.7), channel_id=1, source_target_pairs={{0,2},{1,3},{2,0},{3,1},{4,6},{5,7},{6,4},{7,5},{8,10},{9,11},{10,... | collective-permute-start | bytes 5505032 | tf_op jit(solution)/shard_map/ppermute | solution.py:641
  1289.2 49.7 %collective-permute-start.36 = (bf16[2,224,1024]{2,1,0:T(8,128)(2,1)}, bf16[2,224,1024]{2,1,0:T(8,128)(2,1)}, u32[]{:S(2)}, u32[]{:S(2)}) collective-permute-start(bf16[2,224,1024]{2,1,0:T(8,128)(2,1)} %get-tuple-element.588), channel_id=1, source_target_pairs={{0,4},{1,5},{2,6},{3,7},{4,0},{5,1},{6,2},{7,3},{8,12},{9,13},{10,... | collective-permute-start | bytes 2752520 | tf_op jit(solution)/shard_map/ppermute | solution.py:641
  1341.2 194.8 %reduce-scatter.5.cloned.1.call-start = ((), (), s32[]{:S(2)}) async-start(), calls=%async_computation.6 | async-start | bytes 1179648 | tf_op jit(solution)/shard_map/reduce_scatter | solution.py:926
  1346.6 96.8 %collective-permute-start.45 = (bf16[2,4,64,2048]{3,2,1,0:T(8,128)(2,1)S(1)}, bf16[2,4,64,2048]{3,2,1,0:T(8,128)(2,1)}, u32[]{:S(2)}, u32[]{:S(2)}) collective-permute-start(bf16[2,4,64,2048]{3,2,1,0:T(8,128)(2,1)S(1)} %fusion.52), channel_id=1, source_target_pairs={{0,1},{1,0},{2,3},{3,2},{4,5},{5,4},{6,7},{7,6},{8,9},{9,8},{10,11... | collective-permute-start | bytes 6291464 | tf_op jit(solution)/shard_map/ppermute | solution.py:641
  1351.5 93.2 %collective-permute-start.44 = (bf16[512,2048]{1,0:T(8,128)(2,1)S(1)}, bf16[512,2048]{1,0:T(8,128)(2,1)}, u32[]{:S(2)}, u32[]{:S(2)}) collective-permute-start(bf16[512,2048]{1,0:T(8,128)(2,1)S(1)} %get-tuple-element.567), channel_id=1, source_target_pairs={{0,16},{8,24},{16,0},{24,8},{1,17},{9,25},{17,1},{25,9},{2,18},{10... | collective-permute-start | bytes 6291464 | tf_op jit(solution)/shard_map/ppermute | solution.py:641
  1356.2 87.1 %collective-permute-start.43 = (bf16[4,64,2048]{2,1,0:T(8,128)(2,1)S(1)}, bf16[4,64,2048]{2,1,0:T(8,128)(2,1)S(1)}, u32[]{:S(2)}, u32[]{:S(2)}) collective-permute-start(bf16[4,64,2048]{2,1,0:T(8,128)(2,1)S(1)} %get-tuple-element.569), channel_id=1, source_target_pairs={{0,16},{8,24},{16,0},{24,8},{1,17},{9,25},{17,1},{25,9},{2,18},{10... | collective-permute-start | bytes 3145736 | tf_op jit(solution)/shard_map/ppermute | solution.py:641
  1358.5 84.8 %collective-permute-start.42 = (bf16[4,64,2048]{2,1,0:T(8,128)(2,1)S(1)}, bf16[4,64,2048]{2,1,0:T(8,128)(2,1)S(1)}, u32[]{:S(2)}, u32[]{:S(2)}) collective-permute-start(bf16[4,64,2048]{2,1,0:T(8,128)(2,1)S(1)} %fusion.75), channel_id=1, source_target_pairs={{0,1},{1,0},{2,3},{3,2},{4,5},{5,4},{6,7},{7,6},{8,9},{9,8},{10,11... | collective-permute-start | bytes 3145736 | tf_op jit(solution)/shard_map/ppermute | solution.py:641
  1367.1 42.0 %collective-permute-start.41 = (bf16[2,64,3584]{2,1,0:T(8,128)(2,1)S(1)}, bf16[2,64,3584]{2,1,0:T(8,128)(2,1)S(1)}, u32[]{:S(2)}, u32[]{:S(2)}) collective-permute-start(bf16[2,64,3584]{2,1,0:T(8,128)(2,1)S(1)} %get-tuple-element.586), channel_id=1, source_target_pairs={{0,4},{1,5},{2,6},{3,7},{4,0},{5,1},{6,2},{7,3},{8,12},{9,13},{10,... | collective-permute-start | bytes 2752520 | tf_op jit(solution)/shard_map/ppermute | solution.py:641
  1451.7 51.5 %collective-permute-start.49 = (bf16[4,64,2048]{2,1,0:T(8,128)(2,1)}, bf16[4,64,2048]{2,1,0:T(8,128)(2,1)}, u32[]{:S(2)}, u32[]{:S(2)}) collective-permute-start(bf16[4,64,2048]{2,1,0:T(8,128)(2,1)} %get-tuple-element.565), channel_id=1, source_target_pairs={{0,16},{8,24},{16,0},{24,8},{1,17},{9,25},{17,1},{25,9},{2,18},{10... | collective-permute-start | bytes 3145736 | tf_op jit(solution)/shard_map/ppermute | solution.py:641
  1456.1 47.2 %collective-permute-start.48 = (bf16[4,64,2048]{2,1,0:T(8,128)(2,1)}, bf16[4,64,2048]{2,1,0:T(8,128)(2,1)}, u32[]{:S(2)}, u32[]{:S(2)}) collective-permute-start(bf16[4,64,2048]{2,1,0:T(8,128)(2,1)} %fusion.79), channel_id=1, source_target_pairs={{0,1},{1,0},{2,3},{3,2},{4,5},{5,4},{6,7},{7,6},{8,9},{9,8},{10,11... | collective-permute-start | bytes 3145736 | tf_op jit(solution)/shard_map/ppermute | solution.py:641
  1460.9 43.4 %collective-permute-start.47 = (bf16[2,2,64,2048]{3,2,1,0:T(8,128)(2,1)}, bf16[2,2,64,2048]{3,2,1,0:T(8,128)(2,1)}, u32[]{:S(2)}, u32[]{:S(2)}) collective-permute-start(bf16[2,2,64,2048]{3,2,1,0:T(8,128)(2,1)} %pad_maximum_fusion.14), channel_id=1, source_target_pairs={{0,2},{1,3},{2,0},{3,1},{4,6},{5,7},{6,4},{7,5},{8,10},{9,11},{10,... | collective-permute-start | bytes 3145736 | tf_op jit(solution)/shard_map/ppermute | solution.py:641
  1464.7 38.6 %collective-permute-start.46 = (bf16[2,64,2048]{2,1,0:T(8,128)(2,1)}, bf16[2,64,2048]{2,1,0:T(8,128)(2,1)}, u32[]{:S(2)}, u32[]{:S(2)}) collective-permute-start(bf16[2,64,2048]{2,1,0:T(8,128)(2,1)} %get-tuple-element.595), channel_id=1, source_target_pairs={{0,4},{1,5},{2,6},{3,7},{4,0},{5,1},{6,2},{7,3},{8,12},{9,13},{10,... | collective-permute-start | bytes 1572872 | tf_op jit(solution)/shard_map/ppermute | solution.py:641
  1508.9 39.4 %collective-permute-start.51 = (bf16[2,2,64,2048]{3,2,1,0:T(8,128)(2,1)}, bf16[2,2,64,2048]{3,2,1,0:T(8,128)(2,1)}, u32[]{:S(2)}, u32[]{:S(2)}) collective-permute-start(bf16[2,2,64,2048]{3,2,1,0:T(8,128)(2,1)} %pad_maximum_fusion.16), channel_id=1, source_target_pairs={{0,2},{1,3},{2,0},{3,1},{4,6},{5,7},{6,4},{7,5},{8,10},{9,11},{10,... | collective-permute-start | bytes 3145736 | tf_op jit(solution)/shard_map/ppermute | solution.py:641
  1512.3 36.0 %collective-permute-start.50 = (bf16[2,64,2048]{2,1,0:T(8,128)(2,1)}, bf16[2,64,2048]{2,1,0:T(8,128)(2,1)}, u32[]{:S(2)}, u32[]{:S(2)}) collective-permute-start(bf16[2,64,2048]{2,1,0:T(8,128)(2,1)} %get-tuple-element.593), channel_id=1, source_target_pairs={{0,4},{1,5},{2,6},{3,7},{4,0},{5,1},{6,2},{7,3},{8,12},{9,13},{10,... | collective-permute-start | bytes 1572872 | tf_op jit(solution)/shard_map/ppermute | solution.py:641
  1550.0 24.8 %collective-permute-start.52 = (bf16[2,64,2048]{2,1,0:T(8,128)(2,1)S(1)}, bf16[2,64,2048]{2,1,0:T(8,128)(2,1)S(1)}, u32[]{:S(2)}, u32[]{:S(2)}) collective-permute-start(bf16[2,64,2048]{2,1,0:T(8,128)(2,1)S(1)} %get-tuple-element.591), channel_id=1, source_target_pairs={{0,4},{1,5},{2,6},{3,7},{4,0},{5,1},{6,2},{7,3},{8,12},{9,13},{10,... | collective-permute-start | bytes 1572872 | tf_op jit(solution)/shard_map/ppermute | solution.py:641
  (145 other events, 1271.8 us)
Sparse Core Ops, SparseCore 0:
  11.7 309.8 all-gather.3
  324.5 181.0 all-gather.5
  508.5 172.9 all-gather.7
  1341.4 65.8 reduce-scatter.2
  1464.8 71.1 reduce-scatter.4
